TPU v7x, 128 devices: a whole 4x4x4 slice. The times are simulated.
128 devices in a mesh: node: 4 (over x), surf: 32 (over z, y, core).
Axes of the slice: x: 4, y: 4, z: 4, core: 2. Of those that a mesh axis runs over, the one named last changes fastest.
Arguments:
- sens: bfloat16 [256, 3, 524288], P('node', None, 'surf'), may hold values from -6 to 6
- psi: float32 [35, 256], replicated, may hold values from -4 to 4
- quad_table: float32 [16], replicated, may hold values from 0.004 to 0.04
- quad_index: int32 [256], replicated, may hold values from 0 to 15
- counts: int32 [1024], P('surf'), may hold values from 1 to 512, 327680 in all
- cells: int32 [1024], P('surf'), may hold values from 0 to 383, as said below
- coords: float32 [3, 524288], P(None, 'surf'), may hold values from 0 to 1
Outputs:
- gradient: float32 [105, 24576], P(None, ('node', 'surf'))
Inputs may be any that keep to these rules, and one draw needn't show every extreme that they name: `counts`: some patch is full, with 512 live points, in every draw. `cells`: cell e belongs to owner e // 3. Within each aligned block of 8 patches, no two patches have the same owner.
All inputs are finite; a program needn't handle non-finite values. No bound on the sum of `counts` on one device may be relied on, other than what follows from the above.
Results may differ from a plain program's by a relative error of at most 0.003.
Values may be sent and summed in bfloat16 or wider, within the bound.
No kernel may reach another device: no remote copies, remote signals or barrier semaphores. Data moves between devices by JAX's collectives and lax.ppermute only.
A program may use at most 128 MiB of HBM per device.

v0:
```python
import jax
import jax.numpy as jnp
from jax import lax
from jax.sharding import PartitionSpec as P

K = 35
NQW = 16
CELLS = 384
PATCH_PTS = 512


def bernstein(coords, live):
    one = 1.0 - coords
    basis = jnp.stack(
        [
            one * one * one,
            3.0 * coords * one * one,
            3.0 * coords * coords * one,
            coords * coords * coords,
        ],
        axis=1,
    )
    weights = basis[0][:, None, None, :] * basis[1][None, :, None, :] * basis[2][None, None, :, :]
    return weights.reshape(64, -1) * live[None, :]


def patch_tiles(chaos, counts, coords):
    npatch = counts.shape[0]
    slots = jnp.arange(PATCH_PTS, dtype=jnp.int32)
    live = (slots[None, :] < counts[:, None]).astype(jnp.float32).reshape(-1)
    bern = bernstein(coords, live).reshape(64, npatch, PATCH_PTS)
    flat = chaos.reshape(3 * K, npatch, PATCH_PTS)
    return jnp.einsum("apn,tpn->pat", flat, bern, precision=lax.Precision.HIGHEST)


def dense_lattice(tiles, cells):
    hits = (cells[:, None] == jnp.arange(CELLS, dtype=jnp.int32)[None, :]).astype(jnp.float32)
    spread = jnp.einsum("pe,pat->aet", hits, tiles, precision=lax.Precision.HIGHEST)
    partial_lattice = spread.reshape(3 * K, CELLS * 64)
    return lax.psum_scatter(partial_lattice, ("node", "surf"), scatter_dimension=1, tiled=True)


def local(sens, psi, quad_table, quad_index, counts, cells, coords):
    groups = lax.axis_size("node")
    group_index = lax.axis_index("node")
    hits = (quad_index[:, None] == jnp.arange(NQW, dtype=jnp.int32)[None, :]).astype(jnp.float32)
    qweight = jnp.dot(hits, quad_table, precision=lax.Precision.HIGHEST)
    coef = (psi * qweight[None, :]).astype(jnp.bfloat16)
    quarter_patches = counts.shape[0] // groups
    quarter_points = quarter_patches * PATCH_PTS
    pstart = group_index * quarter_patches
    qstart = group_index * quarter_points
    own_counts = lax.dynamic_slice_in_dim(counts, pstart, quarter_patches, 0)
    own_cells = lax.dynamic_slice_in_dim(cells, pstart, quarter_patches, 0)
    own_coords = lax.dynamic_slice_in_dim(coords, qstart, quarter_points, 1)
    chaos = jnp.einsum(
        "kq,qcn->kcn",
        coef,
        lax.all_to_all(sens, "node", split_axis=2, concat_axis=0, tiled=True),
        preferred_element_type=jnp.float32,
    )
    tiles = patch_tiles(chaos, own_counts, own_coords)
    return dense_lattice(tiles, own_cells)


def solution(mesh):
    in_specs = (P("node", None, "surf"), P(), P(), P(), P("surf"), P("surf"), P(None, "surf"))
    out_specs = P(None, ("node", "surf"))
    return jax.shard_map(local, mesh=mesh, in_specs=in_specs, out_specs=out_specs, check_vma=False)
```

profile of v0, /device:TPU:0, one launch (start us, length us, event | category | flops | bytes accessed | tf_op | source)
XLA Modules:
  0.0 415.6 jit_solution(15547998422458433283)
XLA Ops:
  6.5 0.0 copy-start
  6.5 20.9 %copy.18 = bf16[64,3,16384]{0,1,2:T(4,128)(2,1)} copy(bf16[64,3,16384]{2,0,1:T(8,128)(2,1)} %param.7) | data formatting | bytes 12582912 | tf_op args[0]
  27.5 14.5 %reshape.49 = bf16[4,2,393216]{2,1,0:T(2,128)(2,1)} reshape(bf16[16384,3,64]{2,1,0:T(4,128)(2,1)} %bitcast.37) | data formatting | bytes 12582912
  42.0 0.0 copy-start.4
  42.0 0.0 copy-start.5
  42.0 0.0 copy-start.3
  42.0 5.4 %all-to-all-start = ((bf16[4,2,393216]{2,1,0:T(2,128)(2,1)}), bf16[4,2,393216]{2,1,0:T(2,128)(2,1)}, u32[]{:S(2)}, u32[]{:S(2)}) async-start(bf16[4,2,393216]{2,1,0:T(2,128)(2,1)} %reshape.49), calls=%async_computation | async-start | bytes 12582912 | tf_op jit(solution)/shard_map/all_to_all | solution.py:59
  47.4 0.0 reduce-scatter.2.cloned.1.call-start
  47.4 0.9 fusion.6
  48.3 0.2 pad_maximum_fusion.4
  48.5 0.1 copy_bitcast_fusion
  48.6 0.1 broadcast_multiply_fusion.2
  48.7 0.3 broadcast_multiply_fusion.1
  49.0 0.7 mul.114
  49.7 0.0 copy-done.4
  49.7 0.1 dynamic_slice.10
  49.8 0.0 copy-done.5
  49.8 0.1 dynamic_slice.11
  49.9 0.0 copy-done
  49.9 0.0 copy-done.3
  49.9 0.2 fusion.3
  50.1 0.1 fusion.14
  50.1 0.2 broadcast_multiply_fusion
  50.3 68.5 %all-to-all-done = bf16[4,2,393216]{2,1,0:T(2,128)(2,1)} async-done(((bf16[4,2,393216]{2,1,0:T(2,128)(2,1)}), bf16[4,2,393216]{2,1,0:T(2,128)(2,1)}, u32[]{:S(2)}, u32[]{:S(2)}) %all-to-all-start) | async-done | bytes 6291488 | tf_op jit(solution)/shard_map/all_to_all | solution.py:59
  118.8 13.5 %reshape.50 = bf16[16384,3,64]{2,1,0:T(4,128)(2,1)} reshape(bf16[4,2,393216]{2,1,0:T(2,128)(2,1)} %all-to-all-done) | data formatting | bytes 12582912
  132.3 0.0 copy-start.2
  132.3 21.7 %copy.19 = bf16[64,3,4,4096]{3,0,2,1:T(8,128)(2,1)} copy(bf16[64,3,4,4096]{0,1,3,2:T(4,128)(2,1)} %bitcast.36) | data formatting | bytes 12582912 | tf_op jit(solution)/shard_map/all_to_all | solution.py:59
  154.0 0.0 copy-done.2
  154.0 4.0 fusion.11
  158.0 1.2 copy.20
  159.2 2.5 reshape.43
  161.7 5.1 %fusion = f32[8,105,64]{1,2,0:T(8,128)S(1)} fusion(f32[105,8,512]{2,1,0:T(8,128)} %reshape.43, f32[64,8,512]{2,1,0:T(8,128)S(1)} %broadcast_multiply_fusion), kind=kOutput, calls=%fused_computation.1 | convolution fusion | flops 330301440 | bytes 2983936 | tf_op jit(solution)/shard_map/apn,tpn->pat/dot_general | solution.py:33
  166.8 0.2 copy.23
  167.0 6.9 %convolution_bitcast_fusion = f32[105,384,64]{1,2,0:T(8,128)} fusion(f32[8,105,64]{2,0,1:T(8,128)S(1)} %copy.23, s32[8]{0:T(128)S(1)} %dynamic_slice.11), kind=kOutput, calls=%fused_computation | convolution fusion | flops 247729152 | bytes 10536992 | tf_op jit(solution)/shard_map/pe,pat->aet/dot_general | solution.py:38
  173.9 12.1 %copy.24 = f32[105,384,64]{0,2,1:T(8,128)} copy(f32[105,384,64]{1,2,0:T(8,128)} %convolution_bitcast_fusion) | data formatting | bytes 20643840 | tf_op jit(solution)/shard_map/pe,pat->aet/transpose | solution.py:38
  186.0 0.0 copy-start.1
  186.0 0.0 reduce-scatter.2.cloned.1.call-update
  186.0 222.7 %reduce-scatter.2.cloned.1.call-done = f32[105,192]{0,1:T(8,128)} async-done(((f32[105,24576]{0,1:T(8,128)}), f32[105,192]{0,1:T(8,128)}) %reduce-scatter.2.cloned.1.call-update) | async-done | bytes 80656 | tf_op jit(solution)/shard_map/reduce_scatter | solution.py:40
  408.8 0.0 copy-done.1
  (1 shorter events, 0.0 us)
Async XLA Ops:
  6.5 43.3 %copy-start = (f32[16]{0:T(128)S(1)}, f32[16]{0:T(128)}, u32[]{:S(2)}) copy-start(f32[16]{0:T(128)} %param.9) | copy-start | bytes 196
  42.0 7.7 %copy-start.4 = (s32[32]{0:T(128)S(1)}, s32[32]{0:T(128)}, u32[]{:S(2)}) copy-start(s32[32]{0:T(128)} %param.11) | copy-start | bytes 388
  42.0 7.8 %copy-start.5 = (s32[32]{0:T(128)S(1)}, s32[32]{0:T(128)}, u32[]{:S(2)}) copy-start(s32[32]{0:T(128)} %param.12) | copy-start | bytes 388
  42.0 7.9 %copy-start.3 = (s32[256]{0:T(256)S(1)}, s32[256]{0:T(256)}, u32[]{:S(2)}) copy-start(s32[256]{0:T(256)} %param.10) | copy-start | bytes 3076
  42.0 76.9 %all-to-all-start = ((bf16[4,2,393216]{2,1,0:T(2,128)(2,1)}), bf16[4,2,393216]{2,1,0:T(2,128)(2,1)}, u32[]{:S(2)}, u32[]{:S(2)}) async-start(bf16[4,2,393216]{2,1,0:T(2,128)(2,1)} %reshape.49), calls=%async_computation | async-start | bytes 12582912 | tf_op jit(solution)/shard_map/all_to_all | solution.py:59
  47.4 361.4 %reduce-scatter.2.cloned.1.call-start = ((), (), s32[]{:S(2)}) async-start(), calls=%async_computation.2 | async-start | bytes 12681216 | tf_op jit(solution)/shard_map/reduce_scatter | solution.py:40
  132.3 21.7 %copy-start.2 = (f32[35,256]{1,0:T(8,128)S(1)}, f32[35,256]{1,0:T(8,128)}, u32[]{:S(2)}) copy-start(f32[35,256]{1,0:T(8,128)} %param.8) | copy-start | bytes 107524
  186.0 222.8 %copy-start.1 = (f32[16]{0:T(128)S(1)}, f32[16]{0:T(128)}, u32[]{:S(2)}) copy-start(f32[16]{0:T(128)} %param.9) | copy-start | bytes 196
Sparse Core Ops, SparseCore 0:
  186.1 222.5 reduce-scatter.1
where the time goes:
time: 417 us; the launch traced here: 416 us
  waiting for transfers between devices  291 us (70%)
  local copies, waits for them, and re-layouts  87.6 us (21%)
  matrix products  16.2 us (4%)
  between operations  13.5 us (3%)
  starting transfers between devices  5.43 us (1%)
    reduce_scatter x1, waiting for transfers between devices, dense_lattice(): lax.psum_scatter(partial_lattice, ('node', 'surf'), scatter_dimension=1,...  223 us
    all_to_all x1, waiting for transfers between devices, local(): lax.all_to_all(sens, 'node', split_axis=2, concat_axis=0, tiled=True)  68.5 us
    unnamed x17, local copies, waits for them, and re-layouts  49.1 us
    all_to_all x1, local copies, waits for them, and re-layouts, local(): lax.all_to_all(sens, 'node', split_axis=2, concat_axis=0, tiled=True)  21.7 us
    transpose x1, local copies, waits for them, and re-layouts, dense_lattice(): jnp.einsum('pe,pat->aet', hits, tiles, precision=lax.Precision.HIGHEST)  12.1 us
  transfers between devices with their start and end apart: 2, of which 2 were waited for; matrix products, arithmetic and copies ran while one was open for 1% of the time, Pallas kernels for 0%

commit v1 on v0

v1 whole, which is shorter than its diff:
```python
import jax
import jax.numpy as jnp
from jax import lax
from jax.experimental import pallas as pl
from jax.experimental.pallas import tpu as pltpu
from jax.sharding import Mesh, PartitionSpec as P

K = 35
NQW = 16
CELLS = 384
PATCH_PTS = 512
NODE_Q = 64
STEP_PATCHES = 4
ROWS = 56
LANES = 128
MIB = 1 << 20


def bernstein_rows(coords, count):
    shape = (8, PATCH_PTS)
    u, v, w = [jnp.broadcast_to(row, shape) for row in coords]
    sub = lax.broadcasted_iota(jnp.int32, shape, 0)
    lane = lax.broadcasted_iota(jnp.int32, shape, 1)
    live = (lane < count).astype(jnp.float32)

    def basis(a):
        one = 1.0 - a
        return one * one * one, 3.0 * a * one * one, 3.0 * a * a * one, a * a * a

    w0, w1, w2, w3 = basis(w)
    low = sub & 3
    wl = jnp.where(low == 0, w0, jnp.where(low == 1, w1, jnp.where(low == 2, w2, w3))) * live
    v0, v1, v2, v3 = basis(v)
    first = sub < 4
    pair01 = jnp.where(first, v0, v1) * wl
    pair23 = jnp.where(first, v2, v3) * wl
    rows = []
    for b in basis(u):
        rows += [b * pair01, b * pair23]
    return jnp.concatenate(rows, axis=0)


def split(x):
    high = x.astype(jnp.bfloat16)
    return high, (x - high.astype(jnp.float32)).astype(jnp.bfloat16)


def weights(table_ref, index_ref, psi_ref, pad_ref, w_ref):
    index = index_ref[...]
    qweight = jnp.zeros(index.shape, jnp.float32)
    for j in range(NQW):
        qweight = jnp.where(index == j, table_ref[j], qweight)
    pad_ref[...] = jnp.zeros_like(pad_ref)
    pad_ref[0:K, :] = psi_ref[...] * qweight
    coef = pad_ref[...].astype(jnp.bfloat16)
    node = lax.axis_index("x")
    row = lax.broadcasted_iota(jnp.int32, (112, 40), 0)
    col = lax.broadcasted_iota(jnp.int32, (112, 40), 1)
    expand = ((row - 3 * col >= 0) & (row - 3 * col < 3)).astype(jnp.float32).astype(jnp.bfloat16)
    spread = jnp.dot(expand, coef, preferred_element_type=jnp.float32).astype(jnp.bfloat16)
    q = lax.broadcasted_iota(jnp.int32, (256, 384), 0)
    col = lax.broadcasted_iota(jnp.int32, (256, 384), 1)
    pick = (q == node * NODE_Q + (col & 63)).astype(jnp.float32).astype(jnp.bfloat16)
    full = jnp.dot(spread, pick, preferred_element_type=jnp.float32)
    row = lax.broadcasted_iota(jnp.int32, (112, 384), 0)
    col = lax.broadcasted_iota(jnp.int32, (112, 384), 1)
    w_ref[...] = jnp.where(row % 3 == (col // 64) % 3, full, 0.0).astype(jnp.bfloat16)


def tiles_kernel(counts_ref, table_ref, index_ref, psi_ref, sens_ref, coords_ref, out_ref, pad_ref, w_ref):
    step = pl.program_id(0)

    @pl.when(step == 0)
    def _():
        weights(table_ref, index_ref, psi_ref, pad_ref, w_ref)

    lower = lax.broadcasted_iota(jnp.int32, (192, LANES), 1) < 64
    lower_slot = lower[:ROWS]
    w = w_ref[...]
    for pair in range(STEP_PATCHES // 2):
        both = []
        for half in range(2):
            i = 2 * pair + half
            at = slice(i * PATCH_PTS, (i + 1) * PATCH_PTS)
            count = counts_ref[step * STEP_PATCHES + i]
            bern = bernstein_rows([coords_ref[c : c + 1, at] for c in range(3)], count)
            high, low = split(bern)
            rhs = jnp.concatenate([high, low], axis=0)
            lhs = jnp.concatenate([sens_ref[c, :, at] for c in range(3)], axis=0)
            s = lax.dot_general(lhs, rhs, (((1,), (1,)), ((), ())), preferred_element_type=jnp.float32)
            both.append(s + pltpu.roll(s, 64, 1))
        high, low = split(jnp.where(lower, both[0], both[1]))
        t = jnp.dot(w, jnp.concatenate([high, low], axis=0), preferred_element_type=jnp.float32)
        top, bottom = t[0:ROWS], t[ROWS : 2 * ROWS]
        out_ref[2 * pair] = jnp.where(lower_slot, top, pltpu.roll(bottom, 64, 1)).astype(jnp.bfloat16)
        out_ref[2 * pair + 1] = jnp.where(lower_slot, pltpu.roll(top, 64, 1), bottom).astype(jnp.bfloat16)


def partial_tiles(sens, psi, quad_table, quad_index, counts, coords):
    npatch = counts.shape[0]
    points = STEP_PATCHES * PATCH_PTS
    smem = pl.BlockSpec(memory_space=pltpu.SMEM)
    return pl.pallas_call(
        tiles_kernel,
        grid=(npatch // STEP_PATCHES,),
        in_specs=[
            smem,
            smem,
            pl.BlockSpec((1, 256), lambda i: (0, 0)),
            pl.BlockSpec((K, 256), lambda i: (0, 0)),
            pl.BlockSpec((3, NODE_Q, points), lambda i: (0, 0, i)),
            pl.BlockSpec((3, points), lambda i: (0, i)),
        ],
        out_specs=pl.BlockSpec((STEP_PATCHES, ROWS, LANES), lambda i: (i, 0, 0)),
        out_shape=jax.ShapeDtypeStruct((npatch, ROWS, LANES), jnp.bfloat16),
        scratch_shapes=[pltpu.VMEM((40, 256), jnp.float32), pltpu.VMEM((112, 384), jnp.bfloat16)],
        compiler_params=pltpu.CompilerParams(vmem_limit_bytes=32 * MIB),
        name="tiles",
    )(counts, quad_table, quad_index.reshape(1, 256), psi, sens.transpose(1, 0, 2), coords)


def node_sum_kernel(cells_ref, in_ref, out_ref):
    row = lax.broadcasted_iota(jnp.int32, (ROWS, LANES), 0)
    lane = lax.broadcasted_iota(jnp.int32, (ROWS, LANES), 1)
    node = lax.axis_index("x")
    for p in range(8):
        total = in_ref[p].astype(jnp.float32)
        for j in range(1, 4):
            total = total + in_ref[8 * j + p].astype(jnp.float32)
        cell = cells_ref[8 * node + p]
        owner = cell // 3
        within = cell - 3 * owner
        mark = jnp.where(lane < 96, owner, within).astype(jnp.float32)
        out_ref[p] = jnp.where((row == ROWS - 1) & (lane >= 64), mark, total).astype(jnp.bfloat16)


def node_sum(parts, cells):
    return pl.pallas_call(
        node_sum_kernel,
        in_specs=[pl.BlockSpec(memory_space=pltpu.SMEM), pl.BlockSpec(memory_space=pltpu.VMEM)],
        out_specs=pl.BlockSpec(memory_space=pltpu.VMEM),
        out_shape=jax.ShapeDtypeStruct((8, ROWS, LANES), jnp.bfloat16),
        compiler_params=pltpu.CompilerParams(vmem_limit_bytes=16 * MIB),
        name="node_sum",
    )(cells, parts)


def combine_kernel(in_ref, out_ref, acc_ref, mark_ref, scalar_ref, sem):
    count = in_ref.shape[0]
    acc_ref[...] = jnp.zeros_like(acc_ref)
    for p in range(count):
        mark_ref[p : p + 1, :] = in_ref[p].astype(jnp.float32)[ROWS - 1 : ROWS, :].astype(jnp.int32)
    copy = pltpu.make_async_copy(mark_ref, scalar_ref, sem)
    copy.start()
    copy.wait()
    my_y, my_core = lax.axis_index("y"), lax.axis_index("core")

    def body(p, carry):
        owner, within = scalar_ref[p, 64], scalar_ref[p, 96]
        surf = owner & 31
        mine = (((surf >> 1) & 3) == my_y) & ((surf & 1) == my_core)

        @pl.when(mine)
        def _():
            at = ((owner >> 5) * 4 + (surf >> 3)) * 3 + within
            acc_ref[at] += in_ref[p].astype(jnp.float32)

        return carry

    lax.fori_loop(0, count, body, 0)
    out_ref[...] = acc_ref[...].astype(jnp.bfloat16)


def combine(tiles):
    count = tiles.shape[0]
    return pl.pallas_call(
        combine_kernel,
        in_specs=[pl.BlockSpec(memory_space=pltpu.VMEM)],
        out_specs=pl.BlockSpec(memory_space=pltpu.VMEM),
        out_shape=jax.ShapeDtypeStruct((48, ROWS, LANES), jnp.bfloat16),
        scratch_shapes=[
            pltpu.VMEM((48, ROWS, LANES), jnp.float32),
            pltpu.VMEM((count, LANES), jnp.int32),
            pltpu.SMEM((count, LANES), jnp.int32),
            pltpu.SemaphoreType.DMA,
        ],
        compiler_params=pltpu.CompilerParams(vmem_limit_bytes=16 * MIB),
        name="combine",
    )(tiles)


def owner_sum_kernel(in_ref, out_ref):
    lower = lax.broadcasted_iota(jnp.int32, (ROWS, LANES), 1) < 64
    cell = []
    for e in range(3):
        total = in_ref[e].astype(jnp.float32)
        for j in range(1, in_ref.shape[0] // 3):
            total = total + in_ref[3 * j + e].astype(jnp.float32)
        cell.append(total)
    a, b, c = cell
    rest = 3 * K - ROWS
    out_ref[0:ROWS, 0:128] = jnp.where(lower, a, pltpu.roll(b, 64, 1))
    out_ref[0:ROWS, 128:192] = c[:, 0:64]
    out_ref[ROWS : 3 * K, 0:128] = jnp.where(lower, pltpu.roll(a, 64, 1), b)[0:rest]
    out_ref[ROWS : 3 * K, 128:192] = pltpu.roll(c, 64, 1)[0:rest, 0:64]


def owner_sum(slots):
    return pl.pallas_call(
        owner_sum_kernel,
        in_specs=[pl.BlockSpec(memory_space=pltpu.VMEM)],
        out_specs=pl.BlockSpec(memory_space=pltpu.VMEM),
        out_shape=jax.ShapeDtypeStruct((3 * K, 192), jnp.float32),
        compiler_params=pltpu.CompilerParams(vmem_limit_bytes=16 * MIB),
        name="owner_sum",
    )(slots)


def local(sens, psi, quad_table, quad_index, counts, cells, coords):
    parts = partial_tiles(sens, psi, quad_table, quad_index, counts, coords)
    parts = lax.all_to_all(parts, "x", 0, 0, tiled=True)
    tiles = node_sum(parts, cells)
    tiles = lax.all_gather(tiles, ("y", "core"), axis=0, tiled=True)
    slots = combine(tiles)
    slots = lax.all_to_all(slots, ("x", "z"), 0, 0, tiled=True)
    return owner_sum(slots)


def solution(mesh):
    inner = Mesh(mesh.devices.reshape(4, 4, 4, 2), ("x", "z", "y", "core"))
    surf = ("z", "y", "core")
    in_specs = (P("x", None, surf), P(), P(), P(), P(surf), P(surf), P(None, surf))
    out_specs = P(None, ("x",) + surf)
    return jax.shard_map(local, mesh=inner, in_specs=in_specs, out_specs=out_specs, check_vma=False)
```

time: 417 us -> 66.3 us (0.16)
  waiting for transfers between devices: 291 us -> 0 us
  local copies, waits for them, and re-layouts: 87.6 us -> 7.26 us
  blocking collectives: 0 us -> 46.5 us
  matrix products: 16.2 us -> 0 us
  between operations: 13.5 us -> 0.03 us
  Pallas kernels: 0 us -> 12.2 us
  starting transfers between devices: 5.43 us -> 0 us
    reduce_scatter x1 -> x0, waiting for transfers between devices: 223 us -> none  [dense_lattice(): lax.psum_scatter(partial_lattice, ('node', 'surf'), scatter_dimension=1,...]
    all_to_all x1 -> x0, waiting for transfers between devices: 68.5 us -> none  [local(): lax.all_to_all(sens, 'node', split_axis=2, concat_axis=0, tiled=True)]
    unnamed x17 -> x14, local copies, waits for them, and re-layouts: 49.1 us -> 6.52 us
    all_to_all x0 -> x2, blocking collectives: none -> 32.3 us  [the longest x1 19.4 us: local(): slots = lax.all_to_all(slots, ('x', 'z'), 0, 0, tiled=True)]
    all_to_all x1 -> x0, local copies, waits for them, and re-layouts: 21.7 us -> none  [local(): lax.all_to_all(sens, 'node', split_axis=2, concat_axis=0, tiled=True)]
    dot_general x4 -> x0, matrix products: 16.2 us -> none  [the longest x1 6.91 us: dense_lattice(): jnp.einsum('pe,pat->aet', hits, tiles, precision=lax.Precision.HIGHEST)]
    all_gather x0 -> x1, blocking collectives: none -> 14.2 us  [local(): tiles = lax.all_gather(tiles, ('y', 'core'), axis=0, tiled=True)]
    pallas_call x0 -> x4, Pallas kernels: none -> 12.2 us  [the longest x1 9.11 us: partial_tiles(): pl.pallas_call(tiles_kernel, grid=(npatch // STEP_PATCHES,), in_specs=[sm...]
  transfers between devices with their start and end apart: 2 -> 0, of which waited for: 2 -> 0; matrix products, arithmetic and copies ran while one was open for 1% -> 0% of each run, Pallas kernels for 0% -> 0%
where the time goes in v1:
time: 66.3 us; the launch traced here: 66 us
  blocking collectives  46.5 us (70%)
  Pallas kernels  12.2 us (18%)
  local copies, waits for them, and re-layouts  7.26 us (11%)
    all_to_all x1, blocking collectives, local(): slots = lax.all_to_all(slots, ('x', 'z'), 0, 0, tiled=True)  19.4 us
    all_gather x1, blocking collectives, local(): tiles = lax.all_gather(tiles, ('y', 'core'), axis=0, tiled=True)  14.2 us
    all_to_all x1, blocking collectives, local(): parts = lax.all_to_all(parts, 'x', 0, 0, tiled=True)  12.9 us
    pallas_call x1, Pallas kernels, partial_tiles(): pl.pallas_call(tiles_kernel, grid=(npatch // STEP_PATCHES,), in_specs=[sm...  9.11 us
    unnamed x14, local copies, waits for them, and re-layouts  6.52 us
    pallas_call x1, Pallas kernels, combine(): pl.pallas_call(combine_kernel, in_specs=[pl.BlockSpec(memory_space=pltpu....  2.36 us

profile of v1, /device:TPU:0, one launch (start us, length us, event | category | flops | bytes accessed | tf_op | source)
XLA Modules:
  0.0 66.0 jit_solution(2640356527224245913)
XLA Ops:
  0.0 0.0 copy-start.6
  0.0 0.0 copy-start
  0.0 2.8 %copy-done = bf16[64,3,16384]{2,0,1:T(8,128)(2,1)S(1)} copy-done((bf16[64,3,16384]{2,0,1:T(8,128)(2,1)S(1)}, bf16[64,3,16384]{2,0,1:T(8,128)(2,1)}, u32[]{:S(2)}) %copy-start) | copy-done | bytes 6291480
  2.8 0.0 copy-start.1
  2.8 0.9 %copy-done.1 = f32[3,16384]{1,0:T(4,128)S(1)} copy-done((f32[3,16384]{1,0:T(4,128)S(1)}, f32[3,16384]{1,0:T(4,128)}, u32[]{:S(2)}) %copy-start.1) | copy-done | bytes 196632
  3.8 0.0 copy-start.2
  3.8 0.8 %copy-done.2 = f32[35,256]{1,0:T(8,128)S(1)} copy-done((f32[35,256]{1,0:T(8,128)S(1)}, f32[35,256]{1,0:T(8,128)}, u32[]{:S(2)}) %copy-start.2) | copy-done | bytes 35864
  4.5 0.0 copy-start.3
  4.5 0.7 %copy-done.3 = s32[256]{0:T(256)S(1)} copy-done((s32[256]{0:T(256)S(1)}, s32[256]{0:T(256)}, u32[]{:S(2)}) %copy-start.3) | copy-done | bytes 1048
  5.2 0.0 copy-start.4
  5.2 0.7 copy-done.4
  5.9 0.0 copy-start.5
  5.9 0.7 copy-done.5
  6.5 9.1 %tiles.1 = bf16[32,56,128]{2,1,0:T(8,128)(2,1)S(1)} custom-call(s32[32]{0:T(128)S(1)} %copy-done.4, f32[16]{0:T(128)S(1)} %copy-done.5, s32[1,256]{1,0:T(1,128)S(1)} %bitcast.3, f32[35,256]{1,0:T(8,128)S(1)} %copy-done.2, bf16[3,64,16384]{2,1,0:T(8,128)(2,1)S(1)} %bitcast.2, f32[3,16384]{1,0:T(4,128)S(1)} %copy-done.1), custom_call_target="tpu_custom_call" | custom-call | tf_op jit(solution)/shard_map/tiles/pallas_call | solution.py:103
  15.6 12.9 %all_to_all.10.in_ref = bf16[32,56,128]{2,1,0:T(8,128)(2,1)S(1)} all-to-all(bf16[32,56,128]{2,1,0:T(8,128)(2,1)S(1)} %tiles.1), channel_id=1, replica_groups=mesh['x'=4,'z'=4,'y'=4,'core'=2] {'x'}, dimensions={0} | all-to-all | bytes 917504 | tf_op jit(solution)/shard_map/all_to_all | solution.py:221
  28.6 0.0 copy-done.6
  28.6 0.6 node_sum.1
  29.2 14.2 %all_gather.3.in_ref = bf16[64,56,128]{2,1,0:T(8,128)(2,1)S(1)} all-gather(bf16[8,56,128]{2,1,0:T(8,128)(2,1)S(1)} %node_sum.1), channel_id=1, replica_groups=mesh['x'=4,'z'=4,'y'=4,'core'=2] {'y','core'}, dimensions={0}, use_global_device_ids=true | all-gather | bytes 1032192 | tf_op jit(solution)/shard_map/all_gather | solution.py:223
  43.3 2.4 %combine.1 = bf16[48,56,128]{2,1,0:T(8,128)(2,1)S(1)} custom-call(bf16[64,56,128]{2,1,0:T(8,128)(2,1)S(1)} %all_gather.3.in_ref), custom_call_target="tpu_custom_call" | custom-call | tf_op jit(solution)/shard_map/combine/pallas_call | solution.py:176
  45.7 19.4 %all_to_all.11.in_ref = bf16[48,56,128]{2,1,0:T(8,128)(2,1)S(1)} all-to-all(bf16[48,56,128]{2,1,0:T(8,128)(2,1)S(1)} %combine.1), channel_id=1, replica_groups=mesh['x'=4,'z'=4,'y'=4,'core'=2] {'x','z'}, dimensions={0} | all-to-all | bytes 1376256 | tf_op jit(solution)/shard_map/all_to_all | solution.py:225
  65.1 0.2 owner_sum.1
  65.3 0.7 %copy.9 = f32[105,192]{0,1:T(8,128)} copy(f32[105,192]{1,0:T(8,128)S(1)} %owner_sum.1) | data formatting | bytes 161280 | tf_op jit(solution)/shard_map/owner_sum/pallas_call | solution.py:209
Async XLA Ops:
  0.0 28.6 %copy-start.6 = (s32[32]{0:T(128)S(1)}, s32[32]{0:T(128)}, u32[]{:S(2)}) copy-start(s32[32]{0:T(128)} %cells_ref.1) | copy-start | bytes 388
  0.0 2.8 %copy-start = (bf16[64,3,16384]{2,0,1:T(8,128)(2,1)S(1)}, bf16[64,3,16384]{2,0,1:T(8,128)(2,1)}, u32[]{:S(2)}) copy-start(bf16[64,3,16384]{2,0,1:T(8,128)(2,1)} %param.7) | copy-start | bytes 18874372
  2.8 0.9 %copy-start.1 = (f32[3,16384]{1,0:T(4,128)S(1)}, f32[3,16384]{1,0:T(4,128)}, u32[]{:S(2)}) copy-start(f32[3,16384]{1,0:T(4,128)} %coords_ref.1) | copy-start | bytes 589828
  3.8 0.8 %copy-start.2 = (f32[35,256]{1,0:T(8,128)S(1)}, f32[35,256]{1,0:T(8,128)}, u32[]{:S(2)}) copy-start(f32[35,256]{1,0:T(8,128)} %psi_ref.1) | copy-start | bytes 107524
  4.5 0.7 %copy-start.3 = (s32[256]{0:T(256)S(1)}, s32[256]{0:T(256)}, u32[]{:S(2)}) copy-start(s32[256]{0:T(256)} %param.10) | copy-start | bytes 3076
  5.2 0.7 copy-start.4
  5.9 0.7 copy-start.5

commit v2 on v1

v2 whole, which is shorter than its diff:
```python
import jax
import jax.numpy as jnp
from jax import lax
from jax.experimental import pallas as pl
from jax.experimental.pallas import tpu as pltpu
from jax.sharding import Mesh, PartitionSpec as P

K = 35
NQW = 16
CELLS = 384
PATCH_PTS = 512
NODE_Q = 64
STEP_PATCHES = 4
HALF = 16
ROWS = 56
LANES = 128
MIB = 1 << 20
KERNEL_VMEM = 57 * MIB


def bernstein_rows(coords, count):
    shape = (8, PATCH_PTS)
    u, v, w = [jnp.broadcast_to(row, shape) for row in coords]
    sub = lax.broadcasted_iota(jnp.int32, shape, 0)
    lane = lax.broadcasted_iota(jnp.int32, shape, 1)
    live = (lane < count).astype(jnp.float32)

    def basis(a):
        one = 1.0 - a
        return one * one * one, 3.0 * a * one * one, 3.0 * a * a * one, a * a * a

    w0, w1, w2, w3 = basis(w)
    low = sub & 3
    wl = jnp.where(low == 0, w0, jnp.where(low == 1, w1, jnp.where(low == 2, w2, w3))) * live
    v0, v1, v2, v3 = basis(v)
    first = sub < 4
    pair01 = jnp.where(first, v0, v1) * wl
    pair23 = jnp.where(first, v2, v3) * wl
    rows = []
    for b in basis(u):
        rows += [b * pair01, b * pair23]
    return jnp.concatenate(rows, axis=0)


def split(x):
    high = x.astype(jnp.bfloat16)
    return high, (x - high.astype(jnp.float32)).astype(jnp.bfloat16)


def weights(table_ref, index_ref, psi_ref, pad_ref, w_ref):
    index = index_ref[...]
    qweight = jnp.zeros(index.shape, jnp.float32)
    for j in range(NQW):
        qweight = jnp.where(index == j, table_ref[j], qweight)
    pad_ref[...] = jnp.zeros_like(pad_ref)
    pad_ref[0:K, :] = psi_ref[...] * qweight
    coef = pad_ref[...].astype(jnp.bfloat16)
    node = lax.axis_index("x")
    row = lax.broadcasted_iota(jnp.int32, (112, 40), 0)
    col = lax.broadcasted_iota(jnp.int32, (112, 40), 1)
    expand = ((row - 3 * col >= 0) & (row - 3 * col < 3)).astype(jnp.float32).astype(jnp.bfloat16)
    spread = jnp.dot(expand, coef, preferred_element_type=jnp.float32).astype(jnp.bfloat16)
    q = lax.broadcasted_iota(jnp.int32, (256, 384), 0)
    col = lax.broadcasted_iota(jnp.int32, (256, 384), 1)
    pick = (q == node * NODE_Q + (col & 63)).astype(jnp.float32).astype(jnp.bfloat16)
    full = jnp.dot(spread, pick, preferred_element_type=jnp.float32)
    row = lax.broadcasted_iota(jnp.int32, (112, 384), 0)
    col = lax.broadcasted_iota(jnp.int32, (112, 384), 1)
    w_ref[...] = jnp.where(row % 3 == (col // 64) % 3, full, 0.0).astype(jnp.bfloat16)


def tiles_of(half, step, counts_ref, sens_ref, coords_ref, w_ref, keep_ref, send_ref):
    lower = lax.broadcasted_iota(jnp.int32, (192, LANES), 1) < 64
    lower_slot = lower[:ROWS]
    w = w_ref[...]
    for pair in range(STEP_PATCHES // 2):
        both = []
        for i in (2 * pair, 2 * pair + 1):
            at = slice(i * PATCH_PTS, (i + 1) * PATCH_PTS)
            count = counts_ref[half * HALF + step * STEP_PATCHES + i]
            bern = bernstein_rows([coords_ref[c : c + 1, at] for c in range(3)], count)
            high, low = split(bern)
            rhs = jnp.concatenate([high, low], axis=0)
            lhs = jnp.concatenate([sens_ref[c, :, at] for c in range(3)], axis=0)
            s = lax.dot_general(lhs, rhs, (((1,), (1,)), ((), ())), preferred_element_type=jnp.float32)
            both.append(s + pltpu.roll(s, 64, 1))
        high, low = split(jnp.where(lower, both[0], both[1]))
        t = jnp.dot(w, jnp.concatenate([high, low], axis=0), preferred_element_type=jnp.float32)
        top, bottom = t[0:ROWS], t[ROWS : 2 * ROWS]
        first = jnp.where(lower_slot, top, pltpu.roll(bottom, 64, 1))
        second = jnp.where(lower_slot, pltpu.roll(top, 64, 1), bottom)
        for i, x in ((2 * pair, first), (2 * pair + 1, second)):
            keep_ref[STEP_PATCHES * step + i] = x
            send_ref[STEP_PATCHES * step + i] = x.astype(jnp.bfloat16)


HALF_STEPS = HALF // STEP_PATCHES
SMEM = pl.BlockSpec(memory_space=pltpu.SMEM)
VMEM = pl.BlockSpec(memory_space=pltpu.VMEM)
HBM = pl.BlockSpec(memory_space=pltpu.HBM)


def stream_copies(half, step, sens_ref, coords_ref, sens_buf, coords_buf, sem):
    points = STEP_PATCHES * PATCH_PTS
    at = pl.ds(pl.multiple_of((half * HALF_STEPS + step) * points, points), points)
    return (
        pltpu.make_async_copy(sens_ref.at[:, :, at], sens_buf.at[step], sem.at[step, 0]),
        pltpu.make_async_copy(coords_ref.at[:, at], coords_buf.at[step], sem.at[step, 1]),
    )


def half_tiles(half, counts_ref, sens_ref, coords_ref, w_ref, keep_hbm, send_hbm, sens_buf, coords_buf, sem, keep_ref, send_ref, out_sem):
    def out_copies(step):
        at = pl.ds(step * STEP_PATCHES, STEP_PATCHES)
        return (
            pltpu.make_async_copy(send_ref.at[at], send_hbm.at[at], out_sem.at[step, 0]),
            pltpu.make_async_copy(keep_ref.at[at], keep_hbm.at[at], out_sem.at[step, 1]),
        )

    def body(step, carry):
        for copy in stream_copies(half, step, sens_ref, coords_ref, sens_buf, coords_buf, sem):
            copy.wait()
        tiles_of(half, step, counts_ref, sens_buf.at[step], coords_buf.at[step], w_ref, keep_ref, send_ref)
        for copy in out_copies(step):
            copy.start()
        return carry

    lax.fori_loop(0, HALF_STEPS, body, 0)
    for step in range(HALF_STEPS):
        for copy in out_copies(step):
            copy.wait()


def start_stream(half, sens_ref, coords_ref, sens_buf, coords_buf, sem):
    for step in range(HALF_STEPS):
        for copy in stream_copies(half, step, sens_ref, coords_ref, sens_buf, coords_buf, sem):
            copy.start()


def first_kernel(
    counts_hbm, table_hbm, index_hbm, psi_hbm, sens_ref, coords_ref, w_hbm, keep_hbm, send_hbm,
    sens_buf, coords_buf, sem, keep_ref, send_ref, out_sem, counts_ref, w_ref, w_sem,
    table_ref, index_ref, psi_ref, small_sem, pad_ref
):
    pairs = ((table_hbm, table_ref), (index_hbm, index_ref), (psi_hbm, psi_ref), (counts_hbm, counts_ref))
    small = [pltpu.make_async_copy(a, b, small_sem.at[i]) for i, (a, b) in enumerate(pairs)]
    for copy in small:
        copy.start()
    start_stream(0, sens_ref, coords_ref, sens_buf, coords_buf, sem)
    for copy in small:
        copy.wait()
    weights(table_ref, index_ref, psi_ref, pad_ref, w_ref)
    w_copy = pltpu.make_async_copy(w_ref, w_hbm, w_sem)
    w_copy.start()
    bufs = (sens_buf, coords_buf, sem, keep_ref, send_ref, out_sem)
    half_tiles(0, counts_ref, sens_ref, coords_ref, w_ref, keep_hbm, send_hbm, *bufs)
    w_copy.wait()


def second_kernel(
    counts_hbm, w_hbm, sens_ref, coords_ref, keep_hbm, send_hbm,
    sens_buf, coords_buf, sem, keep_ref, send_ref, out_sem, counts_ref, w_ref, w_sem, small_sem
):
    small = [pltpu.make_async_copy(counts_hbm, counts_ref, small_sem), pltpu.make_async_copy(w_hbm, w_ref, w_sem)]
    for copy in small:
        copy.start()
    start_stream(1, sens_ref, coords_ref, sens_buf, coords_buf, sem)
    for copy in small:
        copy.wait()
    bufs = (sens_buf, coords_buf, sem, keep_ref, send_ref, out_sem)
    half_tiles(1, counts_ref, sens_ref, coords_ref, w_ref, keep_hbm, send_hbm, *bufs)


def partial_tiles(half, counts, first, second, sens, coords):
    points = STEP_PATCHES * PATCH_PTS
    tiles = [jax.ShapeDtypeStruct((HALF, ROWS, LANES), t) for t in (jnp.float32, jnp.bfloat16)]
    scratch = [
        pltpu.VMEM((HALF_STEPS, 3, NODE_Q, points), jnp.bfloat16),
        pltpu.VMEM((HALF_STEPS, 3, points), jnp.float32),
        pltpu.SemaphoreType.DMA((HALF_STEPS, 2)),
        pltpu.VMEM((HALF, ROWS, LANES), jnp.float32),
        pltpu.VMEM((HALF, ROWS, LANES), jnp.bfloat16),
        pltpu.SemaphoreType.DMA((HALF_STEPS, 2)),
        pltpu.SMEM(counts.shape, jnp.int32),
        pltpu.VMEM((112, 384), jnp.bfloat16),
        pltpu.SemaphoreType.DMA,
    ]
    kinds = dict(
        compiler_params=pltpu.CompilerParams(vmem_limit_bytes=KERNEL_VMEM),
        cost_estimate=pl.CostEstimate(flops=int(8e9), bytes_accessed=int(4e6), transcendentals=0),
    )
    if half == 0:
        table, index = first
        return pl.pallas_call(
            first_kernel,
            in_specs=[HBM] * 6,
            out_specs=[HBM] * 3,
            out_shape=[jax.ShapeDtypeStruct((112, 384), jnp.bfloat16)] + tiles,
            scratch_shapes=scratch
            + [
                pltpu.SMEM((NQW,), jnp.float32),
                pltpu.VMEM((1, 256), jnp.int32),
                pltpu.VMEM((K, 256), jnp.float32),
                pltpu.SemaphoreType.DMA((4,)),
                pltpu.VMEM((40, 256), jnp.float32),
            ],
            name="tiles_first",
            **kinds,
        )(counts, table, index.reshape(1, 256), second, sens, coords)
    return pl.pallas_call(
        second_kernel,
        in_specs=[HBM] * 4,
        out_specs=[HBM] * 2,
        out_shape=tiles,
        scratch_shapes=scratch + [pltpu.SemaphoreType.DMA],
        name="tiles_second",
        **kinds,
    )(counts, first, sens, coords)


def small_call(kernel, out_shape, in_specs, args, name, scratch=()):
    many = isinstance(out_shape, list)
    return pl.pallas_call(
        kernel,
        in_specs=in_specs,
        out_specs=[VMEM] * len(out_shape) if many else VMEM,
        out_shape=out_shape,
        scratch_shapes=list(scratch),
        compiler_params=pltpu.CompilerParams(vmem_limit_bytes=16 * MIB),
        name=name,
    )(*args)


def pair_sum_kernel(keep_ref, recv_ref, after_ref, sum_ref, send_ref):
    del after_ref
    total = keep_ref[...] + recv_ref[...].astype(jnp.float32)
    sum_ref[...] = total
    send_ref[...] = total.astype(jnp.bfloat16)


def pair_sum(keep, recv, after):
    out = [jax.ShapeDtypeStruct(keep.shape, t) for t in (jnp.float32, jnp.bfloat16)]
    in_specs = [VMEM, VMEM, pl.BlockSpec(memory_space=pl.ANY)]
    return small_call(pair_sum_kernel, out, in_specs, (keep, recv, after), "pair_sum")


def add_mine(cells_ref, dense_ref, count, tile):
    my_x, my_core = lax.axis_index("x"), lax.axis_index("core")

    def body(p, carry):
        cell = cells_ref[p]
        owner = cell // 3
        within = cell - 3 * owner

        @pl.when(((owner >> 5) == my_x) & ((owner & 1) == my_core))
        def _():
            at = ((owner & 31) >> 1) * 3 + within
            dense_ref[at] += tile(p)

        return carry

    lax.fori_loop(0, count, body, 0)


def own_kernel(cells_ref, a_ref, b_ref, dense_ref):
    dense_ref[...] = jnp.zeros_like(dense_ref)
    add_mine(cells_ref, dense_ref, HALF, lambda p: a_ref[p])
    add_mine(cells_ref.at[pl.ds(HALF, HALF)], dense_ref, HALF, lambda p: b_ref[p])


def other_kernel(cells_ref, dense_ref, a_ref, b_ref, out_ref, acc_ref):
    acc_ref[...] = dense_ref[...]
    add_mine(cells_ref, acc_ref, HALF, lambda p: a_ref[p].astype(jnp.float32))
    add_mine(cells_ref.at[pl.ds(HALF, HALF)], acc_ref, HALF, lambda p: b_ref[p].astype(jnp.float32))
    out_ref[...] = acc_ref[...].astype(jnp.bfloat16)


def owner_sum_kernel(in_ref, out_ref):
    lower = lax.broadcasted_iota(jnp.int32, (ROWS, LANES), 1) < 64
    cell = []
    for e in range(3):
        total = in_ref[e].astype(jnp.float32)
        for j in range(1, in_ref.shape[0] // 3):
            total = total + in_ref[3 * j + e].astype(jnp.float32)
        cell.append(total)
    a, b, c = cell
    ab = jnp.concatenate([jnp.where(lower, a, pltpu.roll(b, 64, 1)), jnp.where(lower, pltpu.roll(a, 64, 1), b)], axis=0)
    cc = jnp.concatenate([c, pltpu.roll(c, 64, 1)], axis=0)
    out_ref[0:128, :] = ab.T[:, 0 : 3 * K]
    out_ref[128:192, :] = cc.T[0:64, 0 : 3 * K]


def double(step):
    near, far = (1, 0, 3, 2), (3, 2, 1, 0)
    order = (near, far) if step == 0 else (far, near)
    return [(2 * x + core, 2 * order[core][x] + core) for x in range(4) for core in range(2)]


def local(sens, psi, quad_table, quad_index, counts, cells, coords):
    swap = [(0, 1), (1, 0)]
    other_cells = lax.ppermute(cells, "core", swap)
    sens = sens.transpose(1, 0, 2)
    w, keep_a, send_a = partial_tiles(0, counts, (quad_table, quad_index), psi, sens, coords)
    recv_a = lax.ppermute(send_a, ("x", "core"), double(0))
    keep_b, send_b = partial_tiles(1, counts, w, None, sens, coords)
    recv_b = lax.ppermute(send_b, ("x", "core"), double(0))
    keep_a, send_a = pair_sum(keep_a, recv_a, w)
    recv_a = lax.ppermute(send_a, ("x", "core"), double(1))
    keep_b, send_b = pair_sum(keep_b, recv_b, send_a)
    recv_b = lax.ppermute(send_b, ("x", "core"), double(1))
    full_a, send_a = pair_sum(keep_a, recv_a, send_b)
    recv_a = lax.ppermute(send_a, "core", swap)
    full_b, send_b = pair_sum(keep_b, recv_b, send_a)
    recv_b = lax.ppermute(send_b, "core", swap)
    slot = (48, ROWS, LANES)
    dense = small_call(own_kernel, jax.ShapeDtypeStruct(slot, jnp.float32), [SMEM, VMEM, VMEM], (cells, full_a, full_b), "own")
    out = jax.ShapeDtypeStruct(slot, jnp.bfloat16)
    args = (other_cells, dense, recv_a, recv_b)
    slots = small_call(other_kernel, out, [SMEM] + [VMEM] * 3, args, "other", [pltpu.VMEM(slot, jnp.float32)])
    slots = lax.all_to_all(slots, ("z", "y"), 0, 0, tiled=True)
    out = jax.ShapeDtypeStruct((192, 3 * K), jnp.float32)
    return small_call(owner_sum_kernel, out, [VMEM], (slots,), "owner_sum").T


def solution(mesh):
    inner = Mesh(mesh.devices.reshape(4, 4, 4, 2), ("x", "z", "y", "core"))
    surf = ("z", "y", "core")
    in_specs = (P("x", None, surf), P(), P(), P(), P(surf), P(surf), P(None, surf))
    out_specs = P(None, ("x",) + surf)
    return jax.shard_map(local, mesh=inner, in_specs=in_specs, out_specs=out_specs, check_vma=False)
```

time: 66.3 us -> 58.9 us (0.89)
  blocking collectives: 46.5 us -> 21.9 us
  waiting for transfers between devices: 0 us -> 10.7 us
  starting transfers between devices: 0 us -> 7.4 us
  local copies, waits for them, and re-layouts: 7.26 us -> 1.03 us
  Pallas kernels: 12.2 us -> 17.4 us
    all_gather x1 -> x0, blocking collectives: 14.2 us -> none  [local(): tiles = lax.all_gather(tiles, ('y', 'core'), axis=0, tiled=True)]
    ppermute x0 -> x7, waiting for transfers between devices: none -> 10.7 us  [the longest x1 5.61 us: local(): recv_b = lax.ppermute(send_b, ('x', 'core'), double(1))]
    all_to_all x2 -> x1, blocking collectives: 32.3 us -> 21.9 us  [local(): slots = lax.all_to_all(slots, ('z', 'y'), 0, 0, tiled=True)]
    ppermute x0 -> x7, starting transfers between devices: none -> 7.4 us  [the longest x1 2.91 us: local(): recv_a = lax.ppermute(send_a, ('x', 'core'), double(1))]
    unnamed x14 -> x8, local copies, waits for them, and re-layouts: 6.52 us -> 1.03 us
    pallas_call x4 -> x9, Pallas kernels: 12.2 us -> 17.4 us  [the longest x1 6.65 us: partial_tiles(): pl.pallas_call(second_kernel, in_specs=[HBM] * 4, out_specs=[HBM] * 2, ou...]
    pallas_call x1 -> x0, local copies, waits for them, and re-layouts: 0.74 us -> none  [owner_sum(): pl.pallas_call(owner_sum_kernel, in_specs=[pl.BlockSpec(memory_space=pltp...]
  transfers between devices with their start and end apart: 0 -> 7, of which waited for: 0 -> 2; matrix products, arithmetic and copies ran while one was open for 0% -> 0% of each run, Pallas kernels for 0% -> 14%
where the time goes in v2:
time: 58.9 us; the launch traced here: 58.5 us
  blocking collectives  21.9 us (37%)
  Pallas kernels  17.4 us (30%)
  waiting for transfers between devices  10.7 us (18%)
  starting transfers between devices  7.4 us (13%)
  local copies, waits for them, and re-layouts  1.03 us (2%)
    all_to_all x1, blocking collectives, local(): slots = lax.all_to_all(slots, ('z', 'y'), 0, 0, tiled=True)  21.9 us
    pallas_call x1, Pallas kernels, partial_tiles(): pl.pallas_call(second_kernel, in_specs=[HBM] * 4, out_specs=[HBM] * 2, ou...  6.65 us
    pallas_call x1, Pallas kernels, partial_tiles(): pl.pallas_call(first_kernel, in_specs=[HBM] * 6, out_specs=[HBM] * 3, out...  6.6 us
    ppermute x1, waiting for transfers between devices, local(): recv_b = lax.ppermute(send_b, ('x', 'core'), double(1))  5.61 us
    ppermute x1, waiting for transfers between devices, local(): recv_b = lax.ppermute(send_b, ('x', 'core'), double(0))  5.07 us
    pallas_call x7, Pallas kernels, small_call(): pl.pallas_call(kernel, in_specs=in_specs, out_specs=[VMEM] * len(out_shap...  4.12 us
    ppermute x1, starting transfers between devices, local(): recv_a = lax.ppermute(send_a, ('x', 'core'), double(1))  2.91 us
    ppermute x1, starting transfers between devices, local(): recv_a = lax.ppermute(send_a, ('x', 'core'), double(0))  1.65 us
  transfers between devices with their start and end apart: 7, of which 2 were waited for; matrix products, arithmetic and copies ran while one was open for 0% of the time, Pallas kernels for 14%

profile of v2, /device:TPU:0, one launch (start us, length us, event | category | flops | bytes accessed | tf_op | source)
XLA Modules:
  0.0 58.5 jit_solution(11971856737844714708)
XLA Ops:
  0.0 6.6 %tiles_first.1 = (bf16[112,384]{1,0:T(8,128)(2,1)}, f32[16,56,128]{2,1,0:T(8,128)}, bf16[16,56,128]{2,1,0:T(8,128)(2,1)}) custom-call(s32[32]{0:T(128)} %counts_hbm.3, f32[16]{0:T(128)} %table_hbm.1, s32[1,256]{1,0:T(1,128)} %bitcast.5, f32[35,256]{1,0:T(8,128)} %psi_hbm.1, bf16[3,64,16384]{2,1,0:T(8,128)(2,1)} %bitcast.3, f32[3,16384]{1,0:T(4,128)} %coords_ref.3), custom_call_target="tpu_custom_call" | custom-call | flops 8000000000 | bytes 4000000 | tf_op jit(solution)/shard_map/tiles_first/pallas_call | solution.py:194
  6.6 1.7 %collective-permute-start.1 = (bf16[16,56,128]{2,1,0:T(8,128)(2,1)}, bf16[16,56,128]{2,1,0:T(8,128)(2,1)S(1)}, u32[]{:S(2)}, u32[]{:S(2)}) collective-permute-start(bf16[16,56,128]{2,1,0:T(8,128)(2,1)} %get-tuple-element.19), channel_id=1, source_target_pairs={{0,32},{1,97},{32,0},{33,65},{64,96},{65,33},{96,64},{97,1},{2,34}... | collective-permute-start | bytes 688136 | tf_op jit(solution)/shard_map/ppermute | solution.py:304
  8.3 0.0 copy-start.1
  8.3 0.0 copy-start.2
  8.3 0.0 copy-start.3
  8.3 6.6 %tiles_second.1 = (f32[16,56,128]{2,1,0:T(8,128)}, bf16[16,56,128]{2,1,0:T(8,128)(2,1)}) custom-call(s32[32]{0:T(128)} %counts_hbm.3, bf16[112,384]{1,0:T(8,128)(2,1)} %get-tuple-element.20.after_ref.w_hbm, bf16[3,64,16384]{2,1,0:T(8,128)(2,1)} %bitcast.4, f32[3,16384]{1,0:T(4,128)} %coords_ref.3), custom_call_target="tpu_custom_call" | custom-call | flops 8000000000 | bytes 4000000 | tf_op jit(solution)/shard_map/tiles_second/pallas_call | solution.py:210
  14.9 0.5 collective-permute-start.3
  15.4 0.0 collective-permute-done.1.recv_ref
  15.5 0.0 copy-done.1
  15.5 0.0 copy-done.2
  15.5 0.1 pair_sum.4
  15.5 2.9 %collective-permute-start.2 = (bf16[16,56,128]{2,1,0:T(8,128)(2,1)S(1)}, bf16[16,56,128]{2,1,0:T(8,128)(2,1)S(1)}, u32[]{:S(2)}, u32[]{:S(2)}) collective-permute-start(bf16[16,56,128]{2,1,0:T(8,128)(2,1)S(1)} %get-tuple-element.22.after_ref), channel_id=1, source_target_pairs={{0,96},{1,33},{32,64},{33,1},{64,32},{65,97},{96,0},{97,65},{2,98}... | collective-permute-start | bytes 688136 | tf_op jit(solution)/shard_map/ppermute | solution.py:308
  18.5 5.1 %collective-permute-done.3.recv_ref = bf16[16,56,128]{2,1,0:T(8,128)(2,1)S(1)} collective-permute-done((bf16[16,56,128]{2,1,0:T(8,128)(2,1)}, bf16[16,56,128]{2,1,0:T(8,128)(2,1)S(1)}, u32[]{:S(2)}, u32[]{:S(2)}) %collective-permute-start.3) | collective-permute-done | bytes 229408 | tf_op jit(solution)/shard_map/ppermute | solution.py:306
  23.5 0.0 copy-start
  23.5 1.0 %copy-done = f32[16,56,128]{2,1,0:T(8,128)S(1)} copy-done((f32[16,56,128]{2,1,0:T(8,128)S(1)}, f32[16,56,128]{2,1,0:T(8,128)}, u32[]{:S(2)}) %copy-start) | copy-done | bytes 458776
  24.5 0.1 pair_sum.5
  24.6 1.6 %collective-permute-start.4 = (bf16[16,56,128]{2,1,0:T(8,128)(2,1)S(1)}, bf16[16,56,128]{2,1,0:T(8,128)(2,1)S(1)}, u32[]{:S(2)}, u32[]{:S(2)}) collective-permute-start(bf16[16,56,128]{2,1,0:T(8,128)(2,1)S(1)} %get-tuple-element.25.after_ref), channel_id=1, source_target_pairs={{0,96},{1,33},{32,64},{33,1},{64,32},{65,97},{96,0},{97,65},{2,98}... | collective-permute-start | bytes 688136 | tf_op jit(solution)/shard_map/ppermute | solution.py:310
  26.2 0.0 collective-permute-done.2.recv_ref
  26.2 0.1 pair_sum.6
  26.3 5.6 %collective-permute-done.4.recv_ref = bf16[16,56,128]{2,1,0:T(8,128)(2,1)S(1)} collective-permute-done((bf16[16,56,128]{2,1,0:T(8,128)(2,1)S(1)}, bf16[16,56,128]{2,1,0:T(8,128)(2,1)S(1)}, u32[]{:S(2)}, u32[]{:S(2)}) %collective-permute-start.4) | collective-permute-done | bytes 229408 | tf_op jit(solution)/shard_map/ppermute | solution.py:310
  31.9 0.1 pair_sum.7
  32.0 0.1 collective-permute-start.6
  32.1 0.5 collective-permute-start.5
  32.6 0.0 copy-done.3
  32.6 0.1 collective-permute-start
  32.7 1.5 %own.1.dense_ref = f32[48,56,128]{2,1,0:T(8,128)S(1)} custom-call(s32[32]{0:T(128)S(1)} %copy-done.3, f32[16,56,128]{2,1,0:T(8,128)S(1)} %get-tuple-element.26.a_ref, f32[16,56,128]{2,1,0:T(8,128)S(1)} %get-tuple-element.29.b_ref), custom_call_target="tpu_custom_call" | custom-call | tf_op jit(solution)/shard_map/own/pallas_call | solution.py:223
  34.2 0.0 collective-permute-done.cells_ref
  34.2 0.0 collective-permute-done.6.b_ref
  34.2 0.0 collective-permute-done.5.a_ref
  34.2 1.5 %other.1 = bf16[48,56,128]{2,1,0:T(8,128)(2,1)S(1)} custom-call(s32[32]{0:T(128)S(1)} %collective-permute-done.cells_ref, f32[48,56,128]{2,1,0:T(8,128)S(1)} %own.1.dense_ref, bf16[16,56,128]{2,1,0:T(8,128)(2,1)S(1)} %collective-permute-done.5.a_ref, bf16[16,56,128]{2,1,0:T(8,128)(2,1)S(1)} %collective-permute-done.6.b_ref), custom_call_target="tpu_custom_call" | custom-call | tf_op jit(solution)/shard_map/other/pallas_call | solution.py:223
  35.7 21.9 %all_to_all.5.in_ref = bf16[48,56,128]{2,1,0:T(8,128)(2,1)S(1)} all-to-all(bf16[48,56,128]{2,1,0:T(8,128)(2,1)S(1)} %other.1), channel_id=1, replica_groups=mesh['x'=4,'z'=4,'y'=4,'core'=2] {'z','y'}, dimensions={0} | all-to-all | bytes 1376256 | tf_op jit(solution)/shard_map/all_to_all | solution.py:320
  57.6 0.9 %owner_sum.1 = f32[192,105]{1,0:T(8,128)} custom-call(bf16[48,56,128]{2,1,0:T(8,128)(2,1)S(1)} %all_to_all.5.in_ref), custom_call_target="tpu_custom_call" | custom-call | tf_op jit(solution)/shard_map/owner_sum/pallas_call | solution.py:223
Async XLA Ops:
  6.6 8.8 %collective-permute-start.1 = (bf16[16,56,128]{2,1,0:T(8,128)(2,1)}, bf16[16,56,128]{2,1,0:T(8,128)(2,1)S(1)}, u32[]{:S(2)}, u32[]{:S(2)}) collective-permute-start(bf16[16,56,128]{2,1,0:T(8,128)(2,1)} %get-tuple-element.19), channel_id=1, source_target_pairs={{0,32},{1,97},{32,0},{33,65},{64,96},{65,33},{96,64},{97,1},{2,34}... | collective-permute-start | bytes 688136 | tf_op jit(solution)/shard_map/ppermute | solution.py:304
  8.3 7.2 %copy-start.1 = (f32[16,56,128]{2,1,0:T(8,128)S(1)}, f32[16,56,128]{2,1,0:T(8,128)}, u32[]{:S(2)}) copy-start(f32[16,56,128]{2,1,0:T(8,128)} %get-tuple-element.18.keep_ref) | copy-start | bytes 1376260
  8.3 7.2 %copy-start.2 = (bf16[112,384]{1,0:T(8,128)(2,1)S(1)}, bf16[112,384]{1,0:T(8,128)(2,1)}, u32[]{:S(2)}) copy-start(bf16[112,384]{1,0:T(8,128)(2,1)} %get-tuple-element.20.after_ref.w_hbm) | copy-start | bytes 258052
  8.3 24.3 %copy-start.3 = (s32[32]{0:T(128)S(1)}, s32[32]{0:T(128)}, u32[]{:S(2)}) copy-start(s32[32]{0:T(128)} %cells_ref.1) | copy-start | bytes 388
  14.9 8.6 %collective-permute-start.3 = (bf16[16,56,128]{2,1,0:T(8,128)(2,1)}, bf16[16,56,128]{2,1,0:T(8,128)(2,1)S(1)}, u32[]{:S(2)}, u32[]{:S(2)}) collective-permute-start(bf16[16,56,128]{2,1,0:T(8,128)(2,1)} %get-tuple-element.24), channel_id=1, source_target_pairs={{0,32},{1,97},{32,0},{33,65},{64,96},{65,33},{96,64},{97,1},{2,34}... | collective-permute-start | bytes 688136 | tf_op jit(solution)/shard_map/ppermute | solution.py:306
  15.5 10.7 %collective-permute-start.2 = (bf16[16,56,128]{2,1,0:T(8,128)(2,1)S(1)}, bf16[16,56,128]{2,1,0:T(8,128)(2,1)S(1)}, u32[]{:S(2)}, u32[]{:S(2)}) collective-permute-start(bf16[16,56,128]{2,1,0:T(8,128)(2,1)S(1)} %get-tuple-element.22.after_ref), channel_id=1, source_target_pairs={{0,96},{1,33},{32,64},{33,1},{64,32},{65,97},{96,0},{97,65},{2,98}... | collective-permute-start | bytes 688136 | tf_op jit(solution)/shard_map/ppermute | solution.py:308
  23.5 1.0 %copy-start = (f32[16,56,128]{2,1,0:T(8,128)S(1)}, f32[16,56,128]{2,1,0:T(8,128)}, u32[]{:S(2)}) copy-start(f32[16,56,128]{2,1,0:T(8,128)} %get-tuple-element.23.keep_ref) | copy-start | bytes 1376260
  24.6 7.3 %collective-permute-start.4 = (bf16[16,56,128]{2,1,0:T(8,128)(2,1)S(1)}, bf16[16,56,128]{2,1,0:T(8,128)(2,1)S(1)}, u32[]{:S(2)}, u32[]{:S(2)}) collective-permute-start(bf16[16,56,128]{2,1,0:T(8,128)(2,1)S(1)} %get-tuple-element.25.after_ref), channel_id=1, source_target_pairs={{0,96},{1,33},{32,64},{33,1},{64,32},{65,97},{96,0},{97,65},{2,98}... | collective-permute-start | bytes 688136 | tf_op jit(solution)/shard_map/ppermute | solution.py:310
  32.0 2.2 %collective-permute-start.6 = (bf16[16,56,128]{2,1,0:T(8,128)(2,1)S(1)}, bf16[16,56,128]{2,1,0:T(8,128)(2,1)S(1)}, u32[]{:S(2)}, u32[]{:S(2)}) collective-permute-start(bf16[16,56,128]{2,1,0:T(8,128)(2,1)S(1)} %get-tuple-element.30), channel_id=1, source_target_pairs={{0,1},{1,0},{2,3},{3,2},{4,5},{5,4},{6,7},{7,6},{8,9},{9,8},{10,11... | collective-permute-start | bytes 688136 | tf_op jit(solution)/shard_map/ppermute | solution.py:314
  32.1 2.1 %collective-permute-start.5 = (bf16[16,56,128]{2,1,0:T(8,128)(2,1)S(1)}, bf16[16,56,128]{2,1,0:T(8,128)(2,1)S(1)}, u32[]{:S(2)}, u32[]{:S(2)}) collective-permute-start(bf16[16,56,128]{2,1,0:T(8,128)(2,1)S(1)} %get-tuple-element.28.after_ref), channel_id=1, source_target_pairs={{0,1},{1,0},{2,3},{3,2},{4,5},{5,4},{6,7},{7,6},{8,9},{9,8},{10,11... | collective-permute-start | bytes 688136 | tf_op jit(solution)/shard_map/ppermute | solution.py:312
  32.6 1.6 %collective-permute-start = (s32[32]{0:T(128)S(1)}, s32[32]{0:T(128)S(1)}, u32[]{:S(2)}, u32[]{:S(2)}) collective-permute-start(s32[32]{0:T(128)S(1)} %copy-done.3), channel_id=1, source_target_pairs={{0,1},{1,0},{2,3},{3,2},{4,5},{5,4},{6,7},{7,6},{8,9},{9,8},{10,11... | collective-permute-start | bytes 392 | tf_op jit(solution)/shard_map/ppermute | solution.py:301

commit v3 on v2

v3 whole, which is shorter than its diff:
```python
import functools

import jax
import jax.numpy as jnp
from jax import lax
from jax.experimental import pallas as pl
from jax.experimental.pallas import tpu as pltpu
from jax.sharding import Mesh, PartitionSpec as P

K = 35
NQW = 16
CELLS = 384
PATCH_PTS = 512
NODE_Q = 64
PART = 16
CHUNK = 8
ROWS = 56
LANES = 128
MIB = 1 << 20
KERNEL_VMEM = 32 * MIB


def bernstein_rows(coords, count):
    shape = (8, PATCH_PTS)
    u, v, w = [jnp.broadcast_to(row, shape) for row in coords]
    sub = lax.broadcasted_iota(jnp.int32, shape, 0)
    lane = lax.broadcasted_iota(jnp.int32, shape, 1)
    live = (lane < count).astype(jnp.float32)

    def basis(a):
        one = 1.0 - a
        return one * one * one, 3.0 * a * one * one, 3.0 * a * a * one, a * a * a

    w0, w1, w2, w3 = basis(w)
    low = sub & 3
    wl = jnp.where(low == 0, w0, jnp.where(low == 1, w1, jnp.where(low == 2, w2, w3))) * live
    v0, v1, v2, v3 = basis(v)
    first = sub < 4
    pair01 = jnp.where(first, v0, v1) * wl
    pair23 = jnp.where(first, v2, v3) * wl
    rows = []
    for b in basis(u):
        rows += [b * pair01, b * pair23]
    return jnp.concatenate(rows, axis=0)


def split(x):
    high = x.astype(jnp.bfloat16)
    return high, (x - high.astype(jnp.float32)).astype(jnp.bfloat16)


SMEM = pl.BlockSpec(memory_space=pltpu.SMEM)
VMEM = pl.BlockSpec(memory_space=pltpu.VMEM)
HBM = pl.BlockSpec(memory_space=pltpu.HBM)
CHUNKS = PART // CHUNK
POINTS = CHUNK * PATCH_PTS


def weights(table_ref, index_ref, psi_ref, pad_ref, w_ref):
    index = index_ref[...]
    qweight = jnp.zeros(index.shape, jnp.float32)
    for j in range(NQW):
        qweight = jnp.where(index == j, table_ref[j], qweight)
    pad_ref[...] = jnp.zeros_like(pad_ref)
    pad_ref[0:K, :] = psi_ref[...] * qweight
    coef = pad_ref[...].astype(jnp.bfloat16)
    node = lax.axis_index("x")
    row = lax.broadcasted_iota(jnp.int32, (112, 40), 0)
    col = lax.broadcasted_iota(jnp.int32, (112, 40), 1)
    expand = ((row - 3 * col >= 0) & (row - 3 * col < 3)).astype(jnp.float32).astype(jnp.bfloat16)
    spread = jnp.dot(expand, coef, preferred_element_type=jnp.float32).astype(jnp.bfloat16)
    q = lax.broadcasted_iota(jnp.int32, (256, 192), 0)
    col = lax.broadcasted_iota(jnp.int32, (256, 192), 1)
    pick = (q == node * NODE_Q + (col & 63)).astype(jnp.float32).astype(jnp.bfloat16)
    full = jnp.dot(spread, pick, preferred_element_type=jnp.float32)
    row = lax.broadcasted_iota(jnp.int32, (112, 192), 0)
    col = lax.broadcasted_iota(jnp.int32, (112, 192), 1)
    w_ref[...] = jnp.where(row % 3 == col // 64, full, 0.0).astype(jnp.bfloat16)


def across(a, b):
    return lax.dot_general(a, b, (((1,), (1,)), ((), ())), preferred_element_type=jnp.float32)


def chunk_tiles(chunk, counts, sens_ref, coords_ref, w, keep_ref, send_ref):
    lower = lax.broadcasted_iota(jnp.int32, (ROWS, LANES), 1) < 64
    for pair in range(CHUNK // 2):
        sums = []
        for i in (2 * pair, 2 * pair + 1):
            at = slice(i * PATCH_PTS, (i + 1) * PATCH_PTS)
            bern = bernstein_rows([coords_ref[chunk, c : c + 1, at] for c in range(3)], counts(chunk * CHUNK + i))
            basis = jnp.concatenate(split(bern), axis=0)
            s = across(basis, sens_ref[chunk, :, :, at].reshape(3 * NODE_Q, PATCH_PTS))
            sums.append(s[0:64] + s[64:128])
        high, low = split(jnp.concatenate(sums, axis=0))
        t = across(w, high) + across(w, low)
        top, bottom = t[0:ROWS], t[ROWS : 2 * ROWS]
        first = jnp.where(lower, top, pltpu.roll(bottom, 64, 1))
        second = jnp.where(lower, pltpu.roll(top, 64, 1), bottom)
        for i, x in ((2 * pair, first), (2 * pair + 1, second)):
            keep_ref[chunk * CHUNK + i] = x
            send_ref[chunk * CHUNK + i] = x.astype(jnp.bfloat16)


def part_copies(part, chunk, sens_hbm, coords_hbm, sens_buf, coords_buf, sem):
    at = pl.ds((part * CHUNKS + chunk) * POINTS, POINTS)
    return (
        pltpu.make_async_copy(sens_hbm.at[:, :, at], sens_buf.at[chunk], sem.at[chunk, 0]),
        pltpu.make_async_copy(coords_hbm.at[:, at], coords_buf.at[chunk], sem.at[chunk, 1]),
    )


def first_kernel(
    counts_hbm, table_hbm, index_hbm, psi_hbm, sens_hbm, coords_hbm,
    keep_ref, send_ref, w_ref, count_rows, sens_next, coords_next,
    sens_buf, coords_buf, sem, next_sem, counts_ref, table_ref, index_ref, psi_ref, small_sem, pad_ref
):
    pairs = ((table_hbm, table_ref), (index_hbm, index_ref), (psi_hbm, psi_ref), (counts_hbm, counts_ref))
    small = [pltpu.make_async_copy(a, b, small_sem.at[i]) for i, (a, b) in enumerate(pairs)]
    mine = [part_copies(0, chunk, sens_hbm, coords_hbm, sens_buf, coords_buf, sem) for chunk in range(CHUNKS)]
    later = [part_copies(1, chunk, sens_hbm, coords_hbm, sens_next, coords_next, next_sem) for chunk in range(CHUNKS)]
    for copy in [*mine[0], *small] + [c for pair in mine[1:] for c in pair]:
        copy.start()
    for copy in small:
        copy.wait()
    for p in range(count_rows.shape[0]):
        count_rows[p : p + 1, :] = jnp.full((1, LANES), counts_ref[p], jnp.int32)
    weights(table_ref, index_ref, psi_ref, pad_ref, w_ref)
    w = w_ref[...]
    for chunk in range(CHUNKS):
        for copy in mine[chunk]:
            copy.wait()
        for copy in later[chunk]:
            copy.start()
        chunk_tiles(chunk, lambda p: counts_ref[p], sens_buf, coords_buf, w, keep_ref, send_ref)
    for pair in later:
        for copy in pair:
            copy.wait()


def later_kernel(part, last, count_rows, w_ref, sens_buf, coords_buf, *rest):
    if last:
        keep_ref, send_ref = rest
        later = []
    else:
        sens_hbm, coords_hbm, keep_ref, send_ref, sens_next, coords_next, next_sem = rest
        later = [
            part_copies(part + 1, chunk, sens_hbm, coords_hbm, sens_next, coords_next, next_sem)
            for chunk in range(CHUNKS)
        ]
    for pair in later:
        for copy in pair:
            copy.start()
    w = w_ref[...]

    def counts(p):
        row = count_rows[part * PART + p : part * PART + p + 1, :]
        return jnp.concatenate([row] * (PATCH_PTS // LANES), axis=1)

    for chunk in range(CHUNKS):
        chunk_tiles(chunk, counts, sens_buf, coords_buf, w, keep_ref, send_ref)
    for pair in later:
        for copy in pair:
            copy.wait()


def kinds():
    return dict(
        compiler_params=pltpu.CompilerParams(vmem_limit_bytes=KERNEL_VMEM),
        cost_estimate=pl.CostEstimate(flops=int(8e9), bytes_accessed=int(4e6), transcendentals=0),
    )


TILES = [jax.ShapeDtypeStruct((PART, ROWS, LANES), t) for t in (jnp.float32, jnp.bfloat16)]
BUFFERS = ((CHUNKS, 3, NODE_Q, POINTS), jnp.bfloat16), ((CHUNKS, 3, POINTS), jnp.float32)
STREAM = [jax.ShapeDtypeStruct(*b) for b in BUFFERS]


def first_part(counts, table, index, psi, sens, coords):
    return pl.pallas_call(
        first_kernel,
        in_specs=[HBM] * 6,
        out_specs=[VMEM] * 6,
        out_shape=TILES
        + [jax.ShapeDtypeStruct((112, 192), jnp.bfloat16), jax.ShapeDtypeStruct((counts.shape[0], LANES), jnp.int32)]
        + STREAM,
        scratch_shapes=[pltpu.VMEM(*b) for b in BUFFERS]
        + [
            pltpu.SemaphoreType.DMA((CHUNKS, 2)),
            pltpu.SemaphoreType.DMA((CHUNKS, 2)),
            pltpu.SMEM(counts.shape, jnp.int32),
            pltpu.SMEM((NQW,), jnp.float32),
            pltpu.VMEM((1, 256), jnp.int32),
            pltpu.VMEM((K, 256), jnp.float32),
            pltpu.SemaphoreType.DMA((4,)),
            pltpu.VMEM((40, 256), jnp.float32),
        ],
        name="tiles_0",
        **kinds(),
    )(counts, table, index, psi, sens, coords)


def later_part(part, count_rows, w, stream, sens, coords):
    last = (part + 1) * PART * PATCH_PTS == sens.shape[2]
    return pl.pallas_call(
        functools.partial(later_kernel, part, last),
        in_specs=[VMEM] * 4 + ([] if last else [HBM] * 2),
        out_specs=[VMEM] * (2 if last else 4),
        out_shape=TILES + ([] if last else STREAM),
        scratch_shapes=[] if last else [pltpu.SemaphoreType.DMA((CHUNKS, 2))],
        name="tiles_%d" % part,
        **kinds(),
    )(count_rows, w, *stream, *([] if last else [sens, coords]))


def all_parts(sens, psi, quad_table, quad_index, counts, coords):
    def hbm(x):
        return pltpu.with_memory_space_constraint(x, pltpu.HBM)

    sens, coords = hbm(sens.transpose(1, 0, 2)), hbm(coords)
    small = hbm(counts), hbm(quad_table), hbm(quad_index.reshape(1, 256)), hbm(psi)
    keep, send, w, count_rows, *stream = first_part(*small, sens, coords)
    yield keep, send, w
    for part in range(1, counts.shape[0] // PART):
        keep, send, *stream = later_part(part, count_rows, w, stream, sens, coords)
        yield keep, send, w


def small_call(kernel, out_shape, in_specs, args, name, scratch=()):
    many = isinstance(out_shape, list)
    return pl.pallas_call(
        kernel,
        in_specs=in_specs,
        out_specs=[VMEM] * len(out_shape) if many else VMEM,
        out_shape=out_shape,
        scratch_shapes=list(scratch),
        compiler_params=pltpu.CompilerParams(vmem_limit_bytes=16 * MIB),
        name=name,
    )(*args)


def pair_sum_kernel(keep_ref, recv_ref, after_ref, sum_ref, send_ref):
    del after_ref
    total = keep_ref[...] + recv_ref[...].astype(jnp.float32)
    sum_ref[...] = total
    send_ref[...] = total.astype(jnp.bfloat16)


def pair_sum(keep, recv, after):
    out = [jax.ShapeDtypeStruct(keep.shape, t) for t in (jnp.float32, jnp.bfloat16)]
    in_specs = [VMEM, VMEM, pl.BlockSpec(memory_space=pl.ANY)]
    return small_call(pair_sum_kernel, out, in_specs, (keep, recv, after), "pair_sum")


def add_mine(cells_ref, start, dense_ref, tiles_ref):
    my_x, my_core = lax.axis_index("x"), lax.axis_index("core")
    for p in range(PART):
        cell = cells_ref[start + p]
        owner = lax.shift_right_logical(cell * 43691, 17)
        within = cell - 3 * owner

        @pl.when(((owner >> 5) == my_x) & ((owner & 1) == my_core))
        def _():
            at = ((owner & 31) >> 1) * 3 + within
            dense_ref[at] += tiles_ref[p].astype(jnp.float32)


def own_kernel(cells_ref, *refs):
    *parts, dense_ref = refs
    dense_ref[...] = jnp.zeros_like(dense_ref)
    for i, part in enumerate(parts):
        add_mine(cells_ref, i * PART, dense_ref, part)


def other_kernel(cells_ref, in_ref, *refs):
    *parts, out_ref, dense_ref = refs
    dense_ref[...] = in_ref[...]
    for i, part in enumerate(parts):
        add_mine(cells_ref, i * PART, dense_ref, part)
    out_ref[...] = dense_ref[...].astype(jnp.bfloat16)


def owner_sum_kernel(in_ref, out_ref):
    lower = lax.broadcasted_iota(jnp.int32, (ROWS, LANES), 1) < 64
    cell = []
    for e in range(3):
        total = in_ref[e].astype(jnp.float32)
        for j in range(1, in_ref.shape[0] // 3):
            total = total + in_ref[3 * j + e].astype(jnp.float32)
        cell.append(total)
    a, b, c = cell
    ab = jnp.concatenate([jnp.where(lower, a, pltpu.roll(b, 64, 1)), jnp.where(lower, pltpu.roll(a, 64, 1), b)], axis=0)
    cc = jnp.concatenate([c, pltpu.roll(c, 64, 1)], axis=0)
    out_ref[0:128, :] = ab.T[:, 0 : 3 * K]
    out_ref[128:192, :] = cc.T[0:64, 0 : 3 * K]


def double(step):
    near, far = (1, 0, 3, 2), (3, 2, 1, 0)
    order = (near, far) if step == 0 else (far, near)
    return [(2 * x + core, 2 * order[core][x] + core) for x in range(4) for core in range(2)]


def local(sens, psi, quad_table, quad_index, counts, cells, coords):
    swap = [(0, 1), (1, 0)]

    def smem(x):
        return pltpu.with_memory_space_constraint(x, pltpu.SMEM)

    other_cells = lax.ppermute(cells, "core", swap)
    held = []
    for keep, send, w in all_parts(sens, psi, quad_table, quad_index, counts, coords):
        held.append((keep, lax.ppermute(send, ("x", "core"), double(0))))
    after = w
    for i, (keep, recv) in enumerate(held):
        keep, after = pair_sum(keep, recv, after)
        held[i] = keep, lax.ppermute(after, ("x", "core"), double(1))
    for i, (keep, recv) in enumerate(held):
        full, after = pair_sum(keep, recv, after)
        held[i] = full, lax.ppermute(after, "core", swap)
    full, swapped = zip(*held)
    slot = (48, ROWS, LANES)
    specs = [VMEM] * len(full)
    dense = jax.ShapeDtypeStruct(slot, jnp.float32)
    dense = small_call(own_kernel, dense, [SMEM] + specs, (smem(cells), *full), "own")
    slots = jax.ShapeDtypeStruct(slot, jnp.bfloat16)
    args = (smem(other_cells), dense, *swapped)
    slots = small_call(other_kernel, slots, [SMEM, VMEM] + specs, args, "other", [pltpu.VMEM(slot, jnp.float32)])
    slots = lax.all_to_all(slots, ("z", "y"), 0, 0, tiled=True)
    out = jax.ShapeDtypeStruct((192, 3 * K), jnp.float32)
    return small_call(owner_sum_kernel, out, [VMEM], (slots,), "owner_sum").T


def solution(mesh):
    inner = Mesh(mesh.devices.reshape(4, 4, 4, 2), ("x", "z", "y", "core"))
    surf = ("z", "y", "core")
    in_specs = (P("x", None, surf), P(), P(), P(), P(surf), P(surf), P(None, surf))
    out_specs = P(None, ("x",) + surf)
    return jax.shard_map(local, mesh=inner, in_specs=in_specs, out_specs=out_specs, check_vma=False)
```

time: 58.9 us -> 50 us (0.85)
  Pallas kernels: 17.4 us -> 10.7 us
  local copies, waits for them, and re-layouts: 1.03 us -> 0.01 us
  blocking collectives: 21.9 us -> 21.3 us
    pallas_call x2, Pallas kernels: 13.2 us -> 7.5 us  [the longest x1 4.86 us: first_part(): pl.pallas_call(first_kernel, in_specs=[HBM] * 6, out_specs=[VMEM] * 6, ou...]
    unnamed x8 -> x2, local copies, waits for them, and re-layouts: 1.03 us -> 0.01 us
    pallas_call x7, Pallas kernels: 4.12 us -> 3.21 us  [small_call(): pl.pallas_call(kernel, in_specs=in_specs, out_specs=[VMEM] * len(out_shap...]
  transfers between devices with their start and end apart: 7 -> 7, of which waited for: 2 -> 5; matrix products, arithmetic and copies ran while one was open for 0% -> 0% of each run, Pallas kernels for 14% -> 8%
where the time goes in v3:
time: 50 us; the launch traced here: 49.8 us
  blocking collectives  21.3 us (43%)
  Pallas kernels  10.7 us (21%)
  waiting for transfers between devices  10.7 us (21%)
  starting transfers between devices  6.97 us (14%)
    all_to_all x1, blocking collectives, local(): slots = lax.all_to_all(slots, ('z', 'y'), 0, 0, tiled=True)  21.3 us
    ppermute x2, waiting for transfers between devices, local(): held[i] = (keep, lax.ppermute(after, ('x', 'core'), double(1)))  6.05 us
    pallas_call x1, Pallas kernels, first_part(): pl.pallas_call(first_kernel, in_specs=[HBM] * 6, out_specs=[VMEM] * 6, ou...  4.86 us
    ppermute x2, waiting for transfers between devices, local(): held.append((keep, lax.ppermute(send, ('x', 'core'), double(0))))  4.42 us
    ppermute x2, starting transfers between devices, local(): held[i] = (keep, lax.ppermute(after, ('x', 'core'), double(1)))  4.12 us
    pallas_call x7, Pallas kernels, small_call(): pl.pallas_call(kernel, in_specs=in_specs, out_specs=[VMEM] * len(out_shap...  3.21 us
    pallas_call x1, Pallas kernels, later_part(): pl.pallas_call(functools.partial(later_kernel, part, last), in_specs=[VME...  2.65 us
    ppermute x2, starting transfers between devices, local(): held.append((keep, lax.ppermute(send, ('x', 'core'), double(0))))  2.18 us
  transfers between devices with their start and end apart: 7, of which 5 were waited for; matrix products, arithmetic and copies ran while one was open for 0% of the time, Pallas kernels for 8%

profile of v3, /device:TPU:0, one launch (start us, length us, event | category | flops | bytes accessed | tf_op | source)
XLA Modules:
  0.0 49.8 jit_solution(5388432591163703685)
XLA Ops:
  0.0 4.9 %tiles_0.1 = (f32[16,56,128]{2,1,0:T(8,128)S(1)}, bf16[16,56,128]{2,1,0:T(8,128)(2,1)S(1)}, bf16[112,192]{1,0:T(8,128)(2,1)S(1)}, s32[32,128]{1,0:T(8,128)S(1)},...) custom-call(s32[32]{0:T(128)} %counts_hbm.1, f32[16]{0:T(128)} %table_hbm.1, s32[1,256]{1,0:T(1,128)} %bitcast.4, ...), custom_call_target="tpu_custom_call" | custom-call | flops 8000000000 | bytes 4000000 | tf_op jit(solution)/shard_map/tiles_0/pallas_call | solution.py:180
  4.9 1.7 %collective-permute-start.1 = (bf16[16,56,128]{2,1,0:T(8,128)(2,1)S(1)}, bf16[16,56,128]{2,1,0:T(8,128)(2,1)S(1)}, u32[]{:S(2)}, u32[]{:S(2)}) collective-permute-start(bf16[16,56,128]{2,1,0:T(8,128)(2,1)S(1)} %get-tuple-element.22), channel_id=1, source_target_pairs={{0,32},{1,97},{32,0},{33,65},{64,96},{65,33},{96,64},{97,1},{2,34}... | collective-permute-start | bytes 688136 | tf_op jit(solution)/shard_map/ppermute | solution.py:313
  6.5 2.6 %tiles_1.1 = (f32[16,56,128]{2,1,0:T(8,128)S(1)}, bf16[16,56,128]{2,1,0:T(8,128)(2,1)S(1)}) custom-call(s32[32,128]{1,0:T(8,128)S(1)} %get-tuple-element.26.count_rows, bf16[112,192]{1,0:T(8,128)(2,1)S(1)} %get-tuple-element.23.after_ref.w_ref, bf16[2,3,64,4096]{3,2,1,0:T(8,128)(2,1)S(1)} %get-tuple-element.27.sens_buf, ...), custom_call_target="tpu_custom_call" | custom-call | flops 8000000000 | bytes 4000000 | tf_op jit(solution)/shard_map/tiles_1/pallas_call | solution.py:205
  9.2 0.0 copy-start
  9.2 0.5 %collective-permute-start.3 = (bf16[16,56,128]{2,1,0:T(8,128)(2,1)S(1)}, bf16[16,56,128]{2,1,0:T(8,128)(2,1)S(1)}, u32[]{:S(2)}, u32[]{:S(2)}) collective-permute-start(bf16[16,56,128]{2,1,0:T(8,128)(2,1)S(1)} %get-tuple-element.30), channel_id=1, source_target_pairs={{0,32},{1,97},{32,0},{33,65},{64,96},{65,33},{96,64},{97,1},{2,34}... | collective-permute-start | bytes 688136 | tf_op jit(solution)/shard_map/ppermute | solution.py:313
  9.7 1.2 %collective-permute-done.1.recv_ref = bf16[16,56,128]{2,1,0:T(8,128)(2,1)S(1)} collective-permute-done((bf16[16,56,128]{2,1,0:T(8,128)(2,1)S(1)}, bf16[16,56,128]{2,1,0:T(8,128)(2,1)S(1)}, u32[]{:S(2)}, u32[]{:S(2)}) %collective-permute-start.1) | collective-permute-done | bytes 229408 | tf_op jit(solution)/shard_map/ppermute | solution.py:313
  11.0 0.1 pair_sum.4
  11.0 2.9 %collective-permute-start.2 = (bf16[16,56,128]{2,1,0:T(8,128)(2,1)S(1)}, bf16[16,56,128]{2,1,0:T(8,128)(2,1)S(1)}, u32[]{:S(2)}, u32[]{:S(2)}) collective-permute-start(bf16[16,56,128]{2,1,0:T(8,128)(2,1)S(1)} %get-tuple-element.25.after_ref), channel_id=1, source_target_pairs={{0,96},{1,33},{32,64},{33,1},{64,32},{65,97},{96,0},{97,65},{2,98}... | collective-permute-start | bytes 688136 | tf_op jit(solution)/shard_map/ppermute | solution.py:317
  14.0 3.2 %collective-permute-done.3.recv_ref = bf16[16,56,128]{2,1,0:T(8,128)(2,1)S(1)} collective-permute-done((bf16[16,56,128]{2,1,0:T(8,128)(2,1)S(1)}, bf16[16,56,128]{2,1,0:T(8,128)(2,1)S(1)}, u32[]{:S(2)}, u32[]{:S(2)}) %collective-permute-start.3) | collective-permute-done | bytes 229408 | tf_op jit(solution)/shard_map/ppermute | solution.py:313
  17.1 0.1 pair_sum.5
  17.2 1.2 %collective-permute-start.4 = (bf16[16,56,128]{2,1,0:T(8,128)(2,1)S(1)}, bf16[16,56,128]{2,1,0:T(8,128)(2,1)S(1)}, u32[]{:S(2)}, u32[]{:S(2)}) collective-permute-start(bf16[16,56,128]{2,1,0:T(8,128)(2,1)S(1)} %get-tuple-element.31.after_ref), channel_id=1, source_target_pairs={{0,96},{1,33},{32,64},{33,1},{64,32},{65,97},{96,0},{97,65},{2,98}... | collective-permute-start | bytes 688136 | tf_op jit(solution)/shard_map/ppermute | solution.py:317
  18.4 0.4 collective-permute-done.2.recv_ref
  18.8 0.1 pair_sum.6
  18.9 5.6 %collective-permute-done.4.recv_ref = bf16[16,56,128]{2,1,0:T(8,128)(2,1)S(1)} collective-permute-done((bf16[16,56,128]{2,1,0:T(8,128)(2,1)S(1)}, bf16[16,56,128]{2,1,0:T(8,128)(2,1)S(1)}, u32[]{:S(2)}, u32[]{:S(2)}) %collective-permute-start.4) | collective-permute-done | bytes 229408 | tf_op jit(solution)/shard_map/ppermute | solution.py:317
  24.5 0.1 pair_sum.7
  24.6 0.1 collective-permute-start.6
  24.7 0.5 collective-permute-start.5
  25.2 0.0 copy-done
  25.2 0.1 collective-permute-start
  25.3 1.0 %own.1.in_ref = f32[48,56,128]{2,1,0:T(8,128)S(1)} custom-call(s32[32]{0:T(128)S(1)} %copy-done, f32[16,56,128]{2,1,0:T(8,128)S(1)} %get-tuple-element.32.refs_0_, f32[16,56,128]{2,1,0:T(8,128)S(1)} %get-tuple-element.35.refs_1_), custom_call_target="tpu_custom_call" | custom-call | tf_op jit(solution)/shard_map/own/pallas_call | solution.py:231
  26.3 0.2 collective-permute-done.cells_ref
  26.5 0.0 collective-permute-done.6.refs_1_
  26.5 0.0 collective-permute-done.5.refs_0_
  26.5 1.1 %other.1 = bf16[48,56,128]{2,1,0:T(8,128)(2,1)S(1)} custom-call(s32[32]{0:T(128)S(1)} %collective-permute-done.cells_ref, f32[48,56,128]{2,1,0:T(8,128)S(1)} %own.1.in_ref, bf16[16,56,128]{2,1,0:T(8,128)(2,1)S(1)} %collective-permute-done.5.refs_0_, bf16[16,56,128]{2,1,0:T(8,128)(2,1)S(1)} %collective-permute-done.6.refs_1_), custom_call_target="tpu_custom_call" | custom-call | tf_op jit(solution)/shard_map/other/pallas_call | solution.py:231
  27.6 21.3 %all_to_all.5.in_ref = bf16[48,56,128]{2,1,0:T(8,128)(2,1)S(1)} all-to-all(bf16[48,56,128]{2,1,0:T(8,128)(2,1)S(1)} %other.1), channel_id=1, replica_groups=mesh['x'=4,'z'=4,'y'=4,'core'=2] {'z','y'}, dimensions={0} | all-to-all | bytes 1376256 | tf_op jit(solution)/shard_map/all_to_all | solution.py:329
  48.9 0.9 %owner_sum.1 = f32[192,105]{1,0:T(8,128)} custom-call(bf16[48,56,128]{2,1,0:T(8,128)(2,1)S(1)} %all_to_all.5.in_ref), custom_call_target="tpu_custom_call" | custom-call | tf_op jit(solution)/shard_map/owner_sum/pallas_call | solution.py:231
Async XLA Ops:
  4.9 6.1 %collective-permute-start.1 = (bf16[16,56,128]{2,1,0:T(8,128)(2,1)S(1)}, bf16[16,56,128]{2,1,0:T(8,128)(2,1)S(1)}, u32[]{:S(2)}, u32[]{:S(2)}) collective-permute-start(bf16[16,56,128]{2,1,0:T(8,128)(2,1)S(1)} %get-tuple-element.22), channel_id=1, source_target_pairs={{0,32},{1,97},{32,0},{33,65},{64,96},{65,33},{96,64},{97,1},{2,34}... | collective-permute-start | bytes 688136 | tf_op jit(solution)/shard_map/ppermute | solution.py:313
  9.2 16.0 %copy-start = (s32[32]{0:T(128)S(1)}, s32[32]{0:T(128)}, u32[]{:S(2)}) copy-start(s32[32]{0:T(128)} %cells_ref.1) | copy-start | bytes 388
  9.2 7.9 %collective-permute-start.3 = (bf16[16,56,128]{2,1,0:T(8,128)(2,1)S(1)}, bf16[16,56,128]{2,1,0:T(8,128)(2,1)S(1)}, u32[]{:S(2)}, u32[]{:S(2)}) collective-permute-start(bf16[16,56,128]{2,1,0:T(8,128)(2,1)S(1)} %get-tuple-element.30), channel_id=1, source_target_pairs={{0,32},{1,97},{32,0},{33,65},{64,96},{65,33},{96,64},{97,1},{2,34}... | collective-permute-start | bytes 688136 | tf_op jit(solution)/shard_map/ppermute | solution.py:313
  11.0 7.8 %collective-permute-start.2 = (bf16[16,56,128]{2,1,0:T(8,128)(2,1)S(1)}, bf16[16,56,128]{2,1,0:T(8,128)(2,1)S(1)}, u32[]{:S(2)}, u32[]{:S(2)}) collective-permute-start(bf16[16,56,128]{2,1,0:T(8,128)(2,1)S(1)} %get-tuple-element.25.after_ref), channel_id=1, source_target_pairs={{0,96},{1,33},{32,64},{33,1},{64,32},{65,97},{96,0},{97,65},{2,98}... | collective-permute-start | bytes 688136 | tf_op jit(solution)/shard_map/ppermute | solution.py:317
  17.2 7.3 %collective-permute-start.4 = (bf16[16,56,128]{2,1,0:T(8,128)(2,1)S(1)}, bf16[16,56,128]{2,1,0:T(8,128)(2,1)S(1)}, u32[]{:S(2)}, u32[]{:S(2)}) collective-permute-start(bf16[16,56,128]{2,1,0:T(8,128)(2,1)S(1)} %get-tuple-element.31.after_ref), channel_id=1, source_target_pairs={{0,96},{1,33},{32,64},{33,1},{64,32},{65,97},{96,0},{97,65},{2,98}... | collective-permute-start | bytes 688136 | tf_op jit(solution)/shard_map/ppermute | solution.py:317
  24.6 1.9 %collective-permute-start.6 = (bf16[16,56,128]{2,1,0:T(8,128)(2,1)S(1)}, bf16[16,56,128]{2,1,0:T(8,128)(2,1)S(1)}, u32[]{:S(2)}, u32[]{:S(2)}) collective-permute-start(bf16[16,56,128]{2,1,0:T(8,128)(2,1)S(1)} %get-tuple-element.36), channel_id=1, source_target_pairs={{0,1},{1,0},{2,3},{3,2},{4,5},{5,4},{6,7},{7,6},{8,9},{9,8},{10,11... | collective-permute-start | bytes 688136 | tf_op jit(solution)/shard_map/ppermute | solution.py:320
  24.7 1.8 %collective-permute-start.5 = (bf16[16,56,128]{2,1,0:T(8,128)(2,1)S(1)}, bf16[16,56,128]{2,1,0:T(8,128)(2,1)S(1)}, u32[]{:S(2)}, u32[]{:S(2)}) collective-permute-start(bf16[16,56,128]{2,1,0:T(8,128)(2,1)S(1)} %get-tuple-element.34.after_ref), channel_id=1, source_target_pairs={{0,1},{1,0},{2,3},{3,2},{4,5},{5,4},{6,7},{7,6},{8,9},{9,8},{10,11... | collective-permute-start | bytes 688136 | tf_op jit(solution)/shard_map/ppermute | solution.py:320
  25.2 1.3 %collective-permute-start = (s32[32]{0:T(128)S(1)}, s32[32]{0:T(128)S(1)}, u32[]{:S(2)}, u32[]{:S(2)}) collective-permute-start(s32[32]{0:T(128)S(1)} %copy-done), channel_id=1, source_target_pairs={{0,1},{1,0},{2,3},{3,2},{4,5},{5,4},{6,7},{7,6},{8,9},{9,8},{10,11... | collective-permute-start | bytes 392 | tf_op jit(solution)/shard_map/ppermute | solution.py:310

commit v4 on v3

--- a/solution.py
+++ b/solution.py
@@ -13,7 +13,8 @@
 PATCH_PTS = 512
 NODE_Q = 64
 PART = 16
-CHUNK = 8
+FIRST_CHUNKS = (4, 12)
+NEXT_CHUNKS = (16,)
 ROWS = 56
 LANES = 128
 MIB = 1 << 20
@@ -52,8 +53,6 @@
 SMEM = pl.BlockSpec(memory_space=pltpu.SMEM)
 VMEM = pl.BlockSpec(memory_space=pltpu.VMEM)
 HBM = pl.BlockSpec(memory_space=pltpu.HBM)
-CHUNKS = PART // CHUNK
-POINTS = CHUNK * PATCH_PTS
 
 
 def weights(table_ref, index_ref, psi_ref, pad_ref, w_ref):
@@ -82,32 +81,44 @@
     return lax.dot_general(a, b, (((1,), (1,)), ((), ())), preferred_element_type=jnp.float32)
 
 
-def chunk_tiles(chunk, counts, sens_ref, coords_ref, w, keep_ref, send_ref):
+def chunk_tiles(patches, counts, sens_ref, coords_ref, w, keep_ref, send_ref):
     lower = lax.broadcasted_iota(jnp.int32, (ROWS, LANES), 1) < 64
-    for pair in range(CHUNK // 2):
+    for pair in range(patches.start, patches.stop, 2):
         sums = []
-        for i in (2 * pair, 2 * pair + 1):
+        for i in (pair, pair + 1):
             at = slice(i * PATCH_PTS, (i + 1) * PATCH_PTS)
-            bern = bernstein_rows([coords_ref[chunk, c : c + 1, at] for c in range(3)], counts(chunk * CHUNK + i))
+            bern = bernstein_rows([coords_ref[c : c + 1, at] for c in range(3)], counts(i))
             basis = jnp.concatenate(split(bern), axis=0)
-            s = across(basis, sens_ref[chunk, :, :, at].reshape(3 * NODE_Q, PATCH_PTS))
+            s = across(basis, sens_ref[:, :, at].reshape(3 * NODE_Q, PATCH_PTS))
             sums.append(s[0:64] + s[64:128])
         high, low = split(jnp.concatenate(sums, axis=0))
         t = across(w, high) + across(w, low)
         top, bottom = t[0:ROWS], t[ROWS : 2 * ROWS]
         first = jnp.where(lower, top, pltpu.roll(bottom, 64, 1))
         second = jnp.where(lower, pltpu.roll(top, 64, 1), bottom)
-        for i, x in ((2 * pair, first), (2 * pair + 1, second)):
-            keep_ref[chunk * CHUNK + i] = x
-            send_ref[chunk * CHUNK + i] = x.astype(jnp.bfloat16)
-
-
-def part_copies(part, chunk, sens_hbm, coords_hbm, sens_buf, coords_buf, sem):
-    at = pl.ds((part * CHUNKS + chunk) * POINTS, POINTS)
-    return (
-        pltpu.make_async_copy(sens_hbm.at[:, :, at], sens_buf.at[chunk], sem.at[chunk, 0]),
-        pltpu.make_async_copy(coords_hbm.at[:, at], coords_buf.at[chunk], sem.at[chunk, 1]),
-    )
+        for i, x in ((pair, first), (pair + 1, second)):
+            keep_ref[i] = x
+            send_ref[i] = x.astype(jnp.bfloat16)
+
+
+def chunks_of(sizes):
+    ends = [sum(sizes[: i + 1]) for i in range(len(sizes))]
+    return [range(end - size, end) for end, size in zip(ends, sizes)]
+
+
+def part_copies(part, sizes, sens_hbm, coords_hbm, sens_buf, coords_buf, sem):
+    copies = []
+    for i, patches in enumerate(chunks_of(sizes)):
+        count = len(patches) * PATCH_PTS
+        here = pl.ds(patches.start * PATCH_PTS, count)
+        there = pl.ds((part * PART + patches.start) * PATCH_PTS, count)
+        copies.append(
+            (
+                pltpu.make_async_copy(sens_hbm.at[:, :, there], sens_buf.at[:, :, here], sem.at[i, 0]),
+                pltpu.make_async_copy(coords_hbm.at[:, there], coords_buf.at[:, here], sem.at[i, 1]),
+            )
+        )
+    return copies
 
 
 def first_kernel(
@@ -117,8 +128,8 @@
 ):
     pairs = ((table_hbm, table_ref), (index_hbm, index_ref), (psi_hbm, psi_ref), (counts_hbm, counts_ref))
     small = [pltpu.make_async_copy(a, b, small_sem.at[i]) for i, (a, b) in enumerate(pairs)]
-    mine = [part_copies(0, chunk, sens_hbm, coords_hbm, sens_buf, coords_buf, sem) for chunk in range(CHUNKS)]
-    later = [part_copies(1, chunk, sens_hbm, coords_hbm, sens_next, coords_next, next_sem) for chunk in range(CHUNKS)]
+    mine = part_copies(0, FIRST_CHUNKS, sens_hbm, coords_hbm, sens_buf, coords_buf, sem)
+    later = part_copies(1, NEXT_CHUNKS, sens_hbm, coords_hbm, sens_next, coords_next, next_sem)
     for copy in [*mine[0], *small] + [c for pair in mine[1:] for c in pair]:
         copy.start()
     for copy in small:
@@ -127,12 +138,12 @@
         count_rows[p : p + 1, :] = jnp.full((1, LANES), counts_ref[p], jnp.int32)
     weights(table_ref, index_ref, psi_ref, pad_ref, w_ref)
     w = w_ref[...]
-    for chunk in range(CHUNKS):
-        for copy in mine[chunk]:
+    for i, patches in enumerate(chunks_of(FIRST_CHUNKS)):
+        for copy in mine[i]:
             copy.wait()
-        for copy in later[chunk]:
+        for copy in later[i] if i < len(later) else ():
             copy.start()
-        chunk_tiles(chunk, lambda p: counts_ref[p], sens_buf, coords_buf, w, keep_ref, send_ref)
+        chunk_tiles(patches, lambda p: counts_ref[p], sens_buf, coords_buf, w, keep_ref, send_ref)
     for pair in later:
         for copy in pair:
             copy.wait()
@@ -144,10 +155,7 @@
         later = []
     else:
         sens_hbm, coords_hbm, keep_ref, send_ref, sens_next, coords_next, next_sem = rest
-        later = [
-            part_copies(part + 1, chunk, sens_hbm, coords_hbm, sens_next, coords_next, next_sem)
-            for chunk in range(CHUNKS)
-        ]
+        later = part_copies(part + 1, NEXT_CHUNKS, sens_hbm, coords_hbm, sens_next, coords_next, next_sem)
     for pair in later:
         for copy in pair:
             copy.start()
@@ -157,8 +165,7 @@
         row = count_rows[part * PART + p : part * PART + p + 1, :]
         return jnp.concatenate([row] * (PATCH_PTS // LANES), axis=1)
 
-    for chunk in range(CHUNKS):
-        chunk_tiles(chunk, counts, sens_buf, coords_buf, w, keep_ref, send_ref)
+    chunk_tiles(range(PART), counts, sens_buf, coords_buf, w, keep_ref, send_ref)
     for pair in later:
         for copy in pair:
             copy.wait()
@@ -172,7 +179,7 @@
 
 
 TILES = [jax.ShapeDtypeStruct((PART, ROWS, LANES), t) for t in (jnp.float32, jnp.bfloat16)]
-BUFFERS = ((CHUNKS, 3, NODE_Q, POINTS), jnp.bfloat16), ((CHUNKS, 3, POINTS), jnp.float32)
+BUFFERS = ((3, NODE_Q, PART * PATCH_PTS), jnp.bfloat16), ((3, PART * PATCH_PTS), jnp.float32)
 STREAM = [jax.ShapeDtypeStruct(*b) for b in BUFFERS]
 
 
@@ -186,8 +193,8 @@
         + STREAM,
         scratch_shapes=[pltpu.VMEM(*b) for b in BUFFERS]
         + [
-            pltpu.SemaphoreType.DMA((CHUNKS, 2)),
-            pltpu.SemaphoreType.DMA((CHUNKS, 2)),
+            pltpu.SemaphoreType.DMA((len(FIRST_CHUNKS), 2)),
+            pltpu.SemaphoreType.DMA((len(NEXT_CHUNKS), 2)),
             pltpu.SMEM(counts.shape, jnp.int32),
             pltpu.SMEM((NQW,), jnp.float32),
             pltpu.VMEM((1, 256), jnp.int32),
@@ -207,7 +214,7 @@
         in_specs=[VMEM] * 4 + ([] if last else [HBM] * 2),
         out_specs=[VMEM] * (2 if last else 4),
         out_shape=TILES + ([] if last else STREAM),
-        scratch_shapes=[] if last else [pltpu.SemaphoreType.DMA((CHUNKS, 2))],
+        scratch_shapes=[] if last else [pltpu.SemaphoreType.DMA((len(NEXT_CHUNKS), 2))],
         name="tiles_%d" % part,
         **kinds(),
     )(count_rows, w, *stream, *([] if last else [sens, coords]))
@@ -226,14 +233,15 @@
         yield keep, send, w
 
 
-def small_call(kernel, out_shape, in_specs, args, name, scratch=()):
+def small_call(kernel, out_shape, in_specs, args, name, aliases=None):
     many = isinstance(out_shape, list)
     return pl.pallas_call(
         kernel,
         in_specs=in_specs,
         out_specs=[VMEM] * len(out_shape) if many else VMEM,
         out_shape=out_shape,
-        scratch_shapes=list(scratch),
+        input_output_aliases=aliases or {},
+        cost_estimate=pl.CostEstimate(flops=1, bytes_accessed=1, transcendentals=0),
         compiler_params=pltpu.CompilerParams(vmem_limit_bytes=16 * MIB),
         name=name,
     )(*args)
@@ -265,19 +273,35 @@
             dense_ref[at] += tiles_ref[p].astype(jnp.float32)
 
 
-def own_kernel(cells_ref, *refs):
-    *parts, dense_ref = refs
+SLOTS = (48, ROWS, LANES)
+DENSE = jax.ShapeDtypeStruct(SLOTS, jnp.float32)
+
+
+def first_add_kernel(start, cells_ref, tiles_ref, dense_ref):
     dense_ref[...] = jnp.zeros_like(dense_ref)
-    for i, part in enumerate(parts):
-        add_mine(cells_ref, i * PART, dense_ref, part)
-
-
-def other_kernel(cells_ref, in_ref, *refs):
-    *parts, out_ref, dense_ref = refs
-    dense_ref[...] = in_ref[...]
-    for i, part in enumerate(parts):
-        add_mine(cells_ref, i * PART, dense_ref, part)
+    add_mine(cells_ref, start, dense_ref, tiles_ref)
+
+
+def add_kernel(start, cells_ref, tiles_ref, in_ref, dense_ref):
+    del in_ref
+    add_mine(cells_ref, start, dense_ref, tiles_ref)
+
+
+def last_add_kernel(start, cells_ref, tiles_ref, in_ref, dense_ref, out_ref):
+    add_kernel(start, cells_ref, tiles_ref, in_ref, dense_ref)
     out_ref[...] = dense_ref[...].astype(jnp.bfloat16)
+
+
+def add(cells, part, tiles, dense, last):
+    start = part * PART
+    if dense is None:
+        kernel = functools.partial(first_add_kernel, start)
+        return small_call(kernel, DENSE, [SMEM, VMEM], (cells, tiles), "first_add")
+    args, specs = (cells, tiles, dense), [SMEM, VMEM, VMEM]
+    if not last:
+        return small_call(functools.partial(add_kernel, start), DENSE, specs, args, "add", {2: 0})
+    out = [DENSE, jax.ShapeDtypeStruct(SLOTS, jnp.bfloat16)]
+    return small_call(functools.partial(last_add_kernel, start), out, specs, args, "last_add", {2: 0})[1]
 
 
 def owner_sum_kernel(in_ref, out_ref):
@@ -315,17 +339,15 @@
     for i, (keep, recv) in enumerate(held):
         keep, after = pair_sum(keep, recv, after)
         held[i] = keep, lax.ppermute(after, ("x", "core"), double(1))
+    cells, other_cells = smem(cells), smem(other_cells)
+    dense = None
     for i, (keep, recv) in enumerate(held):
-        full, after = pair_sum(keep, recv, after)
-        held[i] = full, lax.ppermute(after, "core", swap)
-    full, swapped = zip(*held)
-    slot = (48, ROWS, LANES)
-    specs = [VMEM] * len(full)
-    dense = jax.ShapeDtypeStruct(slot, jnp.float32)
-    dense = small_call(own_kernel, dense, [SMEM] + specs, (smem(cells), *full), "own")
-    slots = jax.ShapeDtypeStruct(slot, jnp.bfloat16)
-    args = (smem(other_cells), dense, *swapped)
-    slots = small_call(other_kernel, slots, [SMEM, VMEM] + specs, args, "other", [pltpu.VMEM(slot, jnp.float32)])
+        full, send = pair_sum(keep, recv, after)
+        held[i] = lax.ppermute(send, "core", swap)
+        after = dense = add(cells, i, full, dense, False)
+    for i, swapped in enumerate(held):
+        dense = add(other_cells, i, swapped, dense, i == len(held) - 1)
+    slots = dense
     slots = lax.all_to_all(slots, ("z", "y"), 0, 0, tiled=True)
     out = jax.ShapeDtypeStruct((192, 3 * K), jnp.float32)
     return small_call(owner_sum_kernel, out, [VMEM], (slots,), "owner_sum").T

time: 50 us -> 49.5 us (0.990)
  waiting for transfers between devices: 10.7 us -> 9.78 us
  Pallas kernels: 10.7 us -> 11.2 us
    pallas_call x7 -> x9, Pallas kernels: 3.21 us -> 4.23 us  [small_call(): pl.pallas_call(kernel, in_specs=in_specs, out_specs=[VMEM] * len(out_shap...]
    ppermute x2, waiting for transfers between devices: 6.05 us -> 5.12 us  [local(): held[i] = (keep, lax.ppermute(after, ('x', 'core'), double(1)))]
  transfers between devices with their start and end apart: 7 -> 7, of which waited for: 5 -> 5; matrix products, arithmetic and copies ran while one was open for 0% -> 0% of each run, Pallas kernels for 8% -> 11%
where the time goes in v4:
time: 49.5 us; the launch traced here: 49.3 us
  blocking collectives  21.2 us (43%)
  Pallas kernels  11.2 us (23%)
  waiting for transfers between devices  9.78 us (20%)
  starting transfers between devices  6.96 us (14%)
    all_to_all x1, blocking collectives, local(): slots = lax.all_to_all(slots, ('z', 'y'), 0, 0, tiled=True)  21.2 us
    ppermute x2, waiting for transfers between devices, local(): held[i] = (keep, lax.ppermute(after, ('x', 'core'), double(1)))  5.12 us
    ppermute x2, waiting for transfers between devices, local(): held.append((keep, lax.ppermute(send, ('x', 'core'), double(0))))  4.43 us
    pallas_call x1, Pallas kernels, first_part(): pl.pallas_call(first_kernel, in_specs=[HBM] * 6, out_specs=[VMEM] * 6, ou...  4.37 us
    pallas_call x9, Pallas kernels, small_call(): pl.pallas_call(kernel, in_specs=in_specs, out_specs=[VMEM] * len(out_shap...  4.23 us
    ppermute x2, starting transfers between devices, local(): held[i] = (keep, lax.ppermute(after, ('x', 'core'), double(1)))  4.12 us
    pallas_call x1, Pallas kernels, later_part(): pl.pallas_call(functools.partial(later_kernel, part, last), in_specs=[VME...  2.65 us
    ppermute x2, starting transfers between devices, local(): held.append((keep, lax.ppermute(send, ('x', 'core'), double(0))))  2.18 us
  transfers between devices with their start and end apart: 7, of which 5 were waited for; matrix products, arithmetic and copies ran while one was open for 0% of the time, Pallas kernels for 11%

profile of v4, /device:TPU:0, one launch (start us, length us, event | category | flops | bytes accessed | tf_op | source)
XLA Modules:
  0.0 49.3 jit_solution(7993528442448730728)
XLA Ops:
  0.0 4.4 %tiles_0.1 = (f32[16,56,128]{2,1,0:T(8,128)S(1)}, bf16[16,56,128]{2,1,0:T(8,128)(2,1)S(1)}, bf16[112,192]{1,0:T(8,128)(2,1)S(1)}, s32[32,128]{1,0:T(8,128)S(1)},...) custom-call(s32[32]{0:T(128)} %counts_hbm.1, f32[16]{0:T(128)} %table_hbm.1, s32[1,256]{1,0:T(1,128)} %bitcast.4, ...), custom_call_target="tpu_custom_call" | custom-call | flops 8000000000 | bytes 4000000 | tf_op jit(solution)/shard_map/tiles_0/pallas_call | solution.py:187
  4.4 1.7 %collective-permute-start.2 = (bf16[16,56,128]{2,1,0:T(8,128)(2,1)S(1)}, bf16[16,56,128]{2,1,0:T(8,128)(2,1)S(1)}, u32[]{:S(2)}, u32[]{:S(2)}) collective-permute-start(bf16[16,56,128]{2,1,0:T(8,128)(2,1)S(1)} %get-tuple-element.29), channel_id=1, source_target_pairs={{0,32},{1,97},{32,0},{33,65},{64,96},{65,33},{96,64},{97,1},{2,34}... | collective-permute-start | bytes 688136 | tf_op jit(solution)/shard_map/ppermute | solution.py:337
  6.0 2.6 %tiles_1.1 = (f32[16,56,128]{2,1,0:T(8,128)S(1)}, bf16[16,56,128]{2,1,0:T(8,128)(2,1)S(1)}) custom-call(s32[32,128]{1,0:T(8,128)S(1)} %get-tuple-element.22.count_rows, bf16[112,192]{1,0:T(8,128)(2,1)S(1)} %get-tuple-element.23.w_ref.after_ref, bf16[3,64,8192]{2,1,0:T(8,128)(2,1)S(1)} %get-tuple-element.24.sens_buf, f32[3,8192]{1,0:T(4,128)S(1)} %get-tuple-element.25.coords_buf), custom_call_target="tpu_custom_call" | custom-call | flops 8000000000 | bytes 4000000 | tf_op jit(solution)/shard_map/tiles_1/pallas_call | solution.py:212
  8.7 0.0 copy-start
  8.7 0.5 %collective-permute-start.1 = (bf16[16,56,128]{2,1,0:T(8,128)(2,1)S(1)}, bf16[16,56,128]{2,1,0:T(8,128)(2,1)S(1)}, u32[]{:S(2)}, u32[]{:S(2)}) collective-permute-start(bf16[16,56,128]{2,1,0:T(8,128)(2,1)S(1)} %get-tuple-element.27), channel_id=1, source_target_pairs={{0,32},{1,97},{32,0},{33,65},{64,96},{65,33},{96,64},{97,1},{2,34}... | collective-permute-start | bytes 688136 | tf_op jit(solution)/shard_map/ppermute | solution.py:337
  9.2 1.3 %collective-permute-done.2.recv_ref = bf16[16,56,128]{2,1,0:T(8,128)(2,1)S(1)} collective-permute-done((bf16[16,56,128]{2,1,0:T(8,128)(2,1)S(1)}, bf16[16,56,128]{2,1,0:T(8,128)(2,1)S(1)}, u32[]{:S(2)}, u32[]{:S(2)}) %collective-permute-start.2) | collective-permute-done | bytes 229408 | tf_op jit(solution)/shard_map/ppermute | solution.py:337
  10.5 0.1 pair_sum.4
  10.5 2.9 %collective-permute-start.4 = (bf16[16,56,128]{2,1,0:T(8,128)(2,1)S(1)}, bf16[16,56,128]{2,1,0:T(8,128)(2,1)S(1)}, u32[]{:S(2)}, u32[]{:S(2)}) collective-permute-start(bf16[16,56,128]{2,1,0:T(8,128)(2,1)S(1)} %get-tuple-element.30.after_ref), channel_id=1, source_target_pairs={{0,96},{1,33},{32,64},{33,1},{64,32},{65,97},{96,0},{97,65},{2,98}... | collective-permute-start | bytes 688136 | tf_op jit(solution)/shard_map/ppermute | solution.py:341
  13.5 3.2 %collective-permute-done.1.recv_ref = bf16[16,56,128]{2,1,0:T(8,128)(2,1)S(1)} collective-permute-done((bf16[16,56,128]{2,1,0:T(8,128)(2,1)S(1)}, bf16[16,56,128]{2,1,0:T(8,128)(2,1)S(1)}, u32[]{:S(2)}, u32[]{:S(2)}) %collective-permute-start.1) | collective-permute-done | bytes 229408 | tf_op jit(solution)/shard_map/ppermute | solution.py:337
  16.6 0.1 pair_sum.5
  16.7 1.2 %collective-permute-start.3 = (bf16[16,56,128]{2,1,0:T(8,128)(2,1)S(1)}, bf16[16,56,128]{2,1,0:T(8,128)(2,1)S(1)}, u32[]{:S(2)}, u32[]{:S(2)}) collective-permute-start(bf16[16,56,128]{2,1,0:T(8,128)(2,1)S(1)} %get-tuple-element.32.after_ref), channel_id=1, source_target_pairs={{0,96},{1,33},{32,64},{33,1},{64,32},{65,97},{96,0},{97,65},{2,98}... | collective-permute-start | bytes 688136 | tf_op jit(solution)/shard_map/ppermute | solution.py:341
  17.9 0.4 collective-permute-done.4.recv_ref
  18.3 0.1 pair_sum.6
  18.4 0.1 collective-permute-start.6
  18.5 0.0 copy-done
  18.5 0.8 %first_add.1.after_ref.in_ref = f32[48,56,128]{2,1,0:T(8,128)S(1)} custom-call(s32[32]{0:T(128)S(1)} %copy-done, f32[16,56,128]{2,1,0:T(8,128)S(1)} %get-tuple-element.34.tiles_ref), custom_call_target="tpu_custom_call" | custom-call | flops 1 | bytes 1 | tf_op jit(solution)/shard_map/first_add/pallas_call | solution.py:238
  19.3 4.7 %collective-permute-done.3.recv_ref = bf16[16,56,128]{2,1,0:T(8,128)(2,1)S(1)} collective-permute-done((bf16[16,56,128]{2,1,0:T(8,128)(2,1)S(1)}, bf16[16,56,128]{2,1,0:T(8,128)(2,1)S(1)}, u32[]{:S(2)}, u32[]{:S(2)}) %collective-permute-start.3) | collective-permute-done | bytes 229408 | tf_op jit(solution)/shard_map/ppermute | solution.py:341
  24.0 0.1 pair_sum.7
  24.1 0.1 collective-permute-start.5
  24.2 0.5 %collective-permute-start = (s32[32]{0:T(128)S(1)}, s32[32]{0:T(128)S(1)}, u32[]{:S(2)}, u32[]{:S(2)}) collective-permute-start(s32[32]{0:T(128)S(1)} %copy-done), channel_id=1, source_target_pairs={{0,1},{1,0},{2,3},{3,2},{4,5},{5,4},{6,7},{7,6},{8,9},{9,8},{10,11... | collective-permute-start | bytes 392 | tf_op jit(solution)/shard_map/ppermute | solution.py:334
  24.7 0.7 %add.2.in_ref = f32[48,56,128]{2,1,0:T(8,128)S(1)} custom-call(s32[32]{0:T(128)S(1)} %copy-done, f32[16,56,128]{2,1,0:T(8,128)S(1)} %get-tuple-element.37.tiles_ref, f32[48,56,128]{2,1,0:T(8,128)S(1)} %first_add.1.after_ref.in_ref), custom_call_target="tpu_custom_call", output_to_operand_aliasing={{}: (2, {})} | custom-call | flops 1 | bytes 1 | tf_op jit(solution)/shard_map/add/pallas_call | solution.py:238
  25.4 0.2 collective-permute-done.cells_ref
  25.7 0.0 collective-permute-done.6.tiles_ref
  25.7 0.7 %add.3.in_ref = f32[48,56,128]{2,1,0:T(8,128)S(1)} custom-call(s32[32]{0:T(128)S(1)} %collective-permute-done.cells_ref, bf16[16,56,128]{2,1,0:T(8,128)(2,1)S(1)} %collective-permute-done.6.tiles_ref, f32[48,56,128]{2,1,0:T(8,128)S(1)} %add.2.in_ref), custom_call_target="tpu_custom_call", output_to_operand_aliasing={{}: (2, {})} | custom-call | flops 1 | bytes 1 | tf_op jit(solution)/shard_map/add/pallas_call | solution.py:238
  26.4 0.0 collective-permute-done.5.tiles_ref
  26.4 0.8 %last_add.1 = (f32[48,56,128]{2,1,0:T(8,128)S(1)}, bf16[48,56,128]{2,1,0:T(8,128)(2,1)S(1)}) custom-call(s32[32]{0:T(128)S(1)} %collective-permute-done.cells_ref, bf16[16,56,128]{2,1,0:T(8,128)(2,1)S(1)} %collective-permute-done.5.tiles_ref, f32[48,56,128]{2,1,0:T(8,128)S(1)} %add.3.in_ref), custom_call_target="tpu_custom_call", output_to_operand_aliasing={{0}: (2, {})} | custom-call | flops 1 | bytes 1 | tf_op jit(solution)/shard_map/last_add/pallas_call | solution.py:238
  27.2 21.2 %all_to_all.5.in_ref = bf16[48,56,128]{2,1,0:T(8,128)(2,1)S(1)} all-to-all(bf16[48,56,128]{2,1,0:T(8,128)(2,1)S(1)} %get-tuple-element.38), channel_id=1, replica_groups=mesh['x'=4,'z'=4,'y'=4,'core'=2] {'z','y'}, dimensions={0} | all-to-all | bytes 1376256 | tf_op jit(solution)/shard_map/all_to_all | solution.py:351
  48.5 0.9 %owner_sum.1 = f32[192,105]{1,0:T(8,128)} custom-call(bf16[48,56,128]{2,1,0:T(8,128)(2,1)S(1)} %all_to_all.5.in_ref), custom_call_target="tpu_custom_call" | custom-call | flops 1 | bytes 1 | tf_op jit(solution)/shard_map/owner_sum/pallas_call | solution.py:238
Async XLA Ops:
  4.4 6.1 %collective-permute-start.2 = (bf16[16,56,128]{2,1,0:T(8,128)(2,1)S(1)}, bf16[16,56,128]{2,1,0:T(8,128)(2,1)S(1)}, u32[]{:S(2)}, u32[]{:S(2)}) collective-permute-start(bf16[16,56,128]{2,1,0:T(8,128)(2,1)S(1)} %get-tuple-element.29), channel_id=1, source_target_pairs={{0,32},{1,97},{32,0},{33,65},{64,96},{65,33},{96,64},{97,1},{2,34}... | collective-permute-start | bytes 688136 | tf_op jit(solution)/shard_map/ppermute | solution.py:337
  8.7 9.8 %copy-start = (s32[32]{0:T(128)S(1)}, s32[32]{0:T(128)}, u32[]{:S(2)}) copy-start(s32[32]{0:T(128)} %cells_ref.3) | copy-start | bytes 388
  8.7 7.9 %collective-permute-start.1 = (bf16[16,56,128]{2,1,0:T(8,128)(2,1)S(1)}, bf16[16,56,128]{2,1,0:T(8,128)(2,1)S(1)}, u32[]{:S(2)}, u32[]{:S(2)}) collective-permute-start(bf16[16,56,128]{2,1,0:T(8,128)(2,1)S(1)} %get-tuple-element.27), channel_id=1, source_target_pairs={{0,32},{1,97},{32,0},{33,65},{64,96},{65,33},{96,64},{97,1},{2,34}... | collective-permute-start | bytes 688136 | tf_op jit(solution)/shard_map/ppermute | solution.py:337
  10.5 7.8 %collective-permute-start.4 = (bf16[16,56,128]{2,1,0:T(8,128)(2,1)S(1)}, bf16[16,56,128]{2,1,0:T(8,128)(2,1)S(1)}, u32[]{:S(2)}, u32[]{:S(2)}) collective-permute-start(bf16[16,56,128]{2,1,0:T(8,128)(2,1)S(1)} %get-tuple-element.30.after_ref), channel_id=1, source_target_pairs={{0,96},{1,33},{32,64},{33,1},{64,32},{65,97},{96,0},{97,65},{2,98}... | collective-permute-start | bytes 688136 | tf_op jit(solution)/shard_map/ppermute | solution.py:341
  16.7 7.3 %collective-permute-start.3 = (bf16[16,56,128]{2,1,0:T(8,128)(2,1)S(1)}, bf16[16,56,128]{2,1,0:T(8,128)(2,1)S(1)}, u32[]{:S(2)}, u32[]{:S(2)}) collective-permute-start(bf16[16,56,128]{2,1,0:T(8,128)(2,1)S(1)} %get-tuple-element.32.after_ref), channel_id=1, source_target_pairs={{0,96},{1,33},{32,64},{33,1},{64,32},{65,97},{96,0},{97,65},{2,98}... | collective-permute-start | bytes 688136 | tf_op jit(solution)/shard_map/ppermute | solution.py:341
  18.4 7.3 %collective-permute-start.6 = (bf16[16,56,128]{2,1,0:T(8,128)(2,1)S(1)}, bf16[16,56,128]{2,1,0:T(8,128)(2,1)S(1)}, u32[]{:S(2)}, u32[]{:S(2)}) collective-permute-start(bf16[16,56,128]{2,1,0:T(8,128)(2,1)S(1)} %get-tuple-element.36), channel_id=1, source_target_pairs={{0,1},{1,0},{2,3},{3,2},{4,5},{5,4},{6,7},{7,6},{8,9},{9,8},{10,11... | collective-permute-start | bytes 688136 | tf_op jit(solution)/shard_map/ppermute | solution.py:346
  24.1 2.3 %collective-permute-start.5 = (bf16[16,56,128]{2,1,0:T(8,128)(2,1)S(1)}, bf16[16,56,128]{2,1,0:T(8,128)(2,1)S(1)}, u32[]{:S(2)}, u32[]{:S(2)}) collective-permute-start(bf16[16,56,128]{2,1,0:T(8,128)(2,1)S(1)} %get-tuple-element.35), channel_id=1, source_target_pairs={{0,1},{1,0},{2,3},{3,2},{4,5},{5,4},{6,7},{7,6},{8,9},{9,8},{10,11... | collective-permute-start | bytes 688136 | tf_op jit(solution)/shard_map/ppermute | solution.py:346
  24.2 1.5 %collective-permute-start = (s32[32]{0:T(128)S(1)}, s32[32]{0:T(128)S(1)}, u32[]{:S(2)}, u32[]{:S(2)}) collective-permute-start(s32[32]{0:T(128)S(1)} %copy-done), channel_id=1, source_target_pairs={{0,1},{1,0},{2,3},{3,2},{4,5},{5,4},{6,7},{7,6},{8,9},{9,8},{10,11... | collective-permute-start | bytes 392 | tf_op jit(solution)/shard_map/ppermute | solution.py:334

commit v5 on v4

--- a/solution.py
+++ b/solution.py
@@ -277,31 +277,25 @@
 DENSE = jax.ShapeDtypeStruct(SLOTS, jnp.float32)
 
 
-def first_add_kernel(start, cells_ref, tiles_ref, dense_ref):
-    dense_ref[...] = jnp.zeros_like(dense_ref)
-    add_mine(cells_ref, start, dense_ref, tiles_ref)
-
-
-def add_kernel(start, cells_ref, tiles_ref, in_ref, dense_ref):
-    del in_ref
-    add_mine(cells_ref, start, dense_ref, tiles_ref)
-
-
-def last_add_kernel(start, cells_ref, tiles_ref, in_ref, dense_ref, out_ref):
-    add_kernel(start, cells_ref, tiles_ref, in_ref, dense_ref)
-    out_ref[...] = dense_ref[...].astype(jnp.bfloat16)
-
-
-def add(cells, part, tiles, dense, last):
-    start = part * PART
-    if dense is None:
-        kernel = functools.partial(first_add_kernel, start)
-        return small_call(kernel, DENSE, [SMEM, VMEM], (cells, tiles), "first_add")
-    args, specs = (cells, tiles, dense), [SMEM, VMEM, VMEM]
-    if not last:
-        return small_call(functools.partial(add_kernel, start), DENSE, specs, args, "add", {2: 0})
-    out = [DENSE, jax.ShapeDtypeStruct(SLOTS, jnp.bfloat16)]
-    return small_call(functools.partial(last_add_kernel, start), out, specs, args, "last_add", {2: 0})[1]
+def add_kernel(plan, zero, last, *refs):
+    cells, refs = refs[:2], refs[2:]
+    tiles, refs = refs[: len(plan)], refs[len(plan) :]
+    dense_ref = refs[0] if zero else refs[1]
+    if zero:
+        dense_ref[...] = jnp.zeros_like(dense_ref)
+    for (which, part), ref in zip(plan, tiles):
+        add_mine(cells[which], part * PART, dense_ref, ref)
+    if last:
+        refs[-1][...] = dense_ref[...].astype(jnp.bfloat16)
+
+
+def add(cells, plan, tiles, dense=None, last=False):
+    zero = dense is None
+    args = [*cells, *tiles] + ([] if zero else [dense])
+    specs = [SMEM] * 2 + [VMEM] * (len(args) - 2)
+    out = [DENSE] + ([jax.ShapeDtypeStruct(SLOTS, jnp.bfloat16)] if last else [])
+    aliases = {} if zero else {len(args) - 1: 0}
+    return small_call(functools.partial(add_kernel, plan, zero, last), out, specs, args, "add", aliases)[-1]
 
 
 def owner_sum_kernel(in_ref, out_ref):
@@ -339,15 +333,18 @@
     for i, (keep, recv) in enumerate(held):
         keep, after = pair_sum(keep, recv, after)
         held[i] = keep, lax.ppermute(after, ("x", "core"), double(1))
-    cells, other_cells = smem(cells), smem(other_cells)
-    dense = None
+    both = smem(cells), smem(other_cells)
+    count = len(held)
+    full, swapped = [], []
     for i, (keep, recv) in enumerate(held):
-        full, send = pair_sum(keep, recv, after)
-        held[i] = lax.ppermute(send, "core", swap)
-        after = dense = add(cells, i, full, dense, False)
-    for i, swapped in enumerate(held):
-        dense = add(other_cells, i, swapped, dense, i == len(held) - 1)
-    slots = dense
+        if i == count - 1:
+            after = dense = add(both, [(0, j) for j in range(i)], full)
+        tiles, after = pair_sum(keep, recv, after)
+        full.append(tiles)
+        swapped.append(lax.ppermute(after, "core", swap))
+    plan = [(0, count - 1)] + [(1, j) for j in range(count - 1)]
+    dense = add(both, plan, [full[-1]] + swapped[:-1], dense)
+    slots = add(both, [(1, count - 1)], swapped[-1:], dense, True)
     slots = lax.all_to_all(slots, ("z", "y"), 0, 0, tiled=True)
     out = jax.ShapeDtypeStruct((192, 3 * K), jnp.float32)
     return small_call(owner_sum_kernel, out, [VMEM], (slots,), "owner_sum").T

time: 49.5 us -> 48.7 us (0.984)
  Pallas kernels: 11.2 us -> 10.7 us
    pallas_call x9 -> x8, Pallas kernels: 4.23 us -> 3.68 us  [small_call(): pl.pallas_call(kernel, in_specs=in_specs, out_specs=[VMEM] * len(out_shap...]
    ppermute x2, waiting for transfers between devices: 5.12 us -> 4.57 us  [local(): held[i] = (keep, lax.ppermute(after, ('x', 'core'), double(1)))]
    ppermute x2, waiting for transfers between devices: 0.01 us -> 0.52 us  [local(): swapped.append(lax.ppermute(after, 'core', swap))]
  transfers between devices with their start and end apart: 7 -> 7, of which waited for: 5 -> 6; matrix products, arithmetic and copies ran while one was open for 0% -> 0% of each run, Pallas kernels for 11% -> 10%
where the time goes in v5:
time: 48.7 us; the launch traced here: 48.5 us
  blocking collectives  21.2 us (44%)
  Pallas kernels  10.7 us (22%)
  waiting for transfers between devices  9.98 us (20%)
  starting transfers between devices  6.58 us (14%)
    all_to_all x1, blocking collectives, local(): slots = lax.all_to_all(slots, ('z', 'y'), 0, 0, tiled=True)  21.2 us
    ppermute x2, waiting for transfers between devices, local(): held[i] = (keep, lax.ppermute(after, ('x', 'core'), double(1)))  4.57 us
    ppermute x2, waiting for transfers between devices, local(): held.append((keep, lax.ppermute(send, ('x', 'core'), double(0))))  4.43 us
    pallas_call x1, Pallas kernels, first_part(): pl.pallas_call(first_kernel, in_specs=[HBM] * 6, out_specs=[VMEM] * 6, ou...  4.37 us
    ppermute x2, starting transfers between devices, local(): held[i] = (keep, lax.ppermute(after, ('x', 'core'), double(1)))  4.12 us
    pallas_call x8, Pallas kernels, small_call(): pl.pallas_call(kernel, in_specs=in_specs, out_specs=[VMEM] * len(out_shap...  3.68 us
    pallas_call x1, Pallas kernels, later_part(): pl.pallas_call(functools.partial(later_kernel, part, last), in_specs=[VME...  2.65 us
    ppermute x2, starting transfers between devices, local(): held.append((keep, lax.ppermute(send, ('x', 'core'), double(0))))  2.18 us
  transfers between devices with their start and end apart: 7, of which 6 were waited for; matrix products, arithmetic and copies ran while one was open for 0% of the time, Pallas kernels for 10%

profile of v5, /device:TPU:0, one launch (start us, length us, event | category | flops | bytes accessed | tf_op | source)
XLA Modules:
  0.0 48.5 jit_solution(4124196434159821542)
XLA Ops:
  0.0 4.4 %tiles_0.1 = (f32[16,56,128]{2,1,0:T(8,128)S(1)}, bf16[16,56,128]{2,1,0:T(8,128)(2,1)S(1)}, bf16[112,192]{1,0:T(8,128)(2,1)S(1)}, s32[32,128]{1,0:T(8,128)S(1)},...) custom-call(s32[32]{0:T(128)} %counts_hbm.1, f32[16]{0:T(128)} %table_hbm.1, s32[1,256]{1,0:T(1,128)} %bitcast.4, ...), custom_call_target="tpu_custom_call" | custom-call | flops 8000000000 | bytes 4000000 | tf_op jit(solution)/shard_map/tiles_0/pallas_call | solution.py:187
  4.4 1.7 %collective-permute-start.2 = (bf16[16,56,128]{2,1,0:T(8,128)(2,1)S(1)}, bf16[16,56,128]{2,1,0:T(8,128)(2,1)S(1)}, u32[]{:S(2)}, u32[]{:S(2)}) collective-permute-start(bf16[16,56,128]{2,1,0:T(8,128)(2,1)S(1)} %get-tuple-element.29), channel_id=1, source_target_pairs={{0,32},{1,97},{32,0},{33,65},{64,96},{65,33},{96,64},{97,1},{2,34}... | collective-permute-start | bytes 688136 | tf_op jit(solution)/shard_map/ppermute | solution.py:331
  6.0 2.6 %tiles_1.1 = (f32[16,56,128]{2,1,0:T(8,128)S(1)}, bf16[16,56,128]{2,1,0:T(8,128)(2,1)S(1)}) custom-call(s32[32,128]{1,0:T(8,128)S(1)} %get-tuple-element.22.count_rows, bf16[112,192]{1,0:T(8,128)(2,1)S(1)} %get-tuple-element.23.w_ref.after_ref, bf16[3,64,8192]{2,1,0:T(8,128)(2,1)S(1)} %get-tuple-element.24.sens_buf, f32[3,8192]{1,0:T(4,128)S(1)} %get-tuple-element.25.coords_buf), custom_call_target="tpu_custom_call" | custom-call | flops 8000000000 | bytes 4000000 | tf_op jit(solution)/shard_map/tiles_1/pallas_call | solution.py:212
  8.7 0.0 copy-start
  8.7 0.5 %collective-permute-start.1 = (bf16[16,56,128]{2,1,0:T(8,128)(2,1)S(1)}, bf16[16,56,128]{2,1,0:T(8,128)(2,1)S(1)}, u32[]{:S(2)}, u32[]{:S(2)}) collective-permute-start(bf16[16,56,128]{2,1,0:T(8,128)(2,1)S(1)} %get-tuple-element.27), channel_id=1, source_target_pairs={{0,32},{1,97},{32,0},{33,65},{64,96},{65,33},{96,64},{97,1},{2,34}... | collective-permute-start | bytes 688136 | tf_op jit(solution)/shard_map/ppermute | solution.py:331
  9.2 1.3 %collective-permute-done.2.recv_ref = bf16[16,56,128]{2,1,0:T(8,128)(2,1)S(1)} collective-permute-done((bf16[16,56,128]{2,1,0:T(8,128)(2,1)S(1)}, bf16[16,56,128]{2,1,0:T(8,128)(2,1)S(1)}, u32[]{:S(2)}, u32[]{:S(2)}) %collective-permute-start.2) | collective-permute-done | bytes 229408 | tf_op jit(solution)/shard_map/ppermute | solution.py:331
  10.5 0.1 pair_sum.4
  10.5 2.9 %collective-permute-start.4 = (bf16[16,56,128]{2,1,0:T(8,128)(2,1)S(1)}, bf16[16,56,128]{2,1,0:T(8,128)(2,1)S(1)}, u32[]{:S(2)}, u32[]{:S(2)}) collective-permute-start(bf16[16,56,128]{2,1,0:T(8,128)(2,1)S(1)} %get-tuple-element.30.after_ref), channel_id=1, source_target_pairs={{0,96},{1,33},{32,64},{33,1},{64,32},{65,97},{96,0},{97,65},{2,98}... | collective-permute-start | bytes 688136 | tf_op jit(solution)/shard_map/ppermute | solution.py:335
  13.5 3.2 %collective-permute-done.1.recv_ref = bf16[16,56,128]{2,1,0:T(8,128)(2,1)S(1)} collective-permute-done((bf16[16,56,128]{2,1,0:T(8,128)(2,1)S(1)}, bf16[16,56,128]{2,1,0:T(8,128)(2,1)S(1)}, u32[]{:S(2)}, u32[]{:S(2)}) %collective-permute-start.1) | collective-permute-done | bytes 229408 | tf_op jit(solution)/shard_map/ppermute | solution.py:331
  16.6 0.1 pair_sum.5
  16.7 1.2 %collective-permute-start.3 = (bf16[16,56,128]{2,1,0:T(8,128)(2,1)S(1)}, bf16[16,56,128]{2,1,0:T(8,128)(2,1)S(1)}, u32[]{:S(2)}, u32[]{:S(2)}) collective-permute-start(bf16[16,56,128]{2,1,0:T(8,128)(2,1)S(1)} %get-tuple-element.32.after_ref), channel_id=1, source_target_pairs={{0,96},{1,33},{32,64},{33,1},{64,32},{65,97},{96,0},{97,65},{2,98}... | collective-permute-start | bytes 688136 | tf_op jit(solution)/shard_map/ppermute | solution.py:335
  17.9 0.0 copy-done
  17.9 0.0 collective-permute-start
  17.9 0.4 collective-permute-done.4.recv_ref
  18.3 0.1 pair_sum.6
  18.4 0.2 collective-permute-start.6
  18.6 0.5 collective-permute-done.refs_1_
  19.0 0.8 %add.3.after_ref.refs_4_ = f32[48,56,128]{2,1,0:T(8,128)S(1)} custom-call(s32[32]{0:T(128)S(1)} %copy-done, s32[32]{0:T(128)S(1)} %collective-permute-done.refs_1_, f32[16,56,128]{2,1,0:T(8,128)S(1)} %get-tuple-element.34.refs_2_), custom_call_target="tpu_custom_call" | custom-call | flops 1 | bytes 1 | tf_op jit(solution)/shard_map/add/pallas_call | solution.py:238
  19.9 4.2 %collective-permute-done.3.recv_ref = bf16[16,56,128]{2,1,0:T(8,128)(2,1)S(1)} collective-permute-done((bf16[16,56,128]{2,1,0:T(8,128)(2,1)S(1)}, bf16[16,56,128]{2,1,0:T(8,128)(2,1)S(1)}, u32[]{:S(2)}, u32[]{:S(2)}) %collective-permute-start.3) | collective-permute-done | bytes 229408 | tf_op jit(solution)/shard_map/ppermute | solution.py:335
  24.0 0.1 pair_sum.7
  24.1 0.1 collective-permute-start.5
  24.2 0.0 collective-permute-done.6.refs_3_
  24.2 0.9 %add.4.refs_3_ = f32[48,56,128]{2,1,0:T(8,128)S(1)} custom-call(s32[32]{0:T(128)S(1)} %copy-done, s32[32]{0:T(128)S(1)} %collective-permute-done.refs_1_, f32[16,56,128]{2,1,0:T(8,128)S(1)} %get-tuple-element.36.refs_2_, bf16[16,56,128]{2,1,0:T(8,128)(2,1)S(1)} %collective-permute-done.6.refs_3_, ...), custom_call_target="tpu_custom_call", output_to_operand_aliasing={{}: (4, {})} | custom-call | flops 1 | bytes 1 | tf_op jit(solution)/shard_map/add/pallas_call | solution.py:238
  25.1 0.5 %collective-permute-done.5.refs_2_ = bf16[16,56,128]{2,1,0:T(8,128)(2,1)S(1)} collective-permute-done((bf16[16,56,128]{2,1,0:T(8,128)(2,1)S(1)}, bf16[16,56,128]{2,1,0:T(8,128)(2,1)S(1)}, u32[]{:S(2)}, u32[]{:S(2)}) %collective-permute-start.5) | collective-permute-done | bytes 229408 | tf_op jit(solution)/shard_map/ppermute | solution.py:344
  25.7 0.8 %add.5 = (f32[48,56,128]{2,1,0:T(8,128)S(1)}, bf16[48,56,128]{2,1,0:T(8,128)(2,1)S(1)}) custom-call(s32[32]{0:T(128)S(1)} %copy-done, s32[32]{0:T(128)S(1)} %collective-permute-done.refs_1_, bf16[16,56,128]{2,1,0:T(8,128)(2,1)S(1)} %collective-permute-done.5.refs_2_, f32[48,56,128]{2,1,0:T(8,128)S(1)} %add.4.refs_3_), custom_call_target="tpu_custom_call", output_to_operand_aliasing={{0}: (3, {})} | custom-call | flops 1 | bytes 1 | tf_op jit(solution)/shard_map/add/pallas_call | solution.py:238
  26.5 21.2 %all_to_all.5.in_ref = bf16[48,56,128]{2,1,0:T(8,128)(2,1)S(1)} all-to-all(bf16[48,56,128]{2,1,0:T(8,128)(2,1)S(1)} %get-tuple-element.38), channel_id=1, replica_groups=mesh['x'=4,'z'=4,'y'=4,'core'=2] {'z','y'}, dimensions={0} | all-to-all | bytes 1376256 | tf_op jit(solution)/shard_map/all_to_all | solution.py:348
  47.7 0.9 %owner_sum.1 = f32[192,105]{1,0:T(8,128)} custom-call(bf16[48,56,128]{2,1,0:T(8,128)(2,1)S(1)} %all_to_all.5.in_ref), custom_call_target="tpu_custom_call" | custom-call | flops 1 | bytes 1 | tf_op jit(solution)/shard_map/owner_sum/pallas_call | solution.py:238
Async XLA Ops:
  4.4 6.1 %collective-permute-start.2 = (bf16[16,56,128]{2,1,0:T(8,128)(2,1)S(1)}, bf16[16,56,128]{2,1,0:T(8,128)(2,1)S(1)}, u32[]{:S(2)}, u32[]{:S(2)}) collective-permute-start(bf16[16,56,128]{2,1,0:T(8,128)(2,1)S(1)} %get-tuple-element.29), channel_id=1, source_target_pairs={{0,32},{1,97},{32,0},{33,65},{64,96},{65,33},{96,64},{97,1},{2,34}... | collective-permute-start | bytes 688136 | tf_op jit(solution)/shard_map/ppermute | solution.py:331
  8.7 9.2 %copy-start = (s32[32]{0:T(128)S(1)}, s32[32]{0:T(128)}, u32[]{:S(2)}) copy-start(s32[32]{0:T(128)} %refs_0_.5) | copy-start | bytes 388
  8.7 7.9 %collective-permute-start.1 = (bf16[16,56,128]{2,1,0:T(8,128)(2,1)S(1)}, bf16[16,56,128]{2,1,0:T(8,128)(2,1)S(1)}, u32[]{:S(2)}, u32[]{:S(2)}) collective-permute-start(bf16[16,56,128]{2,1,0:T(8,128)(2,1)S(1)} %get-tuple-element.27), channel_id=1, source_target_pairs={{0,32},{1,97},{32,0},{33,65},{64,96},{65,33},{96,64},{97,1},{2,34}... | collective-permute-start | bytes 688136 | tf_op jit(solution)/shard_map/ppermute | solution.py:331
  10.5 7.8 %collective-permute-start.4 = (bf16[16,56,128]{2,1,0:T(8,128)(2,1)S(1)}, bf16[16,56,128]{2,1,0:T(8,128)(2,1)S(1)}, u32[]{:S(2)}, u32[]{:S(2)}) collective-permute-start(bf16[16,56,128]{2,1,0:T(8,128)(2,1)S(1)} %get-tuple-element.30.after_ref), channel_id=1, source_target_pairs={{0,96},{1,33},{32,64},{33,1},{64,32},{65,97},{96,0},{97,65},{2,98}... | collective-permute-start | bytes 688136 | tf_op jit(solution)/shard_map/ppermute | solution.py:335
  16.7 7.3 %collective-permute-start.3 = (bf16[16,56,128]{2,1,0:T(8,128)(2,1)S(1)}, bf16[16,56,128]{2,1,0:T(8,128)(2,1)S(1)}, u32[]{:S(2)}, u32[]{:S(2)}) collective-permute-start(bf16[16,56,128]{2,1,0:T(8,128)(2,1)S(1)} %get-tuple-element.32.after_ref), channel_id=1, source_target_pairs={{0,96},{1,33},{32,64},{33,1},{64,32},{65,97},{96,0},{97,65},{2,98}... | collective-permute-start | bytes 688136 | tf_op jit(solution)/shard_map/ppermute | solution.py:335
  17.9 1.1 %collective-permute-start = (s32[32]{0:T(128)S(1)}, s32[32]{0:T(128)S(1)}, u32[]{:S(2)}, u32[]{:S(2)}) collective-permute-start(s32[32]{0:T(128)S(1)} %copy-done), channel_id=1, source_target_pairs={{0,1},{1,0},{2,3},{3,2},{4,5},{5,4},{6,7},{7,6},{8,9},{9,8},{10,11... | collective-permute-start | bytes 392 | tf_op jit(solution)/shard_map/ppermute | solution.py:328
  18.4 5.8 %collective-permute-start.6 = (bf16[16,56,128]{2,1,0:T(8,128)(2,1)S(1)}, bf16[16,56,128]{2,1,0:T(8,128)(2,1)S(1)}, u32[]{:S(2)}, u32[]{:S(2)}) collective-permute-start(bf16[16,56,128]{2,1,0:T(8,128)(2,1)S(1)} %get-tuple-element.37), channel_id=1, source_target_pairs={{0,1},{1,0},{2,3},{3,2},{4,5},{5,4},{6,7},{7,6},{8,9},{9,8},{10,11... | collective-permute-start | bytes 688136 | tf_op jit(solution)/shard_map/ppermute | solution.py:344
  24.1 1.6 %collective-permute-start.5 = (bf16[16,56,128]{2,1,0:T(8,128)(2,1)S(1)}, bf16[16,56,128]{2,1,0:T(8,128)(2,1)S(1)}, u32[]{:S(2)}, u32[]{:S(2)}) collective-permute-start(bf16[16,56,128]{2,1,0:T(8,128)(2,1)S(1)} %get-tuple-element.35), channel_id=1, source_target_pairs={{0,1},{1,0},{2,3},{3,2},{4,5},{5,4},{6,7},{7,6},{8,9},{9,8},{10,11... | collective-permute-start | bytes 688136 | tf_op jit(solution)/shard_map/ppermute | solution.py:344

commit v6 on v5

--- a/solution.py
+++ b/solution.py
@@ -328,11 +328,11 @@
     other_cells = lax.ppermute(cells, "core", swap)
     held = []
     for keep, send, w in all_parts(sens, psi, quad_table, quad_index, counts, coords):
-        held.append((keep, lax.ppermute(send, ("x", "core"), double(0))))
+        held.append((keep, lax.ppermute(send, ("x", "core"), double(len(held) % 2))))
     after = w
     for i, (keep, recv) in enumerate(held):
         keep, after = pair_sum(keep, recv, after)
-        held[i] = keep, lax.ppermute(after, ("x", "core"), double(1))
+        held[i] = keep, lax.ppermute(after, ("x", "core"), double((i + 1) % 2))
     both = smem(cells), smem(other_cells)
     count = len(held)
     full, swapped = [], []

time: 48.7 us -> 47.1 us (0.967)
  waiting for transfers between devices: 9.98 us -> 7.21 us
  starting transfers between devices: 6.58 us -> 7.45 us
    ppermute x4, waiting for transfers between devices: 9 us -> 6.69 us  [the longest x2 4.91 us: local(): held[i] = (keep, lax.ppermute(after, ('x', 'core'), double((i + 1) % 2)))]
    ppermute x4, starting transfers between devices: 6.29 us -> 7.2 us  [the longest x2 3.83 us: local(): lax.ppermute(send, ('x', 'core'), double(len(held) % 2))]
  transfers between devices with their start and end apart: 7 -> 7, of which waited for: 6 -> 4; matrix products, arithmetic and copies ran while one was open for 0% -> 0% of each run, Pallas kernels for 10% -> 10%
where the time goes in v6:
time: 47.1 us; the launch traced here: 46.9 us
  blocking collectives  21.4 us (45%)
  Pallas kernels  10.7 us (23%)
  starting transfers between devices  7.45 us (16%)
  waiting for transfers between devices  7.21 us (15%)
    all_to_all x1, blocking collectives, local(): slots = lax.all_to_all(slots, ('z', 'y'), 0, 0, tiled=True)  21.4 us
    ppermute x2, waiting for transfers between devices, local(): held[i] = (keep, lax.ppermute(after, ('x', 'core'), double((i + 1) % 2)))  4.91 us
    pallas_call x1, Pallas kernels, first_part(): pl.pallas_call(first_kernel, in_specs=[HBM] * 6, out_specs=[VMEM] * 6, ou...  4.37 us
    ppermute x2, starting transfers between devices, local(): lax.ppermute(send, ('x', 'core'), double(len(held) % 2))  3.83 us
    pallas_call x8, Pallas kernels, small_call(): pl.pallas_call(kernel, in_specs=in_specs, out_specs=[VMEM] * len(out_shap...  3.69 us
    ppermute x2, starting transfers between devices, local(): held[i] = (keep, lax.ppermute(after, ('x', 'core'), double((i + 1) % 2)))  3.37 us
    pallas_call x1, Pallas kernels, later_part(): pl.pallas_call(functools.partial(later_kernel, part, last), in_specs=[VME...  2.65 us
    ppermute x2, waiting for transfers between devices, local(): lax.ppermute(send, ('x', 'core'), double(len(held) % 2))  1.78 us
  transfers between devices with their start and end apart: 7, of which 4 were waited for; matrix products, arithmetic and copies ran while one was open for 0% of the time, Pallas kernels for 10%

profile of v6, /device:TPU:0, one launch (start us, length us, event | category | flops | bytes accessed | tf_op | source)
XLA Modules:
  0.0 46.9 jit_solution(8939280742861826628)
XLA Ops:
  0.0 4.4 %tiles_0.1 = (f32[16,56,128]{2,1,0:T(8,128)S(1)}, bf16[16,56,128]{2,1,0:T(8,128)(2,1)S(1)}, bf16[112,192]{1,0:T(8,128)(2,1)S(1)}, s32[32,128]{1,0:T(8,128)S(1)},...) custom-call(s32[32]{0:T(128)} %counts_hbm.1, f32[16]{0:T(128)} %table_hbm.1, s32[1,256]{1,0:T(1,128)} %bitcast.4, ...), custom_call_target="tpu_custom_call" | custom-call | flops 8000000000 | bytes 4000000 | tf_op jit(solution)/shard_map/tiles_0/pallas_call | solution.py:187
  4.4 1.7 %collective-permute-start.2 = (bf16[16,56,128]{2,1,0:T(8,128)(2,1)S(1)}, bf16[16,56,128]{2,1,0:T(8,128)(2,1)S(1)}, u32[]{:S(2)}, u32[]{:S(2)}) collective-permute-start(bf16[16,56,128]{2,1,0:T(8,128)(2,1)S(1)} %get-tuple-element.29), channel_id=1, source_target_pairs={{0,32},{1,97},{32,0},{33,65},{64,96},{65,33},{96,64},{97,1},{2,34}... | collective-permute-start | bytes 688136 | tf_op jit(solution)/shard_map/ppermute | solution.py:331
  6.0 2.6 %tiles_1.1 = (f32[16,56,128]{2,1,0:T(8,128)S(1)}, bf16[16,56,128]{2,1,0:T(8,128)(2,1)S(1)}) custom-call(s32[32,128]{1,0:T(8,128)S(1)} %get-tuple-element.22.count_rows, bf16[112,192]{1,0:T(8,128)(2,1)S(1)} %get-tuple-element.23.w_ref.after_ref, bf16[3,64,8192]{2,1,0:T(8,128)(2,1)S(1)} %get-tuple-element.24.sens_buf, f32[3,8192]{1,0:T(4,128)S(1)} %get-tuple-element.25.coords_buf), custom_call_target="tpu_custom_call" | custom-call | flops 8000000000 | bytes 4000000 | tf_op jit(solution)/shard_map/tiles_1/pallas_call | solution.py:212
  8.7 0.0 copy-start
  8.7 2.2 %collective-permute-start.1 = (bf16[16,56,128]{2,1,0:T(8,128)(2,1)S(1)}, bf16[16,56,128]{2,1,0:T(8,128)(2,1)S(1)}, u32[]{:S(2)}, u32[]{:S(2)}) collective-permute-start(bf16[16,56,128]{2,1,0:T(8,128)(2,1)S(1)} %get-tuple-element.27), channel_id=1, source_target_pairs={{0,96},{1,33},{32,64},{33,1},{64,32},{65,97},{96,0},{97,65},{2,98}... | collective-permute-start | bytes 688136 | tf_op jit(solution)/shard_map/ppermute | solution.py:331
  10.9 0.0 collective-permute-done.2.recv_ref
  10.9 0.1 pair_sum.4
  10.9 3.3 %collective-permute-start.4 = (bf16[16,56,128]{2,1,0:T(8,128)(2,1)S(1)}, bf16[16,56,128]{2,1,0:T(8,128)(2,1)S(1)}, u32[]{:S(2)}, u32[]{:S(2)}) collective-permute-start(bf16[16,56,128]{2,1,0:T(8,128)(2,1)S(1)} %get-tuple-element.30.after_ref), channel_id=1, source_target_pairs={{0,96},{1,33},{32,64},{33,1},{64,32},{65,97},{96,0},{97,65},{2,98}... | collective-permute-start | bytes 688136 | tf_op jit(solution)/shard_map/ppermute | solution.py:335
  14.2 1.8 %collective-permute-done.1.recv_ref = bf16[16,56,128]{2,1,0:T(8,128)(2,1)S(1)} collective-permute-done((bf16[16,56,128]{2,1,0:T(8,128)(2,1)S(1)}, bf16[16,56,128]{2,1,0:T(8,128)(2,1)S(1)}, u32[]{:S(2)}, u32[]{:S(2)}) %collective-permute-start.1) | collective-permute-done | bytes 229408 | tf_op jit(solution)/shard_map/ppermute | solution.py:331
  16.0 0.1 pair_sum.5
  16.1 0.1 collective-permute-start.3
  16.2 0.0 copy-done
  16.2 0.1 collective-permute-start
  16.3 3.1 %collective-permute-done.4.recv_ref = bf16[16,56,128]{2,1,0:T(8,128)(2,1)S(1)} collective-permute-done((bf16[16,56,128]{2,1,0:T(8,128)(2,1)S(1)}, bf16[16,56,128]{2,1,0:T(8,128)(2,1)S(1)}, u32[]{:S(2)}, u32[]{:S(2)}) %collective-permute-start.4) | collective-permute-done | bytes 229408 | tf_op jit(solution)/shard_map/ppermute | solution.py:335
  19.4 0.1 pair_sum.6
  19.5 0.1 collective-permute-start.6
  19.6 0.0 collective-permute-done.refs_1_
  19.6 0.8 %add.3.after_ref.refs_4_ = f32[48,56,128]{2,1,0:T(8,128)S(1)} custom-call(s32[32]{0:T(128)S(1)} %copy-done, s32[32]{0:T(128)S(1)} %collective-permute-done.refs_1_, f32[16,56,128]{2,1,0:T(8,128)S(1)} %get-tuple-element.34.refs_2_), custom_call_target="tpu_custom_call" | custom-call | flops 1 | bytes 1 | tf_op jit(solution)/shard_map/add/pallas_call | solution.py:238
  20.4 1.8 %collective-permute-done.3.recv_ref = bf16[16,56,128]{2,1,0:T(8,128)(2,1)S(1)} collective-permute-done((bf16[16,56,128]{2,1,0:T(8,128)(2,1)S(1)}, bf16[16,56,128]{2,1,0:T(8,128)(2,1)S(1)}, u32[]{:S(2)}, u32[]{:S(2)}) %collective-permute-start.3) | collective-permute-done | bytes 229408 | tf_op jit(solution)/shard_map/ppermute | solution.py:335
  22.2 0.1 pair_sum.7
  22.3 0.1 collective-permute-start.5
  22.3 0.0 collective-permute-done.6.refs_3_
  22.4 0.9 %add.4.refs_3_ = f32[48,56,128]{2,1,0:T(8,128)S(1)} custom-call(s32[32]{0:T(128)S(1)} %copy-done, s32[32]{0:T(128)S(1)} %collective-permute-done.refs_1_, f32[16,56,128]{2,1,0:T(8,128)S(1)} %get-tuple-element.36.refs_2_, bf16[16,56,128]{2,1,0:T(8,128)(2,1)S(1)} %collective-permute-done.6.refs_3_, ...), custom_call_target="tpu_custom_call", output_to_operand_aliasing={{}: (4, {})} | custom-call | flops 1 | bytes 1 | tf_op jit(solution)/shard_map/add/pallas_call | solution.py:238
  23.3 0.5 %collective-permute-done.5.refs_2_ = bf16[16,56,128]{2,1,0:T(8,128)(2,1)S(1)} collective-permute-done((bf16[16,56,128]{2,1,0:T(8,128)(2,1)S(1)}, bf16[16,56,128]{2,1,0:T(8,128)(2,1)S(1)}, u32[]{:S(2)}, u32[]{:S(2)}) %collective-permute-start.5) | collective-permute-done | bytes 229408 | tf_op jit(solution)/shard_map/ppermute | solution.py:344
  23.8 0.8 %add.5 = (f32[48,56,128]{2,1,0:T(8,128)S(1)}, bf16[48,56,128]{2,1,0:T(8,128)(2,1)S(1)}) custom-call(s32[32]{0:T(128)S(1)} %copy-done, s32[32]{0:T(128)S(1)} %collective-permute-done.refs_1_, bf16[16,56,128]{2,1,0:T(8,128)(2,1)S(1)} %collective-permute-done.5.refs_2_, f32[48,56,128]{2,1,0:T(8,128)S(1)} %add.4.refs_3_), custom_call_target="tpu_custom_call", output_to_operand_aliasing={{0}: (3, {})} | custom-call | flops 1 | bytes 1 | tf_op jit(solution)/shard_map/add/pallas_call | solution.py:238
  24.6 21.4 %all_to_all.5.in_ref = bf16[48,56,128]{2,1,0:T(8,128)(2,1)S(1)} all-to-all(bf16[48,56,128]{2,1,0:T(8,128)(2,1)S(1)} %get-tuple-element.38), channel_id=1, replica_groups=mesh['x'=4,'z'=4,'y'=4,'core'=2] {'z','y'}, dimensions={0} | all-to-all | bytes 1376256 | tf_op jit(solution)/shard_map/all_to_all | solution.py:348
  46.1 0.9 %owner_sum.1 = f32[192,105]{1,0:T(8,128)} custom-call(bf16[48,56,128]{2,1,0:T(8,128)(2,1)S(1)} %all_to_all.5.in_ref), custom_call_target="tpu_custom_call" | custom-call | flops 1 | bytes 1 | tf_op jit(solution)/shard_map/owner_sum/pallas_call | solution.py:238
Async XLA Ops:
  4.4 6.5 %collective-permute-start.2 = (bf16[16,56,128]{2,1,0:T(8,128)(2,1)S(1)}, bf16[16,56,128]{2,1,0:T(8,128)(2,1)S(1)}, u32[]{:S(2)}, u32[]{:S(2)}) collective-permute-start(bf16[16,56,128]{2,1,0:T(8,128)(2,1)S(1)} %get-tuple-element.29), channel_id=1, source_target_pairs={{0,32},{1,97},{32,0},{33,65},{64,96},{65,33},{96,64},{97,1},{2,34}... | collective-permute-start | bytes 688136 | tf_op jit(solution)/shard_map/ppermute | solution.py:331
  8.7 7.5 %copy-start = (s32[32]{0:T(128)S(1)}, s32[32]{0:T(128)}, u32[]{:S(2)}) copy-start(s32[32]{0:T(128)} %refs_0_.5) | copy-start | bytes 388
  8.7 7.3 %collective-permute-start.1 = (bf16[16,56,128]{2,1,0:T(8,128)(2,1)S(1)}, bf16[16,56,128]{2,1,0:T(8,128)(2,1)S(1)}, u32[]{:S(2)}, u32[]{:S(2)}) collective-permute-start(bf16[16,56,128]{2,1,0:T(8,128)(2,1)S(1)} %get-tuple-element.27), channel_id=1, source_target_pairs={{0,96},{1,33},{32,64},{33,1},{64,32},{65,97},{96,0},{97,65},{2,98}... | collective-permute-start | bytes 688136 | tf_op jit(solution)/shard_map/ppermute | solution.py:331
  10.9 8.5 %collective-permute-start.4 = (bf16[16,56,128]{2,1,0:T(8,128)(2,1)S(1)}, bf16[16,56,128]{2,1,0:T(8,128)(2,1)S(1)}, u32[]{:S(2)}, u32[]{:S(2)}) collective-permute-start(bf16[16,56,128]{2,1,0:T(8,128)(2,1)S(1)} %get-tuple-element.30.after_ref), channel_id=1, source_target_pairs={{0,96},{1,33},{32,64},{33,1},{64,32},{65,97},{96,0},{97,65},{2,98}... | collective-permute-start | bytes 688136 | tf_op jit(solution)/shard_map/ppermute | solution.py:335
  16.1 6.1 %collective-permute-start.3 = (bf16[16,56,128]{2,1,0:T(8,128)(2,1)S(1)}, bf16[16,56,128]{2,1,0:T(8,128)(2,1)S(1)}, u32[]{:S(2)}, u32[]{:S(2)}) collective-permute-start(bf16[16,56,128]{2,1,0:T(8,128)(2,1)S(1)} %get-tuple-element.32.after_ref), channel_id=1, source_target_pairs={{0,32},{1,97},{32,0},{33,65},{64,96},{65,33},{96,64},{97,1},{2,34}... | collective-permute-start | bytes 688136 | tf_op jit(solution)/shard_map/ppermute | solution.py:335
  16.2 3.4 %collective-permute-start = (s32[32]{0:T(128)S(1)}, s32[32]{0:T(128)S(1)}, u32[]{:S(2)}, u32[]{:S(2)}) collective-permute-start(s32[32]{0:T(128)S(1)} %copy-done), channel_id=1, source_target_pairs={{0,1},{1,0},{2,3},{3,2},{4,5},{5,4},{6,7},{7,6},{8,9},{9,8},{10,11... | collective-permute-start | bytes 392 | tf_op jit(solution)/shard_map/ppermute | solution.py:328
  19.5 2.9 %collective-permute-start.6 = (bf16[16,56,128]{2,1,0:T(8,128)(2,1)S(1)}, bf16[16,56,128]{2,1,0:T(8,128)(2,1)S(1)}, u32[]{:S(2)}, u32[]{:S(2)}) collective-permute-start(bf16[16,56,128]{2,1,0:T(8,128)(2,1)S(1)} %get-tuple-element.37), channel_id=1, source_target_pairs={{0,1},{1,0},{2,3},{3,2},{4,5},{5,4},{6,7},{7,6},{8,9},{9,8},{10,11... | collective-permute-start | bytes 688136 | tf_op jit(solution)/shard_map/ppermute | solution.py:344
  22.3 1.6 %collective-permute-start.5 = (bf16[16,56,128]{2,1,0:T(8,128)(2,1)S(1)}, bf16[16,56,128]{2,1,0:T(8,128)(2,1)S(1)}, u32[]{:S(2)}, u32[]{:S(2)}) collective-permute-start(bf16[16,56,128]{2,1,0:T(8,128)(2,1)S(1)} %get-tuple-element.35), channel_id=1, source_target_pairs={{0,1},{1,0},{2,3},{3,2},{4,5},{5,4},{6,7},{7,6},{8,9},{9,8},{10,11... | collective-permute-start | bytes 688136 | tf_op jit(solution)/shard_map/ppermute | solution.py:344

commit v7 on v6

--- a/solution.py
+++ b/solution.py
@@ -134,15 +134,17 @@
         copy.start()
     for copy in small:
         copy.wait()
+    for copy in later[0]:
+        copy.start()
     for p in range(count_rows.shape[0]):
         count_rows[p : p + 1, :] = jnp.full((1, LANES), counts_ref[p], jnp.int32)
+    for copy in mine[0]:
+        copy.wait()
     weights(table_ref, index_ref, psi_ref, pad_ref, w_ref)
     w = w_ref[...]
     for i, patches in enumerate(chunks_of(FIRST_CHUNKS)):
-        for copy in mine[i]:
+        for copy in mine[i] if i > 0 else ():
             copy.wait()
-        for copy in later[i] if i < len(later) else ():
-            copy.start()
         chunk_tiles(patches, lambda p: counts_ref[p], sens_buf, coords_buf, w, keep_ref, send_ref)
     for pair in later:
         for copy in pair:
@@ -269,7 +271,7 @@
 
         @pl.when(((owner >> 5) == my_x) & ((owner & 1) == my_core))
         def _():
-            at = ((owner & 31) >> 1) * 3 + within
+            at = (((owner >> 1) & 3) * 4 + ((owner >> 3) & 3)) * 3 + within
             dense_ref[at] += tiles_ref[p].astype(jnp.float32)
 
 
@@ -345,7 +347,7 @@
     plan = [(0, count - 1)] + [(1, j) for j in range(count - 1)]
     dense = add(both, plan, [full[-1]] + swapped[:-1], dense)
     slots = add(both, [(1, count - 1)], swapped[-1:], dense, True)
-    slots = lax.all_to_all(slots, ("z", "y"), 0, 0, tiled=True)
+    slots = lax.all_to_all(slots, ("y", "z"), 0, 0, tiled=True)
     out = jax.ShapeDtypeStruct((192, 3 * K), jnp.float32)
     return small_call(owner_sum_kernel, out, [VMEM], (slots,), "owner_sum").T
 

time: 47.1 us -> 46.7 us (level)
  no operation moved by 1% of the time
where the time goes in v7:
time: 46.7 us; the launch traced here: 46.6 us
  blocking collectives  21.2 us (45%)
  Pallas kernels  10.6 us (23%)
  starting transfers between devices  7.44 us (16%)
  waiting for transfers between devices  7.21 us (15%)
    all_to_all x1, blocking collectives, local(): slots = lax.all_to_all(slots, ('y', 'z'), 0, 0, tiled=True)  21.2 us
    ppermute x2, waiting for transfers between devices, local(): held[i] = (keep, lax.ppermute(after, ('x', 'core'), double((i + 1) % 2)))  4.91 us
    pallas_call x1, Pallas kernels, first_part(): pl.pallas_call(first_kernel, in_specs=[HBM] * 6, out_specs=[VMEM] * 6, ou...  4.25 us
    ppermute x2, starting transfers between devices, local(): lax.ppermute(send, ('x', 'core'), double(len(held) % 2))  3.83 us
    pallas_call x8, Pallas kernels, small_call(): pl.pallas_call(kernel, in_specs=in_specs, out_specs=[VMEM] * len(out_shap...  3.69 us
    ppermute x2, starting transfers between devices, local(): held[i] = (keep, lax.ppermute(after, ('x', 'core'), double((i + 1) % 2)))  3.35 us
    pallas_call x1, Pallas kernels, later_part(): pl.pallas_call(functools.partial(later_kernel, part, last), in_specs=[VME...  2.65 us
    ppermute x2, waiting for transfers between devices, local(): lax.ppermute(send, ('x', 'core'), double(len(held) % 2))  1.79 us
  transfers between devices with their start and end apart: 7, of which 4 were waited for; matrix products, arithmetic and copies ran while one was open for 0% of the time, Pallas kernels for 10%

profile of v7, /device:TPU:0, one launch (start us, length us, event | category | flops | bytes accessed | tf_op | source)
XLA Modules:
  0.0 46.6 jit_solution(6526974769847315963)
XLA Ops:
  0.0 4.3 %tiles_0.1 = (f32[16,56,128]{2,1,0:T(8,128)S(1)}, bf16[16,56,128]{2,1,0:T(8,128)(2,1)S(1)}, bf16[112,192]{1,0:T(8,128)(2,1)S(1)}, s32[32,128]{1,0:T(8,128)S(1)},...) custom-call(s32[32]{0:T(128)} %counts_hbm.1, f32[16]{0:T(128)} %table_hbm.1, s32[1,256]{1,0:T(1,128)} %bitcast.4, ...), custom_call_target="tpu_custom_call" | custom-call | flops 8000000000 | bytes 4000000 | tf_op jit(solution)/shard_map/tiles_0/pallas_call | solution.py:189
  4.3 1.7 %collective-permute-start.2 = (bf16[16,56,128]{2,1,0:T(8,128)(2,1)S(1)}, bf16[16,56,128]{2,1,0:T(8,128)(2,1)S(1)}, u32[]{:S(2)}, u32[]{:S(2)}) collective-permute-start(bf16[16,56,128]{2,1,0:T(8,128)(2,1)S(1)} %get-tuple-element.29), channel_id=1, source_target_pairs={{0,32},{1,97},{32,0},{33,65},{64,96},{65,33},{96,64},{97,1},{2,34}... | collective-permute-start | bytes 688136 | tf_op jit(solution)/shard_map/ppermute | solution.py:333
  5.9 2.6 %tiles_1.1 = (f32[16,56,128]{2,1,0:T(8,128)S(1)}, bf16[16,56,128]{2,1,0:T(8,128)(2,1)S(1)}) custom-call(s32[32,128]{1,0:T(8,128)S(1)} %get-tuple-element.22.count_rows, bf16[112,192]{1,0:T(8,128)(2,1)S(1)} %get-tuple-element.23.w_ref.after_ref, bf16[3,64,8192]{2,1,0:T(8,128)(2,1)S(1)} %get-tuple-element.24.sens_buf, f32[3,8192]{1,0:T(4,128)S(1)} %get-tuple-element.25.coords_buf), custom_call_target="tpu_custom_call" | custom-call | flops 8000000000 | bytes 4000000 | tf_op jit(solution)/shard_map/tiles_1/pallas_call | solution.py:214
  8.6 0.0 copy-start
  8.6 2.2 %collective-permute-start.1 = (bf16[16,56,128]{2,1,0:T(8,128)(2,1)S(1)}, bf16[16,56,128]{2,1,0:T(8,128)(2,1)S(1)}, u32[]{:S(2)}, u32[]{:S(2)}) collective-permute-start(bf16[16,56,128]{2,1,0:T(8,128)(2,1)S(1)} %get-tuple-element.27), channel_id=1, source_target_pairs={{0,96},{1,33},{32,64},{33,1},{64,32},{65,97},{96,0},{97,65},{2,98}... | collective-permute-start | bytes 688136 | tf_op jit(solution)/shard_map/ppermute | solution.py:333
  10.8 0.0 collective-permute-done.2.recv_ref
  10.8 0.1 pair_sum.4
  10.8 3.3 %collective-permute-start.4 = (bf16[16,56,128]{2,1,0:T(8,128)(2,1)S(1)}, bf16[16,56,128]{2,1,0:T(8,128)(2,1)S(1)}, u32[]{:S(2)}, u32[]{:S(2)}) collective-permute-start(bf16[16,56,128]{2,1,0:T(8,128)(2,1)S(1)} %get-tuple-element.30.after_ref), channel_id=1, source_target_pairs={{0,96},{1,33},{32,64},{33,1},{64,32},{65,97},{96,0},{97,65},{2,98}... | collective-permute-start | bytes 688136 | tf_op jit(solution)/shard_map/ppermute | solution.py:337
  14.1 1.8 %collective-permute-done.1.recv_ref = bf16[16,56,128]{2,1,0:T(8,128)(2,1)S(1)} collective-permute-done((bf16[16,56,128]{2,1,0:T(8,128)(2,1)S(1)}, bf16[16,56,128]{2,1,0:T(8,128)(2,1)S(1)}, u32[]{:S(2)}, u32[]{:S(2)}) %collective-permute-start.1) | collective-permute-done | bytes 229408 | tf_op jit(solution)/shard_map/ppermute | solution.py:333
  15.9 0.1 pair_sum.5
  16.0 0.1 collective-permute-start.3
  16.1 0.0 copy-done
  16.1 0.1 collective-permute-start
  16.2 3.1 %collective-permute-done.4.recv_ref = bf16[16,56,128]{2,1,0:T(8,128)(2,1)S(1)} collective-permute-done((bf16[16,56,128]{2,1,0:T(8,128)(2,1)S(1)}, bf16[16,56,128]{2,1,0:T(8,128)(2,1)S(1)}, u32[]{:S(2)}, u32[]{:S(2)}) %collective-permute-start.4) | collective-permute-done | bytes 229408 | tf_op jit(solution)/shard_map/ppermute | solution.py:337
  19.3 0.1 pair_sum.6
  19.3 0.1 collective-permute-start.6
  19.4 0.0 collective-permute-done.refs_1_
  19.4 0.8 %add.3.after_ref.refs_4_ = f32[48,56,128]{2,1,0:T(8,128)S(1)} custom-call(s32[32]{0:T(128)S(1)} %copy-done, s32[32]{0:T(128)S(1)} %collective-permute-done.refs_1_, f32[16,56,128]{2,1,0:T(8,128)S(1)} %get-tuple-element.34.refs_2_), custom_call_target="tpu_custom_call" | custom-call | flops 1 | bytes 1 | tf_op jit(solution)/shard_map/add/pallas_call | solution.py:240
  20.3 1.8 %collective-permute-done.3.recv_ref = bf16[16,56,128]{2,1,0:T(8,128)(2,1)S(1)} collective-permute-done((bf16[16,56,128]{2,1,0:T(8,128)(2,1)S(1)}, bf16[16,56,128]{2,1,0:T(8,128)(2,1)S(1)}, u32[]{:S(2)}, u32[]{:S(2)}) %collective-permute-start.3) | collective-permute-done | bytes 229408 | tf_op jit(solution)/shard_map/ppermute | solution.py:337
  22.1 0.1 pair_sum.7
  22.1 0.1 collective-permute-start.5
  22.2 0.0 collective-permute-done.6.refs_3_
  22.2 1.0 %add.4.refs_3_ = f32[48,56,128]{2,1,0:T(8,128)S(1)} custom-call(s32[32]{0:T(128)S(1)} %copy-done, s32[32]{0:T(128)S(1)} %collective-permute-done.refs_1_, f32[16,56,128]{2,1,0:T(8,128)S(1)} %get-tuple-element.36.refs_2_, bf16[16,56,128]{2,1,0:T(8,128)(2,1)S(1)} %collective-permute-done.6.refs_3_, ...), custom_call_target="tpu_custom_call", output_to_operand_aliasing={{}: (4, {})} | custom-call | flops 1 | bytes 1 | tf_op jit(solution)/shard_map/add/pallas_call | solution.py:240
  23.2 0.5 %collective-permute-done.5.refs_2_ = bf16[16,56,128]{2,1,0:T(8,128)(2,1)S(1)} collective-permute-done((bf16[16,56,128]{2,1,0:T(8,128)(2,1)S(1)}, bf16[16,56,128]{2,1,0:T(8,128)(2,1)S(1)}, u32[]{:S(2)}, u32[]{:S(2)}) %collective-permute-start.5) | collective-permute-done | bytes 229408 | tf_op jit(solution)/shard_map/ppermute | solution.py:346
  23.7 0.8 %add.5 = (f32[48,56,128]{2,1,0:T(8,128)S(1)}, bf16[48,56,128]{2,1,0:T(8,128)(2,1)S(1)}) custom-call(s32[32]{0:T(128)S(1)} %copy-done, s32[32]{0:T(128)S(1)} %collective-permute-done.refs_1_, bf16[16,56,128]{2,1,0:T(8,128)(2,1)S(1)} %collective-permute-done.5.refs_2_, f32[48,56,128]{2,1,0:T(8,128)S(1)} %add.4.refs_3_), custom_call_target="tpu_custom_call", output_to_operand_aliasing={{0}: (3, {})} | custom-call | flops 1 | bytes 1 | tf_op jit(solution)/shard_map/add/pallas_call | solution.py:240
  24.5 21.2 %all_to_all.5.in_ref = bf16[48,56,128]{2,1,0:T(8,128)(2,1)S(1)} all-to-all(bf16[48,56,128]{2,1,0:T(8,128)(2,1)S(1)} %get-tuple-element.38), channel_id=1, replica_groups=mesh['x'=4,'z'=4,'y'=4,'core'=2] {'y','z'}, dimensions={0} | all-to-all | bytes 1376256 | tf_op jit(solution)/shard_map/all_to_all | solution.py:350
  45.7 0.9 %owner_sum.1 = f32[192,105]{1,0:T(8,128)} custom-call(bf16[48,56,128]{2,1,0:T(8,128)(2,1)S(1)} %all_to_all.5.in_ref), custom_call_target="tpu_custom_call" | custom-call | flops 1 | bytes 1 | tf_op jit(solution)/shard_map/owner_sum/pallas_call | solution.py:240
Async XLA Ops:
  4.3 6.5 %collective-permute-start.2 = (bf16[16,56,128]{2,1,0:T(8,128)(2,1)S(1)}, bf16[16,56,128]{2,1,0:T(8,128)(2,1)S(1)}, u32[]{:S(2)}, u32[]{:S(2)}) collective-permute-start(bf16[16,56,128]{2,1,0:T(8,128)(2,1)S(1)} %get-tuple-element.29), channel_id=1, source_target_pairs={{0,32},{1,97},{32,0},{33,65},{64,96},{65,33},{96,64},{97,1},{2,34}... | collective-permute-start | bytes 688136 | tf_op jit(solution)/shard_map/ppermute | solution.py:333
  8.6 7.5 %copy-start = (s32[32]{0:T(128)S(1)}, s32[32]{0:T(128)}, u32[]{:S(2)}) copy-start(s32[32]{0:T(128)} %refs_0_.5) | copy-start | bytes 388
  8.6 7.3 %collective-permute-start.1 = (bf16[16,56,128]{2,1,0:T(8,128)(2,1)S(1)}, bf16[16,56,128]{2,1,0:T(8,128)(2,1)S(1)}, u32[]{:S(2)}, u32[]{:S(2)}) collective-permute-start(bf16[16,56,128]{2,1,0:T(8,128)(2,1)S(1)} %get-tuple-element.27), channel_id=1, source_target_pairs={{0,96},{1,33},{32,64},{33,1},{64,32},{65,97},{96,0},{97,65},{2,98}... | collective-permute-start | bytes 688136 | tf_op jit(solution)/shard_map/ppermute | solution.py:333
  10.8 8.4 %collective-permute-start.4 = (bf16[16,56,128]{2,1,0:T(8,128)(2,1)S(1)}, bf16[16,56,128]{2,1,0:T(8,128)(2,1)S(1)}, u32[]{:S(2)}, u32[]{:S(2)}) collective-permute-start(bf16[16,56,128]{2,1,0:T(8,128)(2,1)S(1)} %get-tuple-element.30.after_ref), channel_id=1, source_target_pairs={{0,96},{1,33},{32,64},{33,1},{64,32},{65,97},{96,0},{97,65},{2,98}... | collective-permute-start | bytes 688136 | tf_op jit(solution)/shard_map/ppermute | solution.py:337
  16.0 6.1 %collective-permute-start.3 = (bf16[16,56,128]{2,1,0:T(8,128)(2,1)S(1)}, bf16[16,56,128]{2,1,0:T(8,128)(2,1)S(1)}, u32[]{:S(2)}, u32[]{:S(2)}) collective-permute-start(bf16[16,56,128]{2,1,0:T(8,128)(2,1)S(1)} %get-tuple-element.32.after_ref), channel_id=1, source_target_pairs={{0,32},{1,97},{32,0},{33,65},{64,96},{65,33},{96,64},{97,1},{2,34}... | collective-permute-start | bytes 688136 | tf_op jit(solution)/shard_map/ppermute | solution.py:337
  16.1 3.4 %collective-permute-start = (s32[32]{0:T(128)S(1)}, s32[32]{0:T(128)S(1)}, u32[]{:S(2)}, u32[]{:S(2)}) collective-permute-start(s32[32]{0:T(128)S(1)} %copy-done), channel_id=1, source_target_pairs={{0,1},{1,0},{2,3},{3,2},{4,5},{5,4},{6,7},{7,6},{8,9},{9,8},{10,11... | collective-permute-start | bytes 392 | tf_op jit(solution)/shard_map/ppermute | solution.py:330
  19.3 2.9 %collective-permute-start.6 = (bf16[16,56,128]{2,1,0:T(8,128)(2,1)S(1)}, bf16[16,56,128]{2,1,0:T(8,128)(2,1)S(1)}, u32[]{:S(2)}, u32[]{:S(2)}) collective-permute-start(bf16[16,56,128]{2,1,0:T(8,128)(2,1)S(1)} %get-tuple-element.37), channel_id=1, source_target_pairs={{0,1},{1,0},{2,3},{3,2},{4,5},{5,4},{6,7},{7,6},{8,9},{9,8},{10,11... | collective-permute-start | bytes 688136 | tf_op jit(solution)/shard_map/ppermute | solution.py:346
  22.1 1.6 %collective-permute-start.5 = (bf16[16,56,128]{2,1,0:T(8,128)(2,1)S(1)}, bf16[16,56,128]{2,1,0:T(8,128)(2,1)S(1)}, u32[]{:S(2)}, u32[]{:S(2)}) collective-permute-start(bf16[16,56,128]{2,1,0:T(8,128)(2,1)S(1)} %get-tuple-element.35), channel_id=1, source_target_pairs={{0,1},{1,0},{2,3},{3,2},{4,5},{5,4},{6,7},{7,6},{8,9},{9,8},{10,11... | collective-permute-start | bytes 688136 | tf_op jit(solution)/shard_map/ppermute | solution.py:346

commit v8 on v7

--- a/solution.py
+++ b/solution.py
@@ -331,7 +331,7 @@
     held = []
     for keep, send, w in all_parts(sens, psi, quad_table, quad_index, counts, coords):
         held.append((keep, lax.ppermute(send, ("x", "core"), double(len(held) % 2))))
-    after = w
+    after = other_cells
     for i, (keep, recv) in enumerate(held):
         keep, after = pair_sum(keep, recv, after)
         held[i] = keep, lax.ppermute(after, ("x", "core"), double((i + 1) % 2))
@@ -339,13 +339,11 @@
     count = len(held)
     full, swapped = [], []
     for i, (keep, recv) in enumerate(held):
-        if i == count - 1:
-            after = dense = add(both, [(0, j) for j in range(i)], full)
         tiles, after = pair_sum(keep, recv, after)
         full.append(tiles)
         swapped.append(lax.ppermute(after, "core", swap))
-    plan = [(0, count - 1)] + [(1, j) for j in range(count - 1)]
-    dense = add(both, plan, [full[-1]] + swapped[:-1], dense)
+    plan = [(0, j) for j in range(count)] + [(1, j) for j in range(count - 1)]
+    dense = add(both, plan, full + swapped[:-1])
     slots = add(both, [(1, count - 1)], swapped[-1:], dense, True)
     slots = lax.all_to_all(slots, ("y", "z"), 0, 0, tiled=True)
     out = jax.ShapeDtypeStruct((192, 3 * K), jnp.float32)

time: 46.7 us -> 46.8 us (level)
  waiting for transfers between devices: 7.21 us -> 8.99 us
  starting transfers between devices: 7.44 us -> 6.25 us
  Pallas kernels: 10.6 us -> 10 us
    ppermute x1, waiting for transfers between devices: 0.01 us -> 1.12 us  [local(): other_cells = lax.ppermute(cells, 'core', swap)]
    ppermute x2, starting transfers between devices: 3.35 us -> 2.24 us  [local(): held[i] = (keep, lax.ppermute(after, ('x', 'core'), double((i + 1) % 2)))]
    ppermute x2, waiting for transfers between devices: 4.91 us -> 5.84 us  [local(): held[i] = (keep, lax.ppermute(after, ('x', 'core'), double((i + 1) % 2)))]
    pallas_call x8 -> x7, Pallas kernels: 3.69 us -> 3.14 us  [small_call(): pl.pallas_call(kernel, in_specs=in_specs, out_specs=[VMEM] * len(out_shap...]
  transfers between devices with their start and end apart: 7 -> 7, of which waited for: 4 -> 5; matrix products, arithmetic and copies ran while one was open for 0% -> 0% of each run, Pallas kernels for 10% -> 9%
where the time goes in v8:
time: 46.8 us; the launch traced here: 46.7 us
  blocking collectives  21.3 us (46%)
  Pallas kernels  10 us (21%)
  waiting for transfers between devices  8.99 us (19%)
  starting transfers between devices  6.25 us (13%)
    all_to_all x1, blocking collectives, local(): slots = lax.all_to_all(slots, ('y', 'z'), 0, 0, tiled=True)  21.3 us
    ppermute x2, waiting for transfers between devices, local(): held[i] = (keep, lax.ppermute(after, ('x', 'core'), double((i + 1) % 2)))  5.84 us
    pallas_call x1, Pallas kernels, first_part(): pl.pallas_call(first_kernel, in_specs=[HBM] * 6, out_specs=[VMEM] * 6, ou...  4.25 us
    ppermute x2, starting transfers between devices, local(): lax.ppermute(send, ('x', 'core'), double(len(held) % 2))  3.83 us
    pallas_call x7, Pallas kernels, small_call(): pl.pallas_call(kernel, in_specs=in_specs, out_specs=[VMEM] * len(out_shap...  3.14 us
    pallas_call x1, Pallas kernels, later_part(): pl.pallas_call(functools.partial(later_kernel, part, last), in_specs=[VME...  2.65 us
    ppermute x2, starting transfers between devices, local(): held[i] = (keep, lax.ppermute(after, ('x', 'core'), double((i + 1) % 2)))  2.24 us
    ppermute x2, waiting for transfers between devices, local(): lax.ppermute(send, ('x', 'core'), double(len(held) % 2))  1.78 us
  transfers between devices with their start and end apart: 7, of which 5 were waited for; matrix products, arithmetic and copies ran while one was open for 0% of the time, Pallas kernels for 9%

profile of v8, /device:TPU:0, one launch (start us, length us, event | category | flops | bytes accessed | tf_op | source)
XLA Modules:
  0.0 46.7 jit_solution(14376031741197507260)
XLA Ops:
  0.0 4.3 %tiles_0.1 = (f32[16,56,128]{2,1,0:T(8,128)S(1)}, bf16[16,56,128]{2,1,0:T(8,128)(2,1)S(1)}, bf16[112,192]{1,0:T(8,128)(2,1)S(1)}, s32[32,128]{1,0:T(8,128)S(1)},...) custom-call(s32[32]{0:T(128)} %counts_hbm.1, f32[16]{0:T(128)} %table_hbm.1, s32[1,256]{1,0:T(1,128)} %bitcast.4, ...), custom_call_target="tpu_custom_call" | custom-call | flops 8000000000 | bytes 4000000 | tf_op jit(solution)/shard_map/tiles_0/pallas_call | solution.py:189
  4.3 1.7 %collective-permute-start.2 = (bf16[16,56,128]{2,1,0:T(8,128)(2,1)S(1)}, bf16[16,56,128]{2,1,0:T(8,128)(2,1)S(1)}, u32[]{:S(2)}, u32[]{:S(2)}) collective-permute-start(bf16[16,56,128]{2,1,0:T(8,128)(2,1)S(1)} %get-tuple-element.29), channel_id=1, source_target_pairs={{0,32},{1,97},{32,0},{33,65},{64,96},{65,33},{96,64},{97,1},{2,34}... | collective-permute-start | bytes 688136 | tf_op jit(solution)/shard_map/ppermute | solution.py:333
  5.9 0.0 copy-start
  5.9 2.6 %tiles_1.1 = (f32[16,56,128]{2,1,0:T(8,128)S(1)}, bf16[16,56,128]{2,1,0:T(8,128)(2,1)S(1)}) custom-call(s32[32,128]{1,0:T(8,128)S(1)} %get-tuple-element.22.count_rows, bf16[112,192]{1,0:T(8,128)(2,1)S(1)} %get-tuple-element.23.w_ref, bf16[3,64,8192]{2,1,0:T(8,128)(2,1)S(1)} %get-tuple-element.24.sens_buf, f32[3,8192]{1,0:T(4,128)S(1)} %get-tuple-element.25.coords_buf), custom_call_target="tpu_custom_call" | custom-call | flops 8000000000 | bytes 4000000 | tf_op jit(solution)/shard_map/tiles_1/pallas_call | solution.py:214
  8.6 2.2 %collective-permute-start.1 = (bf16[16,56,128]{2,1,0:T(8,128)(2,1)S(1)}, bf16[16,56,128]{2,1,0:T(8,128)(2,1)S(1)}, u32[]{:S(2)}, u32[]{:S(2)}) collective-permute-start(bf16[16,56,128]{2,1,0:T(8,128)(2,1)S(1)} %get-tuple-element.27), channel_id=1, source_target_pairs={{0,96},{1,33},{32,64},{33,1},{64,32},{65,97},{96,0},{97,65},{2,98}... | collective-permute-start | bytes 688136 | tf_op jit(solution)/shard_map/ppermute | solution.py:333
  10.8 0.0 copy-done
  10.8 0.0 collective-permute-start
  10.8 1.1 %collective-permute-done.after_ref.refs_1_ = s32[32]{0:T(128)S(1)} collective-permute-done((s32[32]{0:T(128)S(1)}, s32[32]{0:T(128)S(1)}, u32[]{:S(2)}, u32[]{:S(2)}) %collective-permute-start) | collective-permute-done | bytes 160 | tf_op jit(solution)/shard_map/ppermute | solution.py:330
  11.9 0.0 collective-permute-done.2.recv_ref
  11.9 0.1 pair_sum.4
  12.0 2.2 %collective-permute-start.4 = (bf16[16,56,128]{2,1,0:T(8,128)(2,1)S(1)}, bf16[16,56,128]{2,1,0:T(8,128)(2,1)S(1)}, u32[]{:S(2)}, u32[]{:S(2)}) collective-permute-start(bf16[16,56,128]{2,1,0:T(8,128)(2,1)S(1)} %get-tuple-element.30.after_ref), channel_id=1, source_target_pairs={{0,96},{1,33},{32,64},{33,1},{64,32},{65,97},{96,0},{97,65},{2,98}... | collective-permute-start | bytes 688136 | tf_op jit(solution)/shard_map/ppermute | solution.py:337
  14.1 1.8 %collective-permute-done.1.recv_ref = bf16[16,56,128]{2,1,0:T(8,128)(2,1)S(1)} collective-permute-done((bf16[16,56,128]{2,1,0:T(8,128)(2,1)S(1)}, bf16[16,56,128]{2,1,0:T(8,128)(2,1)S(1)}, u32[]{:S(2)}, u32[]{:S(2)}) %collective-permute-start.1) | collective-permute-done | bytes 229408 | tf_op jit(solution)/shard_map/ppermute | solution.py:333
  15.9 0.1 pair_sum.5
  16.0 0.1 collective-permute-start.3
  16.0 3.8 %collective-permute-done.4.recv_ref = bf16[16,56,128]{2,1,0:T(8,128)(2,1)S(1)} collective-permute-done((bf16[16,56,128]{2,1,0:T(8,128)(2,1)S(1)}, bf16[16,56,128]{2,1,0:T(8,128)(2,1)S(1)}, u32[]{:S(2)}, u32[]{:S(2)}) %collective-permute-start.4) | collective-permute-done | bytes 229408 | tf_op jit(solution)/shard_map/ppermute | solution.py:337
  19.9 0.1 pair_sum.6
  19.9 0.1 collective-permute-start.6
  20.0 2.0 %collective-permute-done.3.recv_ref = bf16[16,56,128]{2,1,0:T(8,128)(2,1)S(1)} collective-permute-done((bf16[16,56,128]{2,1,0:T(8,128)(2,1)S(1)}, bf16[16,56,128]{2,1,0:T(8,128)(2,1)S(1)}, u32[]{:S(2)}, u32[]{:S(2)}) %collective-permute-start.3) | collective-permute-done | bytes 229408 | tf_op jit(solution)/shard_map/ppermute | solution.py:337
  22.1 0.1 pair_sum.7
  22.1 0.1 collective-permute-start.5
  22.2 0.0 collective-permute-done.6.refs_4_
  22.2 1.2 %add.2.refs_3_ = f32[48,56,128]{2,1,0:T(8,128)S(1)} custom-call(s32[32]{0:T(128)S(1)} %copy-done, s32[32]{0:T(128)S(1)} %collective-permute-done.after_ref.refs_1_, f32[16,56,128]{2,1,0:T(8,128)S(1)} %get-tuple-element.36.refs_2_, f32[16,56,128]{2,1,0:T(8,128)S(1)} %get-tuple-element.37.refs_3_, bf16[16,56,128]{2,1,0:T(8,128)(2,1)S(1)} %collective-permute-done.6.refs_4_), custom_call_target="tpu_custom_call" | custom-call | flops 1 | bytes 1 | tf_op jit(solution)/shard_map/add/pallas_call | solution.py:240
  23.4 0.2 collective-permute-done.5.refs_2_
  23.7 0.8 %add.3 = (f32[48,56,128]{2,1,0:T(8,128)S(1)}, bf16[48,56,128]{2,1,0:T(8,128)(2,1)S(1)}) custom-call(s32[32]{0:T(128)S(1)} %copy-done, s32[32]{0:T(128)S(1)} %collective-permute-done.after_ref.refs_1_, bf16[16,56,128]{2,1,0:T(8,128)(2,1)S(1)} %collective-permute-done.5.refs_2_, f32[48,56,128]{2,1,0:T(8,128)S(1)} %add.2.refs_3_), custom_call_target="tpu_custom_call", output_to_operand_aliasing={{0}: (3, {})} | custom-call | flops 1 | bytes 1 | tf_op jit(solution)/shard_map/add/pallas_call | solution.py:240
  24.5 21.3 %all_to_all.5.in_ref = bf16[48,56,128]{2,1,0:T(8,128)(2,1)S(1)} all-to-all(bf16[48,56,128]{2,1,0:T(8,128)(2,1)S(1)} %get-tuple-element.38), channel_id=1, replica_groups=mesh['x'=4,'z'=4,'y'=4,'core'=2] {'y','z'}, dimensions={0} | all-to-all | bytes 1376256 | tf_op jit(solution)/shard_map/all_to_all | solution.py:348
  45.8 0.9 %owner_sum.1 = f32[192,105]{1,0:T(8,128)} custom-call(bf16[48,56,128]{2,1,0:T(8,128)(2,1)S(1)} %all_to_all.5.in_ref), custom_call_target="tpu_custom_call" | custom-call | flops 1 | bytes 1 | tf_op jit(solution)/shard_map/owner_sum/pallas_call | solution.py:240
Async XLA Ops:
  4.3 7.6 %collective-permute-start.2 = (bf16[16,56,128]{2,1,0:T(8,128)(2,1)S(1)}, bf16[16,56,128]{2,1,0:T(8,128)(2,1)S(1)}, u32[]{:S(2)}, u32[]{:S(2)}) collective-permute-start(bf16[16,56,128]{2,1,0:T(8,128)(2,1)S(1)} %get-tuple-element.29), channel_id=1, source_target_pairs={{0,32},{1,97},{32,0},{33,65},{64,96},{65,33},{96,64},{97,1},{2,34}... | collective-permute-start | bytes 688136 | tf_op jit(solution)/shard_map/ppermute | solution.py:333
  5.9 4.8 %copy-start = (s32[32]{0:T(128)S(1)}, s32[32]{0:T(128)}, u32[]{:S(2)}) copy-start(s32[32]{0:T(128)} %refs_0_.3) | copy-start | bytes 388
  8.6 7.3 %collective-permute-start.1 = (bf16[16,56,128]{2,1,0:T(8,128)(2,1)S(1)}, bf16[16,56,128]{2,1,0:T(8,128)(2,1)S(1)}, u32[]{:S(2)}, u32[]{:S(2)}) collective-permute-start(bf16[16,56,128]{2,1,0:T(8,128)(2,1)S(1)} %get-tuple-element.27), channel_id=1, source_target_pairs={{0,96},{1,33},{32,64},{33,1},{64,32},{65,97},{96,0},{97,65},{2,98}... | collective-permute-start | bytes 688136 | tf_op jit(solution)/shard_map/ppermute | solution.py:333
  10.8 1.1 %collective-permute-start = (s32[32]{0:T(128)S(1)}, s32[32]{0:T(128)S(1)}, u32[]{:S(2)}, u32[]{:S(2)}) collective-permute-start(s32[32]{0:T(128)S(1)} %copy-done), channel_id=1, source_target_pairs={{0,1},{1,0},{2,3},{3,2},{4,5},{5,4},{6,7},{7,6},{8,9},{9,8},{10,11... | collective-permute-start | bytes 392 | tf_op jit(solution)/shard_map/ppermute | solution.py:330
  12.0 7.9 %collective-permute-start.4 = (bf16[16,56,128]{2,1,0:T(8,128)(2,1)S(1)}, bf16[16,56,128]{2,1,0:T(8,128)(2,1)S(1)}, u32[]{:S(2)}, u32[]{:S(2)}) collective-permute-start(bf16[16,56,128]{2,1,0:T(8,128)(2,1)S(1)} %get-tuple-element.30.after_ref), channel_id=1, source_target_pairs={{0,96},{1,33},{32,64},{33,1},{64,32},{65,97},{96,0},{97,65},{2,98}... | collective-permute-start | bytes 688136 | tf_op jit(solution)/shard_map/ppermute | solution.py:337
  16.0 6.1 %collective-permute-start.3 = (bf16[16,56,128]{2,1,0:T(8,128)(2,1)S(1)}, bf16[16,56,128]{2,1,0:T(8,128)(2,1)S(1)}, u32[]{:S(2)}, u32[]{:S(2)}) collective-permute-start(bf16[16,56,128]{2,1,0:T(8,128)(2,1)S(1)} %get-tuple-element.32.after_ref), channel_id=1, source_target_pairs={{0,32},{1,97},{32,0},{33,65},{64,96},{65,33},{96,64},{97,1},{2,34}... | collective-permute-start | bytes 688136 | tf_op jit(solution)/shard_map/ppermute | solution.py:337
  19.9 2.3 %collective-permute-start.6 = (bf16[16,56,128]{2,1,0:T(8,128)(2,1)S(1)}, bf16[16,56,128]{2,1,0:T(8,128)(2,1)S(1)}, u32[]{:S(2)}, u32[]{:S(2)}) collective-permute-start(bf16[16,56,128]{2,1,0:T(8,128)(2,1)S(1)} %get-tuple-element.34.after_ref), channel_id=1, source_target_pairs={{0,1},{1,0},{2,3},{3,2},{4,5},{5,4},{6,7},{7,6},{8,9},{9,8},{10,11... | collective-permute-start | bytes 688136 | tf_op jit(solution)/shard_map/ppermute | solution.py:344
  22.1 1.6 %collective-permute-start.5 = (bf16[16,56,128]{2,1,0:T(8,128)(2,1)S(1)}, bf16[16,56,128]{2,1,0:T(8,128)(2,1)S(1)}, u32[]{:S(2)}, u32[]{:S(2)}) collective-permute-start(bf16[16,56,128]{2,1,0:T(8,128)(2,1)S(1)} %get-tuple-element.35), channel_id=1, source_target_pairs={{0,1},{1,0},{2,3},{3,2},{4,5},{5,4},{6,7},{7,6},{8,9},{9,8},{10,11... | collective-permute-start | bytes 688136 | tf_op jit(solution)/shard_map/ppermute | solution.py:344

commit v9 on v8

--- a/solution.py
+++ b/solution.py
@@ -13,7 +13,7 @@
 PATCH_PTS = 512
 NODE_Q = 64
 PART = 16
-FIRST_CHUNKS = (4, 12)
+FIRST_CHUNKS = (2, 14)
 NEXT_CHUNKS = (16,)
 ROWS = 56
 LANES = 128

time: 46.8 us -> 47 us (level)
  no operation moved by 1% of the time
where the time goes in v9:
time: 47 us; the launch traced here: 46.9 us
  blocking collectives  21.3 us (45%)
  Pallas kernels  10.2 us (22%)
  waiting for transfers between devices  8.98 us (19%)
  starting transfers between devices  6.26 us (13%)
    all_to_all x1, blocking collectives, local(): slots = lax.all_to_all(slots, ('y', 'z'), 0, 0, tiled=True)  21.3 us
    ppermute x2, waiting for transfers between devices, local(): held[i] = (keep, lax.ppermute(after, ('x', 'core'), double((i + 1) % 2)))  5.84 us
    pallas_call x1, Pallas kernels, first_part(): pl.pallas_call(first_kernel, in_specs=[HBM] * 6, out_specs=[VMEM] * 6, ou...  4.42 us
    ppermute x2, starting transfers between devices, local(): lax.ppermute(send, ('x', 'core'), double(len(held) % 2))  3.83 us
    pallas_call x7, Pallas kernels, small_call(): pl.pallas_call(kernel, in_specs=in_specs, out_specs=[VMEM] * len(out_shap...  3.15 us
    pallas_call x1, Pallas kernels, later_part(): pl.pallas_call(functools.partial(later_kernel, part, last), in_specs=[VME...  2.65 us
    ppermute x2, starting transfers between devices, local(): held[i] = (keep, lax.ppermute(after, ('x', 'core'), double((i + 1) % 2)))  2.26 us
    ppermute x2, waiting for transfers between devices, local(): lax.ppermute(send, ('x', 'core'), double(len(held) % 2))  1.77 us
  transfers between devices with their start and end apart: 7, of which 5 were waited for; matrix products, arithmetic and copies ran while one was open for 0% of the time, Pallas kernels for 9%

profile of v9, /device:TPU:0, one launch (start us, length us, event | category | flops | bytes accessed | tf_op | source)
XLA Modules:
  0.0 46.9 jit_solution(12177443090655860871)
XLA Ops:
  0.0 4.4 %tiles_0.1 = (f32[16,56,128]{2,1,0:T(8,128)S(1)}, bf16[16,56,128]{2,1,0:T(8,128)(2,1)S(1)}, bf16[112,192]{1,0:T(8,128)(2,1)S(1)}, s32[32,128]{1,0:T(8,128)S(1)},...) custom-call(s32[32]{0:T(128)} %counts_hbm.1, f32[16]{0:T(128)} %table_hbm.1, s32[1,256]{1,0:T(1,128)} %bitcast.4, ...), custom_call_target="tpu_custom_call" | custom-call | flops 8000000000 | bytes 4000000 | tf_op jit(solution)/shard_map/tiles_0/pallas_call | solution.py:189
  4.4 1.7 %collective-permute-start.2 = (bf16[16,56,128]{2,1,0:T(8,128)(2,1)S(1)}, bf16[16,56,128]{2,1,0:T(8,128)(2,1)S(1)}, u32[]{:S(2)}, u32[]{:S(2)}) collective-permute-start(bf16[16,56,128]{2,1,0:T(8,128)(2,1)S(1)} %get-tuple-element.29), channel_id=1, source_target_pairs={{0,32},{1,97},{32,0},{33,65},{64,96},{65,33},{96,64},{97,1},{2,34}... | collective-permute-start | bytes 688136 | tf_op jit(solution)/shard_map/ppermute | solution.py:333
  6.1 0.0 copy-start
  6.1 2.6 %tiles_1.1 = (f32[16,56,128]{2,1,0:T(8,128)S(1)}, bf16[16,56,128]{2,1,0:T(8,128)(2,1)S(1)}) custom-call(s32[32,128]{1,0:T(8,128)S(1)} %get-tuple-element.22.count_rows, bf16[112,192]{1,0:T(8,128)(2,1)S(1)} %get-tuple-element.23.w_ref, bf16[3,64,8192]{2,1,0:T(8,128)(2,1)S(1)} %get-tuple-element.24.sens_buf, f32[3,8192]{1,0:T(4,128)S(1)} %get-tuple-element.25.coords_buf), custom_call_target="tpu_custom_call" | custom-call | flops 8000000000 | bytes 4000000 | tf_op jit(solution)/shard_map/tiles_1/pallas_call | solution.py:214
  8.7 2.2 %collective-permute-start.1 = (bf16[16,56,128]{2,1,0:T(8,128)(2,1)S(1)}, bf16[16,56,128]{2,1,0:T(8,128)(2,1)S(1)}, u32[]{:S(2)}, u32[]{:S(2)}) collective-permute-start(bf16[16,56,128]{2,1,0:T(8,128)(2,1)S(1)} %get-tuple-element.27), channel_id=1, source_target_pairs={{0,96},{1,33},{32,64},{33,1},{64,32},{65,97},{96,0},{97,65},{2,98}... | collective-permute-start | bytes 688136 | tf_op jit(solution)/shard_map/ppermute | solution.py:333
  10.9 0.0 copy-done
  10.9 0.0 collective-permute-start
  10.9 1.1 %collective-permute-done.after_ref.refs_1_ = s32[32]{0:T(128)S(1)} collective-permute-done((s32[32]{0:T(128)S(1)}, s32[32]{0:T(128)S(1)}, u32[]{:S(2)}, u32[]{:S(2)}) %collective-permute-start) | collective-permute-done | bytes 160 | tf_op jit(solution)/shard_map/ppermute | solution.py:330
  12.0 0.0 collective-permute-done.2.recv_ref
  12.0 0.1 pair_sum.4
  12.1 2.2 %collective-permute-start.4 = (bf16[16,56,128]{2,1,0:T(8,128)(2,1)S(1)}, bf16[16,56,128]{2,1,0:T(8,128)(2,1)S(1)}, u32[]{:S(2)}, u32[]{:S(2)}) collective-permute-start(bf16[16,56,128]{2,1,0:T(8,128)(2,1)S(1)} %get-tuple-element.30.after_ref), channel_id=1, source_target_pairs={{0,96},{1,33},{32,64},{33,1},{64,32},{65,97},{96,0},{97,65},{2,98}... | collective-permute-start | bytes 688136 | tf_op jit(solution)/shard_map/ppermute | solution.py:337
  14.3 1.8 %collective-permute-done.1.recv_ref = bf16[16,56,128]{2,1,0:T(8,128)(2,1)S(1)} collective-permute-done((bf16[16,56,128]{2,1,0:T(8,128)(2,1)S(1)}, bf16[16,56,128]{2,1,0:T(8,128)(2,1)S(1)}, u32[]{:S(2)}, u32[]{:S(2)}) %collective-permute-start.1) | collective-permute-done | bytes 229408 | tf_op jit(solution)/shard_map/ppermute | solution.py:333
  16.0 0.1 pair_sum.5
  16.1 0.1 collective-permute-start.3
  16.2 3.8 %collective-permute-done.4.recv_ref = bf16[16,56,128]{2,1,0:T(8,128)(2,1)S(1)} collective-permute-done((bf16[16,56,128]{2,1,0:T(8,128)(2,1)S(1)}, bf16[16,56,128]{2,1,0:T(8,128)(2,1)S(1)}, u32[]{:S(2)}, u32[]{:S(2)}) %collective-permute-start.4) | collective-permute-done | bytes 229408 | tf_op jit(solution)/shard_map/ppermute | solution.py:337
  20.0 0.1 pair_sum.6
  20.1 0.1 collective-permute-start.6
  20.2 2.0 %collective-permute-done.3.recv_ref = bf16[16,56,128]{2,1,0:T(8,128)(2,1)S(1)} collective-permute-done((bf16[16,56,128]{2,1,0:T(8,128)(2,1)S(1)}, bf16[16,56,128]{2,1,0:T(8,128)(2,1)S(1)}, u32[]{:S(2)}, u32[]{:S(2)}) %collective-permute-start.3) | collective-permute-done | bytes 229408 | tf_op jit(solution)/shard_map/ppermute | solution.py:337
  22.2 0.1 pair_sum.7
  22.3 0.1 collective-permute-start.5
  22.4 0.0 collective-permute-done.6.refs_4_
  22.4 1.2 %add.2.refs_3_ = f32[48,56,128]{2,1,0:T(8,128)S(1)} custom-call(s32[32]{0:T(128)S(1)} %copy-done, s32[32]{0:T(128)S(1)} %collective-permute-done.after_ref.refs_1_, f32[16,56,128]{2,1,0:T(8,128)S(1)} %get-tuple-element.36.refs_2_, f32[16,56,128]{2,1,0:T(8,128)S(1)} %get-tuple-element.37.refs_3_, bf16[16,56,128]{2,1,0:T(8,128)(2,1)S(1)} %collective-permute-done.6.refs_4_), custom_call_target="tpu_custom_call" | custom-call | flops 1 | bytes 1 | tf_op jit(solution)/shard_map/add/pallas_call | solution.py:240
  23.6 0.3 collective-permute-done.5.refs_2_
  23.9 0.8 %add.3 = (f32[48,56,128]{2,1,0:T(8,128)S(1)}, bf16[48,56,128]{2,1,0:T(8,128)(2,1)S(1)}) custom-call(s32[32]{0:T(128)S(1)} %copy-done, s32[32]{0:T(128)S(1)} %collective-permute-done.after_ref.refs_1_, bf16[16,56,128]{2,1,0:T(8,128)(2,1)S(1)} %collective-permute-done.5.refs_2_, f32[48,56,128]{2,1,0:T(8,128)S(1)} %add.2.refs_3_), custom_call_target="tpu_custom_call", output_to_operand_aliasing={{0}: (3, {})} | custom-call | flops 1 | bytes 1 | tf_op jit(solution)/shard_map/add/pallas_call | solution.py:240
  24.7 21.3 %all_to_all.5.in_ref = bf16[48,56,128]{2,1,0:T(8,128)(2,1)S(1)} all-to-all(bf16[48,56,128]{2,1,0:T(8,128)(2,1)S(1)} %get-tuple-element.38), channel_id=1, replica_groups=mesh['x'=4,'z'=4,'y'=4,'core'=2] {'y','z'}, dimensions={0} | all-to-all | bytes 1376256 | tf_op jit(solution)/shard_map/all_to_all | solution.py:348
  46.0 0.9 %owner_sum.1 = f32[192,105]{1,0:T(8,128)} custom-call(bf16[48,56,128]{2,1,0:T(8,128)(2,1)S(1)} %all_to_all.5.in_ref), custom_call_target="tpu_custom_call" | custom-call | flops 1 | bytes 1 | tf_op jit(solution)/shard_map/owner_sum/pallas_call | solution.py:240
Async XLA Ops:
  4.4 7.6 %collective-permute-start.2 = (bf16[16,56,128]{2,1,0:T(8,128)(2,1)S(1)}, bf16[16,56,128]{2,1,0:T(8,128)(2,1)S(1)}, u32[]{:S(2)}, u32[]{:S(2)}) collective-permute-start(bf16[16,56,128]{2,1,0:T(8,128)(2,1)S(1)} %get-tuple-element.29), channel_id=1, source_target_pairs={{0,32},{1,97},{32,0},{33,65},{64,96},{65,33},{96,64},{97,1},{2,34}... | collective-permute-start | bytes 688136 | tf_op jit(solution)/shard_map/ppermute | solution.py:333
  6.1 4.8 %copy-start = (s32[32]{0:T(128)S(1)}, s32[32]{0:T(128)}, u32[]{:S(2)}) copy-start(s32[32]{0:T(128)} %refs_0_.3) | copy-start | bytes 388
  8.7 7.3 %collective-permute-start.1 = (bf16[16,56,128]{2,1,0:T(8,128)(2,1)S(1)}, bf16[16,56,128]{2,1,0:T(8,128)(2,1)S(1)}, u32[]{:S(2)}, u32[]{:S(2)}) collective-permute-start(bf16[16,56,128]{2,1,0:T(8,128)(2,1)S(1)} %get-tuple-element.27), channel_id=1, source_target_pairs={{0,96},{1,33},{32,64},{33,1},{64,32},{65,97},{96,0},{97,65},{2,98}... | collective-permute-start | bytes 688136 | tf_op jit(solution)/shard_map/ppermute | solution.py:333
  10.9 1.1 %collective-permute-start = (s32[32]{0:T(128)S(1)}, s32[32]{0:T(128)S(1)}, u32[]{:S(2)}, u32[]{:S(2)}) collective-permute-start(s32[32]{0:T(128)S(1)} %copy-done), channel_id=1, source_target_pairs={{0,1},{1,0},{2,3},{3,2},{4,5},{5,4},{6,7},{7,6},{8,9},{9,8},{10,11... | collective-permute-start | bytes 392 | tf_op jit(solution)/shard_map/ppermute | solution.py:330
  12.1 7.9 %collective-permute-start.4 = (bf16[16,56,128]{2,1,0:T(8,128)(2,1)S(1)}, bf16[16,56,128]{2,1,0:T(8,128)(2,1)S(1)}, u32[]{:S(2)}, u32[]{:S(2)}) collective-permute-start(bf16[16,56,128]{2,1,0:T(8,128)(2,1)S(1)} %get-tuple-element.30.after_ref), channel_id=1, source_target_pairs={{0,96},{1,33},{32,64},{33,1},{64,32},{65,97},{96,0},{97,65},{2,98}... | collective-permute-start | bytes 688136 | tf_op jit(solution)/shard_map/ppermute | solution.py:337
  16.1 6.1 %collective-permute-start.3 = (bf16[16,56,128]{2,1,0:T(8,128)(2,1)S(1)}, bf16[16,56,128]{2,1,0:T(8,128)(2,1)S(1)}, u32[]{:S(2)}, u32[]{:S(2)}) collective-permute-start(bf16[16,56,128]{2,1,0:T(8,128)(2,1)S(1)} %get-tuple-element.32.after_ref), channel_id=1, source_target_pairs={{0,32},{1,97},{32,0},{33,65},{64,96},{65,33},{96,64},{97,1},{2,34}... | collective-permute-start | bytes 688136 | tf_op jit(solution)/shard_map/ppermute | solution.py:337
  20.1 2.3 %collective-permute-start.6 = (bf16[16,56,128]{2,1,0:T(8,128)(2,1)S(1)}, bf16[16,56,128]{2,1,0:T(8,128)(2,1)S(1)}, u32[]{:S(2)}, u32[]{:S(2)}) collective-permute-start(bf16[16,56,128]{2,1,0:T(8,128)(2,1)S(1)} %get-tuple-element.34.after_ref), channel_id=1, source_target_pairs={{0,1},{1,0},{2,3},{3,2},{4,5},{5,4},{6,7},{7,6},{8,9},{9,8},{10,11... | collective-permute-start | bytes 688136 | tf_op jit(solution)/shard_map/ppermute | solution.py:344
  22.3 1.6 %collective-permute-start.5 = (bf16[16,56,128]{2,1,0:T(8,128)(2,1)S(1)}, bf16[16,56,128]{2,1,0:T(8,128)(2,1)S(1)}, u32[]{:S(2)}, u32[]{:S(2)}) collective-permute-start(bf16[16,56,128]{2,1,0:T(8,128)(2,1)S(1)} %get-tuple-element.35), channel_id=1, source_target_pairs={{0,1},{1,0},{2,3},{3,2},{4,5},{5,4},{6,7},{7,6},{8,9},{9,8},{10,11... | collective-permute-start | bytes 688136 | tf_op jit(solution)/shard_map/ppermute | solution.py:344
